TPU v7x, 32 devices: a whole 2x2x4 slice. The times are simulated.
32 devices in a mesh: row: 4 (over y, x), col: 8 (over z, core).
Axes of the slice: x: 2, y: 2, z: 4, core: 2. Of those that a mesh axis runs over, the one named last changes fastest.
Arguments:
- latent: bfloat16 [2, 128, 128, 512], P(None, 'row', 'col'), may hold values from -6 to 6
- w_qkv: bfloat16 [512, 1536], replicated, may hold values from -3 to 3
- w_out: bfloat16 [512, 512], replicated, may hold values from -0.25 to 0.25
- ln_gain: float32 [512], replicated, may hold values from 0.5 to 2
- dw_kernel: bfloat16 [3, 3, 512], replicated, may hold values from -1.1953125 to 1.1953125
- grad_out: bfloat16 [2, 128, 128, 512], P(None, 'row', 'col'), may hold values from -6 to 6
Outputs:
- grad_latent: bfloat16 [2, 128, 128, 512], P(None, 'row', 'col')
- grad_qkv: float32 [512, 1536], P(('row', 'col'))
- grad_wout: float32 [512, 512], P(('row', 'col'))
- grad_gain: float32 [512], replicated
- grad_kernel: float32 [3, 3, 512], replicated
All inputs are finite; a program needn't handle non-finite values.
Results may differ from a plain program's by a relative error of at most 0.03.
The roundings to bfloat16 on the way count: a program that leaves them out, or rounds other values in their place, can miss the bound.
Values may be sent and summed in bfloat16 or wider, within the bound.
No kernel may reach another device: no remote copies, remote signals or barrier semaphores. Data moves between devices by JAX's collectives and lax.ppermute only.
A program may use at most 128 MiB of HBM per device.

v0:
```python
import jax
import jax.numpy as jnp
from jax import lax
from jax.sharding import PartitionSpec as P

HEADS = 16
HEAD = 32
GRID = 8


def extended(cells, sides, width):
    for axis, dim in sides:
        count = lax.axis_size(axis)
        ends = count - 1
        head = lax.slice_in_dim(cells, 0, width, axis=dim)
        tail = lax.slice_in_dim(cells, cells.shape[dim] - width, cells.shape[dim], axis=dim)
        cells = jnp.concatenate(
            [
                lax.ppermute(tail, axis, [(i, (i + 1) % count) for i in range(ends)]),
                cells,
                lax.ppermute(head, axis, [((i + 1) % count, i) for i in range(ends)]),
            ],
            axis=dim,
        )
    return cells


def spatial_mix(padded, kernel, rows, cols, flipped):
    total = jnp.zeros((padded.shape[0], rows, cols, padded.shape[3]), jnp.float32)
    for row_shift in range(3):
        for col_shift in range(3):
            row_start = 2 - row_shift if flipped else row_shift
            col_start = 2 - col_shift if flipped else col_shift
            total = total + kernel[row_shift, col_shift] * padded[
                :, row_start : row_start + rows, col_start : col_start + cols
            ].astype(jnp.float32)
    return total


def tile_to_seven(tiled, row_count, col_count):
    batches, tile_rows, tile_cols, features = tiled.shape
    return tiled.reshape(
        batches,
        GRID // row_count,
        row_count,
        tile_rows // GRID,
        col_count,
        tile_cols // col_count,
        features,
    )


def seven_to_tile(seven):
    shape_seven = seven.shape
    return seven.reshape(
        shape_seven[0],
        shape_seven[1] * shape_seven[2] * shape_seven[3],
        shape_seven[4] * shape_seven[5],
        shape_seven[6],
    )


def relayout(block):
    shape_seven = block.shape
    moved = jnp.transpose(block, (0, 1, 3, 2, 4, 5, 6))
    merged = moved.reshape(
        shape_seven[0],
        shape_seven[1],
        shape_seven[3],
        shape_seven[2] * shape_seven[4],
        shape_seven[5],
        shape_seven[6],
    )
    traded = lax.all_to_all(merged, ("row", "col"), split_axis=3, concat_axis=3, tiled=True)
    split_back = traded.reshape(
        shape_seven[0],
        shape_seven[1],
        shape_seven[3],
        shape_seven[2],
        shape_seven[4],
        shape_seven[5],
        shape_seven[6],
    )
    return jnp.transpose(split_back, (0, 1, 3, 2, 4, 5, 6))


def to_windows(seven):
    shape_seven = seven.shape
    shaped = seven.reshape(
        shape_seven[0],
        GRID,
        shape_seven[3],
        GRID,
        shape_seven[4] // GRID,
        shape_seven[5],
        shape_seven[6],
    )
    return jnp.transpose(shaped, (0, 2, 4, 5, 1, 3, 6)).reshape(-1, GRID * GRID, shape_seven[6])


def from_windows(flat, shape_seven):
    shaped = flat.reshape(
        shape_seven[0],
        shape_seven[3],
        shape_seven[4] // GRID,
        shape_seven[5],
        GRID,
        GRID,
        shape_seven[6],
    )
    return jnp.transpose(shaped, (0, 4, 1, 5, 2, 3, 6)).reshape(shape_seven)


def contract_rows(left, right):
    return lax.dot_general(
        left, right, (((0,), (0,)), ((), ())), preferred_element_type=jnp.float32
    )


def contract_cols(left, right):
    return lax.dot_general(
        left, right, (((1,), (1,)), ((), ())), preferred_element_type=jnp.float32
    )


def shards(latent, w_qkv, w_out, ln_gain, dw_kernel, grad_out):
    batches, tile_rows, tile_cols, features = latent.shape
    row_count = lax.axis_size("row")
    col_count = lax.axis_size("col")
    score_scale = HEAD ** (-0.5)
    kernel = dw_kernel.astype(jnp.float32)
    latent_padded = extended(latent, (("row", 1), ("col", 2)), 1)
    mixed = (
        latent.astype(jnp.float32) + spatial_mix(latent_padded, kernel, tile_rows, tile_cols, False)
    ).astype(jnp.bfloat16)
    mixed_f = mixed.astype(jnp.float32)
    centred = mixed_f - jnp.mean(mixed_f, axis=-1, keepdims=True)
    rstd = lax.rsqrt(jnp.mean(centred * centred, axis=-1, keepdims=True) + 1e-05)
    nhat = centred * rstd
    normed = (nhat * ln_gain).astype(jnp.bfloat16)
    normed_seven = relayout(tile_to_seven(normed, row_count, col_count))
    shape_seven = normed_seven.shape
    normed_win = to_windows(normed_seven)
    count = normed_win.shape[0]
    normed_flat = normed_win.reshape(-1, features)
    packed = jnp.dot(normed_flat, w_qkv, preferred_element_type=jnp.float32).astype(jnp.bfloat16)
    packed = packed.reshape(count, GRID * GRID, 3, HEADS, HEAD)
    query_b = packed[:, :, 0]
    key_b = packed[:, :, 1]
    value_b = packed[:, :, 2]
    scores = (
        jnp.einsum("wqhd,wkhd->whqk", query_b, key_b, preferred_element_type=jnp.float32)
        * score_scale
    )
    probs = jax.nn.softmax(scores, axis=-1)
    probs_b = probs.astype(jnp.bfloat16)
    attended = jnp.einsum(
        "whqk,wkhd->wqhd", probs_b, value_b, preferred_element_type=jnp.float32
    ).astype(jnp.bfloat16)
    attended_tile = seven_to_tile(
        relayout(from_windows(attended.reshape(count, GRID * GRID, features), shape_seven))
    )
    attended_side = attended_tile.reshape(-1, features)
    grad_side = grad_out.reshape(-1, features)
    piece = attended_side
    wout_rows = lax.psum_scatter(
        contract_rows(piece, grad_side), ("row", "col"), scatter_dimension=0, tiled=True
    )
    d_att_side = contract_cols(grad_side, w_out).astype(jnp.bfloat16)
    d_att_seven = relayout(
        tile_to_seven(
            d_att_side.reshape(batches, tile_rows, tile_cols, features), row_count, col_count
        )
    )
    d_att = to_windows(d_att_seven).reshape(count, GRID * GRID, HEADS, HEAD)
    d_probs = jnp.einsum("wqhd,wkhd->whqk", d_att, value_b, preferred_element_type=jnp.float32)
    d_value = jnp.einsum(
        "whqk,wqhd->wkhd", probs_b, d_att, preferred_element_type=jnp.float32
    ).astype(jnp.bfloat16)
    d_scores = (
        probs * (d_probs - jnp.sum(probs * d_probs, axis=-1, keepdims=True)) * score_scale
    ).astype(jnp.bfloat16)
    d_query = jnp.einsum(
        "whqk,wkhd->wqhd", d_scores, key_b, preferred_element_type=jnp.float32
    ).astype(jnp.bfloat16)
    d_key = jnp.einsum(
        "whqk,wqhd->wkhd", d_scores, query_b, preferred_element_type=jnp.float32
    ).astype(jnp.bfloat16)
    d_packed = jnp.stack([d_query, d_key, d_value], axis=2).reshape(-1, 3 * features)
    piece = normed_flat
    qkv_rows = lax.psum_scatter(
        contract_rows(piece, d_packed), ("row", "col"), scatter_dimension=0, tiled=True
    )
    d_normed = contract_cols(d_packed, w_qkv).astype(jnp.bfloat16)
    d_normed_tile = seven_to_tile(
        relayout(from_windows(d_normed.reshape(count, GRID * GRID, features), shape_seven))
    )
    d_normed_f = d_normed_tile.astype(jnp.float32)
    gain_local = jnp.sum(d_normed_f * nhat, axis=(0, 1, 2))
    scaled = d_normed_f * ln_gain
    d_mixed = grad_out.astype(jnp.float32) + rstd * (
        scaled
        - jnp.mean(scaled, axis=-1, keepdims=True)
        - nhat * jnp.mean(scaled * nhat, axis=-1, keepdims=True)
    )
    d_mixed_b = d_mixed.astype(jnp.bfloat16)
    d_padded = extended(d_mixed_b, (("row", 1), ("col", 2)), 1)
    d_mixed_f = d_mixed_b.astype(jnp.float32)
    grad_latent = (d_mixed_f + spatial_mix(d_padded, kernel, tile_rows, tile_cols, True)).astype(
        jnp.bfloat16
    )
    kernel_terms = []
    for row_shift in range(3):
        for col_shift in range(3):
            window_part = latent_padded[
                :, row_shift : row_shift + tile_rows, col_shift : col_shift + tile_cols
            ].astype(jnp.float32)
            kernel_terms.append(jnp.sum(d_mixed_f * window_part, axis=(0, 1, 2)))
    kernel_local = jnp.stack(kernel_terms, axis=0).reshape(3, 3, features)
    gain_total, kernel_total = lax.psum((gain_local, kernel_local), ("row", "col"))
    return (grad_latent, qkv_rows, wout_rows, gain_total, kernel_total)


def solution(mesh):
    in_specs = (P(None, "row", "col", None), P(), P(), P(), P(), P(None, "row", "col", None))
    out_specs = (
        P(None, "row", "col", None),
        P(("row", "col"), None),
        P(("row", "col"), None),
        P(),
        P(),
    )
    return jax.shard_map(shards, mesh=mesh, in_specs=in_specs, out_specs=out_specs, check_vma=False)
```

profile of v0, /device:TPU:0, one launch (start us, length us, event | category | flops | bytes accessed | tf_op | source)
XLA Modules:
  0.0 466.5 jit_solution(15907264101802420179)
XLA Ops:
  8.1 4.8 %collective-permute-start = (bf16[2,1,16,512]{3,2,1,0:T(8,128)(2,1)S(1)}, bf16[2,1,16,512]{3,2,1,0:T(8,128)(2,1)S(1)}, u32[]{:S(2)}, u32[]{:S(2)}) collective-permute-start(bf16[2,1,16,512]{3,2,1,0:T(8,128)(2,1)S(1)} %get-tuple-element.54), channel_id=1, source_target_pairs={{0,8},{8,16},{16,24},{1,9},{9,17},{17,25},{2,10},{10,18},{18,26},{... | collective-permute-start | bytes 98312 | tf_op jit(solution)/shard_map/ppermute | solution.py:19
  12.9 1.3 collective-permute-start.1
  14.2 3.1 convolution_convert_fusion.2
  17.3 1.5 reshape_reshape.19
  19.0 2.1 copy.154
  21.0 7.1 %all-to-all-start.1 = ((bf16[2,2,4,32,2,512]{5,4,2,1,0,3:T(2,128)(2,1)}), bf16[2,2,4,32,2,512]{5,4,2,1,0,3:T(2,128)(2,1)}, u32[]{:S(2)}, u32[]{:S(2)}) async-start(bf16[2,2,4,32,2,512]{5,4,2,1,0,3:T(2,128)(2,1)} %copy.154), calls=%async_computation.1 | async-start | bytes 2097152 | tf_op jit(solution)/shard_map/all_to_all | solution.py:74
  28.6 1.4 collective-permute-start.3
  30.0 3.0 collective-permute-start.2
  33.1 0.9 collective-permute-done.2
  34.0 4.2 convert_reduce_fusion
  39.2 1.1 copy.144
  40.5 2.1 copy.146
  42.6 13.2 %all-to-all-done.1 = bf16[2,2,4,32,2,512]{5,4,2,1,0,3:T(2,128)(2,1)} async-done(((bf16[2,2,4,32,2,512]{5,4,2,1,0,3:T(2,128)(2,1)}), bf16[2,2,4,32,2,512]{5,4,2,1,0,3:T(2,128)(2,1)}, u32[]{:S(2)}, u32[]{:S(2)}) %all-to-all-start.1) | async-done | bytes 1048608 | tf_op jit(solution)/shard_map/all_to_all | solution.py:74
  55.8 11.7 %all-to-all-start = ((bf16[2,2,4,32,2,512]{5,4,2,1,0,3:T(2,128)(2,1)}), bf16[2,2,4,32,2,512]{5,4,2,1,0,3:T(2,128)(2,1)}, u32[]{:S(2)}, u32[]{:S(2)}) async-start(bf16[2,2,4,32,2,512]{5,4,2,1,0,3:T(2,128)(2,1)} %copy.146), calls=%async_computation | async-start | bytes 2097152 | tf_op jit(solution)/shard_map/all_to_all | solution.py:74
  67.4 1.8 copy.210
  69.4 1.1 copy.157
  70.5 5.9 %reshape_reshape.20 = bf16[16,64,16,32]{3,2,1,0:T(8,128)(2,1)} reshape(bf16[2,4,1,2,8,8,512]{6,5,4,3,1,0,2:T(8,128)(2,1)} %copy.157) | data formatting | bytes 2097152 | tf_op jit(solution)/shard_map/reshape;reshape | solution.py:175
  76.4 5.8 %copy.159 = bf16[16,64,16,32]{1,3,2,0:T(8,128)(2,1)} copy(bf16[16,64,16,32]{3,2,1,0:T(8,128)(2,1)} %reshape_reshape.20) | data formatting | bytes 2097152 | tf_op jit(solution)/shard_map/reshape;reshape | solution.py:175
  82.1 12.8 %all-to-all-done = bf16[2,2,4,32,2,512]{5,4,2,1,0,3:T(2,128)(2,1)} async-done(((bf16[2,2,4,32,2,512]{5,4,2,1,0,3:T(2,128)(2,1)}), bf16[2,2,4,32,2,512]{5,4,2,1,0,3:T(2,128)(2,1)}, u32[]{:S(2)}, u32[]{:S(2)}) %all-to-all-start) | async-done | bytes 1048608 | tf_op jit(solution)/shard_map/all_to_all | solution.py:74
  95.0 1.8 copy.212
  97.0 0.9 copy-done.12
  98.0 3.5 convolution_convert_fusion
  101.5 4.7 %copy.150 = bf16[1024,1536]{0,1:T(8,128)(2,1)} copy(bf16[1024,1536]{1,0:T(8,128)(2,1)} %convolution_convert_fusion) | data formatting | bytes 6291456 | tf_op jit(solution)/shard_map/convert_element_type | solution.py:146
  106.2 9.2 %reshape.109 = bf16[16,64,3,16,32]{1,0,4,3,2:T(8,128)(2,1)} reshape(bf16[1024,1536]{0,1:T(8,128)(2,1)} %copy.150) | data formatting | bytes 6291456 | tf_op jit(solution)/shard_map/reshape | solution.py:147
  115.4 4.5 fusion.79
  119.9 1.3 copy-done.8
  121.8 1.9 fusion.66
  123.8 12.2 %fusion.84 = (f32[16,16,64]{2,1,0:T(8,128)S(1)}, f32[16,16,64,64]{2,3,1,0:T(8,128)S(1)}) fusion(f32[16,16,64,64]{2,3,1,0:T(8,128)S(1)} %fusion.66), kind=kOutput, calls=%fused_computation.139 | output fusion | flops 4194367 | bytes 8454144 | tf_op jit(solution)/shard_map/sub | solution.py:155
  135.9 3.2 copy-done.7
  139.1 2.9 convert_bitcast_fusion.1
  142.0 5.6 %copy.172 = bf16[16,64,16,32]{3,2,1,0:T(8,128)(2,1)} copy(bf16[16,64,16,32]{1,3,2,0:T(8,128)(2,1)} %convert_bitcast_fusion.1) | data formatting | bytes 2097152 | tf_op jit(solution)/shard_map/convert_element_type | solution.py:159
  147.7 7.2 %reshape_reshape.22 = bf16[2,4,1,2,8,8,512]{6,5,4,3,1,0,2:T(8,128)(2,1)} reshape(bf16[16,64,16,32]{3,2,1,0:T(8,128)(2,1)} %copy.172) | data formatting | bytes 2097152 | tf_op jit(solution)/shard_map/reshape;reshape | solution.py:102
  154.9 3.3 copy.174
  158.1 3.4 all-to-all-start.3
  161.6 6.8 %fusion.67 = f32[16,16,64,64]{2,3,1,0:T(8,128)} fusion(bf16[16,64,16,32]{1,3,2,0:T(8,128)(2,1)} %copy.159, bf16[16,64,1,16,32]{1,0,4,3,2:T(8,128)(2,1)} %copy-done.10), kind=kOutput, calls=%fused_computation.95 | convolution fusion | flops 67108864 | bytes 6291456 | tf_op jit(solution)/shard_map/wqhd,wkhd->whqk/dot_general | solution.py:176
  168.4 15.5 %convert_bitcast_fusion.3 = bf16[16,64,1,16,32]{1,4,3,0,2:T(8,128)(2,1)} fusion(f32[16,16,64,64]{2,3,1,0:T(8,128)} %fusion.67, bf16[16,64,1,16,32]{1,0,4,3,2:T(8,128)(2,1)} %copy-done.9, f32[16,16,64,64]{2,3,1,0:T(8,128)} %copy-done.7, f32[16,16,64]{2,1,0:T(8,128)S(1)} %get-tuple-element.64), kind=kOutput, calls=%fused_computation.90 | convolution fusion | flops 74989632 | bytes 10551296 | tf_op jit(solution)/shard_map/whqk,wqhd->wkhd/dot_general | solution.py:186
  183.9 15.7 %convert_bitcast_fusion.4 = bf16[16,64,1,16,32]{1,4,3,0,2:T(8,128)(2,1)} fusion(f32[16,16,64,64]{2,3,1,0:T(8,128)} %fusion.67, bf16[16,64,1,16,32]{1,0,4,3,2:T(8,128)(2,1)} %copy-done.8, f32[16,16,64,64]{2,3,1,0:T(8,128)} %copy-done.7, f32[16,16,64]{2,1,0:T(8,128)S(1)} %get-tuple-element.64), kind=kOutput, calls=%fused_computation.91 | convolution fusion | flops 74989632 | bytes 10551296 | tf_op jit(solution)/shard_map/whqk,wkhd->wqhd/dot_general | solution.py:183
  199.6 7.6 %convert_bitcast_fusion.2 = bf16[16,64,1,16,32]{1,4,3,0,2:T(8,128)(2,1)} fusion(bf16[16,64,16,32]{1,3,2,0:T(8,128)(2,1)} %copy.159, f32[16,16,64,64]{2,3,1,0:T(8,128)} %copy-done.7, f32[16,16,64]{2,1,0:T(8,128)S(1)} %get-tuple-element.64), kind=kOutput, calls=%fused_computation.85 | convolution fusion | flops 69730304 | bytes 6356992 | tf_op jit(solution)/shard_map/whqk,wqhd->wkhd/dot_general | solution.py:177
  207.2 1.8 copy.209
  209.0 2.0 copy.176
  211.1 2.4 reshape_reshape.23
  213.5 3.3 fusion.86
  216.7 4.4 pad_maximum_fusion
  221.1 9.9 %copy.164 = bf16[16,64,3,16,32]{1,0,4,3,2:T(8,128)(2,1)} copy(bf16[16,64,3,16,32]{1,4,3,0,2:T(8,128)(2,1)S(1)} %pad_maximum_fusion) | data formatting | bytes 6291456 | tf_op jit(solution)/shard_map/stack | solution.py:189
  231.1 9.6 %reshape.114 = bf16[1024,1536]{0,1:T(8,128)(2,1)} reshape(bf16[16,64,3,16,32]{1,0,4,3,2:T(8,128)(2,1)} %copy.164) | data formatting | bytes 6291456 | tf_op jit(solution)/shard_map/reshape | solution.py:189
  240.7 3.7 convolution_convert_fusion.1
  244.4 2.1 copy.165
  246.5 5.9 %all-to-all-start.2 = ((bf16[2,2,4,32,2,512]{5,4,2,1,0,3:T(2,128)(2,1)}), bf16[2,2,4,32,2,512]{5,4,2,1,0,3:T(2,128)(2,1)}, u32[]{:S(2)}, u32[]{:S(2)}) async-start(bf16[2,2,4,32,2,512]{5,4,2,1,0,3:T(2,128)(2,1)} %bitcast.131), calls=%async_computation.2 | async-start | bytes 2097152 | tf_op jit(solution)/shard_map/all_to_all | solution.py:74
  252.4 5.7 %fusion.85 = f32[512,1536]{1,0:T(8,128)} fusion(bf16[1024,512]{1,0:T(8,128)(2,1)} %bitcast.143, bf16[1024,1536]{0,1:T(8,128)(2,1)} %reshape.114), kind=kOutput, calls=%fused_computation.140 | convolution fusion | flops 1610612736 | bytes 7340032 | tf_op jit(solution)/shard_map/dot_general | solution.py:115
  258.2 24.0 %all-to-all-done.2 = bf16[2,2,4,32,2,512]{5,4,2,1,0,3:T(2,128)(2,1)} async-done(((bf16[2,2,4,32,2,512]{5,4,2,1,0,3:T(2,128)(2,1)}), bf16[2,2,4,32,2,512]{5,4,2,1,0,3:T(2,128)(2,1)}, u32[]{:S(2)}, u32[]{:S(2)}) %all-to-all-start.2) | async-done | bytes 1048608 | tf_op jit(solution)/shard_map/all_to_all | solution.py:74
  282.1 1.8 convert_bitcast_fusion
  284.0 3.0 copy.167
  287.0 1.9 fusion.37
  289.4 2.6 fusion.27
  292.1 9.0 %fusion.52 = (f32[512]{0:T(512)S(1)}, f32[512]{0:T(512)S(1)}, f32[512]{0:T(512)S(1)}, f32[512]{0:T(512)S(1)}, f32[512]{0:T(512)S(1)}, /*index=5*/f32[512]{0:T(51...) fusion(bf16[2,34,1,512]{3,2,1,0:T(2,128)(2,1)S(1)} %collective-permute-done.3, ...), kind=kLoop, calls=%fused_computation.80 | loop fusion | flops 33025536 | bytes 7647232 | tf_op jit(solution)/shard_map/reduce_sum | solution.py:218
  301.1 1.3 collective-permute-start.5
  302.4 4.5 collective-permute-start.4
  307.0 1.6 collective-permute-done.4
  308.8 1.3 collective-permute-start.6
  310.1 3.0 collective-permute-start.7
  313.2 40.7 %all-reduce = (f32[512]{0:T(512)}, f32[3,3,512]{2,1,0:T(4,128)}) all-reduce(f32[512]{0:T(512)S(1)} %get-tuple-element.20, f32[3,3,512]{2,1,0:T(4,128)S(1)} %reshape.120), channel_id=1, replica_groups=mesh['row'=4,'col'=8] {'row','col'}, use_global_device_ids=true, to_apply=%region_10.0 | all-reduce | flops 5120 | bytes 40960 | tf_op jit(solution)/shard_map/psum | solution.py:220
  353.9 2.7 pad_maximum_fusion.1
  356.6 3.5 fusion.43
  360.1 99.3 %reduce-scatter.3.cloned.1.call-done = f32[16,1536]{1,0:T(8,128)} async-done(((f32[512,1536]{1,0:T(8,128)}), f32[16,1536]{1,0:T(8,128)}) %reduce-scatter.3.cloned.1.call-update) | async-done | bytes 98320 | tf_op jit(solution)/shard_map/reduce_scatter | solution.py:191
  (63 shorter events, 4.6 us)
Async XLA Ops:
  7.2 90.8 %copy-start = (bf16[512,1536]{1,0:T(8,128)(2,1)S(1)}, bf16[512,1536]{1,0:T(8,128)(2,1)}, u32[]{:S(2)}) copy-start(bf16[512,1536]{1,0:T(8,128)(2,1)} %param.7) | copy-start | bytes 4718596
  8.1 20.1 %collective-permute-start = (bf16[2,1,16,512]{3,2,1,0:T(8,128)(2,1)S(1)}, bf16[2,1,16,512]{3,2,1,0:T(8,128)(2,1)S(1)}, u32[]{:S(2)}, u32[]{:S(2)}) collective-permute-start(bf16[2,1,16,512]{3,2,1,0:T(8,128)(2,1)S(1)} %get-tuple-element.54), channel_id=1, source_target_pairs={{0,8},{8,16},{16,24},{1,9},{9,17},{17,25},{2,10},{10,18},{18,26},{... | collective-permute-start | bytes 98312 | tf_op jit(solution)/shard_map/ppermute | solution.py:19
  12.9 15.4 %collective-permute-start.1 = (bf16[2,1,16,512]{3,2,1,0:T(8,128)(2,1)S(1)}, bf16[2,1,16,512]{3,2,1,0:T(8,128)(2,1)S(1)}, u32[]{:S(2)}, u32[]{:S(2)}) collective-permute-start(bf16[2,1,16,512]{3,2,1,0:T(8,128)(2,1)S(1)} %get-tuple-element.53), channel_id=1, source_target_pairs={{8,0},{16,8},{24,16},{9,1},{17,9},{25,17},{10,2},{18,10},{26,18},{... | collective-permute-start | bytes 98312 | tf_op jit(solution)/shard_map/ppermute | solution.py:21
  19.0 9.2 %copy-start.4 = (bf16[2,32,16,512]{3,2,1,0:T(8,128)(2,1)S(1)}, bf16[2,32,16,512]{3,2,1,0:T(8,128)(2,1)}, u32[]{:S(2)}) copy-start(bf16[2,32,16,512]{3,2,1,0:T(8,128)(2,1)} %param.6) | copy-start | bytes 3145732
  21.0 12.0 %copy-start.14 = (bf16[3,3,512]{2,1,0:T(4,128)(2,1)S(1)}, bf16[3,3,512]{2,1,0:T(4,128)(2,1)}, u32[]{:S(2)}) copy-start(bf16[3,3,512]{2,1,0:T(4,128)(2,1)} %param.10) | copy-start | bytes 27652
  21.0 34.7 %all-to-all-start.1 = ((bf16[2,2,4,32,2,512]{5,4,2,1,0,3:T(2,128)(2,1)}), bf16[2,2,4,32,2,512]{5,4,2,1,0,3:T(2,128)(2,1)}, u32[]{:S(2)}, u32[]{:S(2)}) async-start(bf16[2,2,4,32,2,512]{5,4,2,1,0,3:T(2,128)(2,1)} %copy.154), calls=%async_computation.1 | async-start | bytes 2097152 | tf_op jit(solution)/shard_map/all_to_all | solution.py:74
  28.2 5.8 %copy-start.5 = (bf16[2,32,16,512]{3,2,1,0:T(8,128)(2,1)S(1)}, bf16[2,32,16,512]{3,2,1,0:T(8,128)(2,1)}, u32[]{:S(2)}) copy-start(bf16[2,32,16,512]{3,2,1,0:T(8,128)(2,1)} %param.6) | copy-start | bytes 3145732
  28.3 9.9 %copy-start.11 = (bf16[2,34,16,512]{3,2,1,0:T(8,128)(2,1)}, bf16[2,34,16,512]{3,2,1,0:T(8,128)(2,1)S(1)}, u32[]{:S(2)}) copy-start(bf16[2,34,16,512]{3,2,1,0:T(8,128)(2,1)S(1)} %constant_dynamic-update-slice_fusion) | copy-start | bytes 3342340
  28.6 4.5 collective-permute-start.3
  30.0 4.0 collective-permute-start.2
  34.0 4.7 %copy-start.13 = (f32[512]{0:T(512)S(1)}, f32[512]{0:T(512)}, u32[]{:S(2)}) copy-start(f32[512]{0:T(512)} %param.9) | copy-start | bytes 6148
  55.8 39.2 %all-to-all-start = ((bf16[2,2,4,32,2,512]{5,4,2,1,0,3:T(2,128)(2,1)}), bf16[2,2,4,32,2,512]{5,4,2,1,0,3:T(2,128)(2,1)}, u32[]{:S(2)}, u32[]{:S(2)}) async-start(bf16[2,2,4,32,2,512]{5,4,2,1,0,3:T(2,128)(2,1)} %copy.146), calls=%async_computation | async-start | bytes 2097152 | tf_op jit(solution)/shard_map/all_to_all | solution.py:74
  97.0 1.0 copy-start.12
  119.8 1.3 copy-start.8
  119.8 2.0 copy-start.9
  119.9 16.1 %copy-start.10 = (bf16[16,64,1,16,32]{1,0,4,3,2:T(8,128)(2,1)}, bf16[16,64,1,16,32]{1,0,4,3,2:T(8,128)(2,1)S(1)}, u32[]{:S(2)}) copy-start(bf16[16,64,1,16,32]{1,0,4,3,2:T(8,128)(2,1)S(1)} %get-tuple-element.42) | copy-start | bytes 3145732
  135.9 3.2 copy-start.7
  158.1 49.1 %all-to-all-start.3 = ((bf16[2,2,4,32,2,512]{5,4,2,1,0,3:T(2,128)(2,1)}), bf16[2,2,4,32,2,512]{5,4,2,1,0,3:T(2,128)(2,1)}, u32[]{:S(2)}, u32[]{:S(2)}) async-start(bf16[2,2,4,32,2,512]{5,4,2,1,0,3:T(2,128)(2,1)} %copy.174), calls=%async_computation.4 | async-start | bytes 2097152 | tf_op jit(solution)/shard_map/all_to_all | solution.py:74
  161.5 198.6 %reduce-scatter.5.cloned.1.call-start = ((), (), s32[]{:S(2)}) async-start(), calls=%async_computation.7 | async-start | bytes 1081344 | tf_op jit(solution)/shard_map/reduce_scatter | solution.py:166
  246.5 35.7 %all-to-all-start.2 = ((bf16[2,2,4,32,2,512]{5,4,2,1,0,3:T(2,128)(2,1)}), bf16[2,2,4,32,2,512]{5,4,2,1,0,3:T(2,128)(2,1)}, u32[]{:S(2)}, u32[]{:S(2)}) async-start(bf16[2,2,4,32,2,512]{5,4,2,1,0,3:T(2,128)(2,1)} %bitcast.131), calls=%async_computation.2 | async-start | bytes 2097152 | tf_op jit(solution)/shard_map/all_to_all | solution.py:74
  252.4 207.0 %reduce-scatter.3.cloned.1.call-start = ((), (), s32[]{:S(2)}) async-start(), calls=%async_computation.6 | async-start | bytes 3244032 | tf_op jit(solution)/shard_map/reduce_scatter | solution.py:191
  289.4 2.7 copy-start.1
  289.4 2.7 copy-start.6
  301.1 7.5 %copy-start.2 = (bf16[2,32,16,512]{3,2,1,0:T(8,128)(2,1)}, bf16[2,32,16,512]{3,2,1,0:T(8,128)(2,1)S(1)}, u32[]{:S(2)}) copy-start(bf16[2,32,16,512]{3,2,1,0:T(8,128)(2,1)S(1)} %get-tuple-element.39) | copy-start | bytes 3145732
  301.1 5.9 %collective-permute-start.5 = (bf16[2,1,16,512]{3,2,1,0:T(8,128)(2,1)S(1)}, bf16[2,1,16,512]{3,2,1,0:T(8,128)(2,1)S(1)}, u32[]{:S(2)}, u32[]{:S(2)}) collective-permute-start(bf16[2,1,16,512]{3,2,1,0:T(8,128)(2,1)S(1)} %get-tuple-element.52), channel_id=1, source_target_pairs={{8,0},{16,8},{24,16},{9,1},{17,9},{25,17},{10,2},{18,10},{26,18},{... | collective-permute-start | bytes 98312 | tf_op jit(solution)/shard_map/ppermute | solution.py:21
  302.4 6.1 %collective-permute-start.4 = (bf16[2,1,16,512]{3,2,1,0:T(8,128)(2,1)S(1)}, bf16[2,1,16,512]{3,2,1,0:T(8,128)(2,1)S(1)}, u32[]{:S(2)}, u32[]{:S(2)}) collective-permute-start(bf16[2,1,16,512]{3,2,1,0:T(8,128)(2,1)S(1)} %get-tuple-element.51), channel_id=1, source_target_pairs={{0,8},{8,16},{16,24},{1,9},{9,17},{17,25},{2,10},{10,18},{18,26},{... | collective-permute-start | bytes 98312 | tf_op jit(solution)/shard_map/ppermute | solution.py:19
  308.8 45.1 %collective-permute-start.6 = (bf16[2,34,1,512]{3,2,1,0:T(2,128)(2,1)S(1)}, bf16[2,34,1,512]{3,2,1,0:T(2,128)(2,1)S(1)}, u32[]{:S(2)}, u32[]{:S(2)}) collective-permute-start(bf16[2,34,1,512]{3,2,1,0:T(2,128)(2,1)S(1)} %get-tuple-element.47), channel_id=1, source_target_pairs={{1,0},{2,1},{3,2},{4,3},{5,4},{6,5},{7,6},{9,8},{10,9},{11,10},{12... | collective-permute-start | bytes 208904 | tf_op jit(solution)/shard_map/ppermute | solution.py:21
  310.1 43.8 %collective-permute-start.7 = (bf16[2,34,1,512]{3,2,1,0:T(2,128)(2,1)S(1)}, bf16[2,34,1,512]{3,2,1,0:T(2,128)(2,1)S(1)}, u32[]{:S(2)}, u32[]{:S(2)}) collective-permute-start(bf16[2,34,1,512]{3,2,1,0:T(2,128)(2,1)S(1)} %get-tuple-element.48), channel_id=1, source_target_pairs={{0,1},{1,2},{2,3},{3,4},{4,5},{5,6},{6,7},{8,9},{9,10},{10,11},{11... | collective-permute-start | bytes 208904 | tf_op jit(solution)/shard_map/ppermute | solution.py:19
  353.9 2.7 copy-start.3
Sparse Core Ops, SparseCore 0:
  216.9 137.2 reduce-scatter.4
  361.1 98.2 reduce-scatter.2
where the time goes:
time: 474 us; the launch traced here: 466 us
  waiting for transfers between devices  152 us (32%)
  local copies, waits for them, and re-layouts  97.1 us (20%)
  matrix products  69.7 us (15%)
  starting transfers between devices  48.9 us (10%)
  other arithmetic  43.4 us (9%)
  blocking collectives  40.7 us (9%)
  between operations  14.8 us (3%)
    reduce_scatter x1, waiting for transfers between devices, shards(): lax.psum_scatter(contract_rows(piece, d_packed), ('row', 'col'), scatter_...  99.3 us
    all_to_all x4, waiting for transfers between devices, relayout(): lax.all_to_all(merged, ('row', 'col'), split_axis=3, concat_axis=3, tiled...  49.9 us
    psum x1, blocking collectives, shards(): lax.psum((gain_local, kernel_local), ('row', 'col'))  40.7 us
    all_to_all x4, starting transfers between devices, relayout(): lax.all_to_all(merged, ('row', 'col'), split_axis=3, concat_axis=3, tiled...  28 us
    dot_general x1, matrix products, shards(): jnp.einsum('whqk,wkhd->wqhd', d_scores, key_b, preferred_element_type=jnp...  15.7 us
    dot_general x1, matrix products, shards(): jnp.einsum('whqk,wqhd->wkhd', d_scores, query_b, preferred_element_type=j...  15.5 us
    ppermute x4, starting transfers between devices, extended(): lax.ppermute(tail, axis, [(i, (i + 1) % count) for i in range(ends)])  15.5 us
    sub x1, other arithmetic, shards(): probs = jax.nn.softmax(scores, axis=-1)  12.2 us
  transfers between devices with their start and end apart: 14, of which 6 were waited for; matrix products, arithmetic and copies ran while one was open for 29% of the time, Pallas kernels for 0%

commit v1 on v0

v1 whole, which is shorter than its diff:
```python
import functools

import jax
import jax.numpy as jnp
import numpy as np
from jax import lax
from jax.experimental import pallas as pl
from jax.experimental.pallas import tpu as pltpu
from jax.sharding import PartitionSpec as P

HEADS = 16
HEAD = 32
GRID = 8
CELLS = GRID * GRID
AXES = ("row", "col")
F32 = jnp.float32
BF16 = jnp.bfloat16
LIMIT = 56 * 1024 * 1024


def dot(left, right, dims=((1,), (0,))):
    return lax.dot_general(left, right, (dims, ((), ())), preferred_element_type=F32)


class Plan:
    def __init__(self, batches, tile_rows, tile_cols, row_count, col_count, cuts):
        devices = row_count * col_count
        high = tile_rows * row_count // GRID
        full = tile_cols * col_count // GRID
        wide = min(full, tile_cols)
        groups = full // wide
        reps_r = tile_rows // high
        reps_s = tile_cols // wide
        reps = reps_r * reps_s
        classes = [(b, a, e) for b in range(batches) for a in range(high) for e in range(wide)]
        edge = [c for c in classes if c[1] in (0, high - 1) or c[2] in (0, wide - 1)]
        rest = [c for c in classes if c not in set(edge)]
        place = {c: (n % devices, n // devices) for n, c in enumerate(edge + rest)}
        slots = len(classes) // devices
        self.edge_slots = -(-len(edge) // devices)
        self.devices = devices
        cells = batches * tile_rows * tile_cols
        bounds = cuts(slots, self.edge_slots)
        self.send, self.sort, self.rows = [], [], []
        self.border = []
        spots = []
        for edge_row in (0, tile_rows - 1):
            spots += [(b, edge_row, w) for b in range(batches) for w in range(tile_cols)]
        for edge_col in (0, tile_cols - 1):
            spots += [(b, h, edge_col) for b in range(batches) for h in range(tile_rows)]
        self.border_tile = np.zeros((len(spots), cells), np.float32)
        for n, (b, h, w) in enumerate(spots):
            self.border_tile[n, (b * tile_rows + h) * tile_cols + w] = 1
        for first, last in zip(bounds[:-1], bounds[1:]):
            size = (last - first) * reps
            rows = devices * size
            send = np.zeros((rows, cells), np.float32)
            for b in range(batches):
                for h in range(tile_rows):
                    for w in range(tile_cols):
                        owner, slot = place[(b, h % high, w % wide)]
                        if first <= slot < last:
                            rep = (h // high) * reps_s + w // wide
                            send[owner * size + (slot - first) * reps + rep, (b * tile_rows + h) * tile_cols + w] = 1
            sort = np.zeros((rows, rows), np.float32)
            for i in range(row_count):
                for j in range(col_count):
                    for slot in range(last - first):
                        for r in range(reps_r):
                            for s in range(reps_s):
                                start = j * tile_cols + s * wide
                                window = slot * groups + (start % full) // wide
                                cell = (i * reps_r + r) * GRID + start // full
                                source = (i * col_count + j) * size + slot * reps + r * reps_s + s
                                sort[window * CELLS + cell, source] = 1
            self.send.append(send)
            self.sort.append(sort)
            self.rows.append(rows)


def pad_rows(matrix, to):
    return np.concatenate([matrix, np.zeros((to - matrix.shape[0], matrix.shape[1]), matrix.dtype)], 0)


def send_kernel(x_ref, *refs):
    count = len(refs) // 2
    for order_ref, out_ref in zip(refs[:count], refs[count:]):
        out_ref[...] = dot(order_ref[...], x_ref[...]).astype(BF16)


def fill_shifts(shift_ref, left_ref, right_ref, side_l, side_r):
    _, batches, rows, cols, feats = shift_ref.shape
    spot = lax.broadcasted_iota(jnp.int32, (cols, feats), 0)
    for b in range(batches):
        side_l[b] = left_ref[b].astype(F32)
        side_r[b] = right_ref[b].astype(F32)

        def step(h, carry, b=b):
            x = shift_ref[1, b, h].astype(F32)
            low = jnp.where(spot == 0, side_l[b, pl.ds(h, 1), :], pltpu.roll(x, 1, 0))
            high = jnp.where(spot == cols - 1, side_r[b, pl.ds(h, 1), :], pltpu.roll(x, cols - 1, 0))
            shift_ref[0, b, h] = low.astype(BF16)
            shift_ref[2, b, h] = high.astype(BF16)
            return carry

        lax.fori_loop(0, rows, step, 0, unroll=2)


def mix_kernel(count, lat_ref, top_ref, bot_ref, left_ref, right_ref, dw_ref, gain_ref, *refs):
    orders = refs[:count]
    outs = refs[count : 2 * count]
    mixed_ref, shift_ref, normed_ref, side_l, side_r = refs[2 * count :]
    batches, rows, cols, feats = lat_ref.shape
    shift_ref[1, :, 1 : rows + 1] = lat_ref[...]
    shift_ref[1, :, 0] = top_ref[:, 0]
    shift_ref[1, :, rows + 1] = bot_ref[:, 0]
    fill_shifts(shift_ref, left_ref, right_ref, side_l, side_r)
    kern = [[dw_ref[i, j : j + 1, :].astype(F32) for j in range(3)] for i in range(3)]
    gain = gain_ref[...]
    for b in range(batches):

        def step(h, carry, b=b):
            total = jnp.zeros((cols, feats), F32)
            for i in range(3):
                for j in range(3):
                    total = total + kern[i][j] * shift_ref[j, b, h + i].astype(F32)
            mixed = (shift_ref[1, b, h + 1].astype(F32) + total).astype(BF16)
            mixed_ref[b, h] = mixed
            mixed = mixed.astype(F32)
            centred = mixed - jnp.mean(mixed, axis=-1, keepdims=True)
            rstd = lax.rsqrt(jnp.mean(centred * centred, axis=-1, keepdims=True) + 1e-05)
            normed_ref[pl.ds(pl.multiple_of((b * rows + h) * cols, cols), cols), :] = (
                centred * rstd * gain
            ).astype(BF16)
            return carry

        lax.fori_loop(0, rows, step, 0, unroll=2)
    for order_ref, out_ref in zip(orders, outs):
        out_ref[...] = dot(order_ref[...], normed_ref[...]).astype(BF16)


def window_kernel(first, last, places, n_ref, g_ref, sort_ref, wqkv_ref, wout_ref, *refs):
    if not first:
        old_ref, refs = refs[0], refs[1:]
    dn_ref, dw_ref, nw, gw, packed, datt, att, dpacked, head_mask, half_mask, acc = refs
    rows, feats = n_ref.shape
    tiles = feats // 256
    scale = HEAD ** (-0.5)
    block = 256 if rows % 256 == 0 else rows

    head_mask[...] = (
        (lax.broadcasted_iota(jnp.int32, (4 * CELLS, 256), 1) // HEAD) % 4
        == lax.broadcasted_iota(jnp.int32, (4 * CELLS, 256), 0) // CELLS
    ).astype(F32).astype(BF16)
    half_mask[...] = (
        lax.broadcasted_iota(jnp.int32, (2 * CELLS, 256), 1) // 128
        == lax.broadcasted_iota(jnp.int32, (2 * CELLS, 256), 0) // CELLS
    ).astype(F32).astype(BF16)

    def project(n, carry):
        at = pl.ds(pl.multiple_of(n * block, block), block)
        normed = dot(sort_ref[at, :], n_ref[...]).astype(BF16)
        nw[at, :] = normed
        packed[at, :] = dot(normed, wqkv_ref[...]).astype(BF16)
        grad = dot(sort_ref[at, :], g_ref[...]).astype(BF16)
        gw[at, :] = grad
        datt[at, :] = dot(grad, wout_ref[...], ((1,), (1,))).astype(BF16)
        return carry

    lax.fori_loop(0, rows // block, project, 0)

    lane = lax.broadcasted_iota(jnp.int32, (CELLS, 256), 1)
    lane_half = lane < 128
    lane_head = (lane // HEAD) % 4

    def fold_heads(full):
        out = full[3 * CELLS :]
        for h in (2, 1, 0):
            out = jnp.where(lane_head == h, full[h * CELLS : (h + 1) * CELLS], out)
        return out

    def one(n, carry):
        at = pl.ds(pl.multiple_of(n * CELLS, CELLS), CELLS)
        for t in range(tiles):
            cols = [slice(p * feats + t * 256, p * feats + (t + 1) * 256) for p in range(3)]
            query = packed[at, cols[0]]
            key = packed[at, cols[1]]
            value = packed[at, cols[2]]
            grad = datt[at, t * 256 : (t + 1) * 256]
            key_big = jnp.concatenate([key] * 4, axis=0) * head_mask[...]
            value_big = jnp.concatenate([value] * 4, axis=0) * head_mask[...]
            query_two = jnp.concatenate([query] * 2, axis=0) * half_mask[...]
            grad_two = jnp.concatenate([grad] * 2, axis=0) * half_mask[...]
            scores = (dot(key_big, query_two, ((1,), (1,))) * scale).reshape(4, CELLS, 2 * CELLS)
            d_probs = dot(value_big, grad_two, ((1,), (1,))).reshape(4, CELLS, 2 * CELLS)
            raised = jnp.exp(scores - jnp.max(scores, axis=1, keepdims=True))
            probs = raised / jnp.sum(raised, axis=1, keepdims=True)
            probs_b = probs.astype(BF16).reshape(4 * CELLS, 2 * CELLS)
            inner = jnp.sum(probs * d_probs, axis=1, keepdims=True)
            d_scores = (
                (probs * (d_probs - inner) * scale).astype(BF16).reshape(4 * CELLS, 2 * CELLS)
            )
            out = dot(probs_b, value_big, ((0,), (0,)))
            att[at, t * 256 : (t + 1) * 256] = jnp.where(
                lane_half, out[:CELLS], out[CELLS:]
            ).astype(BF16)
            d_query = dot(d_scores, key_big, ((0,), (0,)))
            dpacked[at, cols[0]] = jnp.where(
                lane_half, d_query[:CELLS], d_query[CELLS:]
            ).astype(BF16)
            dpacked[at, cols[1]] = fold_heads(dot(d_scores, query_two)).astype(BF16)
            dpacked[at, cols[2]] = fold_heads(dot(probs_b, grad_two)).astype(BF16)
        return carry

    lax.fori_loop(0, rows // CELLS, one, 0)

    def back(n, carry):
        at = pl.ds(pl.multiple_of(n * block, block), block)
        gw_free = dot(dpacked[at, :], wqkv_ref[...], ((1,), (1,))).astype(BF16)
        datt[at, :] = gw_free
        return carry

    lax.fori_loop(0, rows // block, back, 0)
    dn_ref[...] = dot(sort_ref[...], datt[...], ((0,), (0,))).astype(BF16)
    normed_t = nw[...].T
    wide = 3 * feats
    for t in range(wide // 256):
        at = slice(t * 256, (t + 1) * 256)
        acc[:, at] = dot(normed_t, dpacked[:, at])
    acc[:, wide:] = dot(att[...].T, gw[...])
    if not first:
        acc[...] += old_ref[...]
    if last:
        size = feats // len(places)
        for n, place in enumerate(places):
            dw_ref[place * size : (place + 1) * size, :] = acc[n * size : (n + 1) * size, :].astype(BF16)
    else:
        dw_ref[...] = acc[...]


def norm_back(d_normed, mixed, grad, gain):
    mixed = mixed.astype(F32)
    centred = mixed - jnp.mean(mixed, axis=-1, keepdims=True)
    rstd = lax.rsqrt(jnp.mean(centred * centred, axis=-1, keepdims=True) + 1e-05)
    nhat = centred * rstd
    scaled = d_normed * gain
    d_mixed = grad.astype(F32) + rstd * (
        scaled
        - jnp.mean(scaled, axis=-1, keepdims=True)
        - nhat * jnp.mean(scaled * nhat, axis=-1, keepdims=True)
    )
    return d_mixed.astype(BF16), nhat


def border_kernel(dn_ref, mixed_ref, grad_ref, pick_dn_ref, pick_ref, gain_ref, out_ref):
    d_normed = dot(pick_dn_ref[...], dn_ref[...])
    mixed = dot(pick_ref[...], mixed_ref[...])
    grad = dot(pick_ref[...], grad_ref[...])
    out_ref[...] = norm_back(d_normed, mixed, grad, gain_ref[...])[0]


def final_kernel(count, *refs):
    dns, orders, refs = refs[:count], refs[count : 2 * count], refs[2 * count :]
    (mixed_ref, grad_ref, x_ref, top_ref, bot_ref, left_ref, right_ref, dw_ref, gain_ref) = refs[:9]
    out_ref, sums_ref, shift_ref, dn, side_l, side_r = refs[9:]
    batches, rows, cols, feats = mixed_ref.shape
    cells = batches * rows * cols
    block = 256

    def unsort(n, carry):
        at = pl.ds(pl.multiple_of(n * block, block), block)
        total = dot(orders[0][at, :], dns[0][...])
        for order, part in zip(orders[1:], dns[1:]):
            total = total + dot(order[at, :], part[...])
        dn[at, :] = total
        return carry

    lax.fori_loop(0, cells // block, unsort, 0)
    gain = gain_ref[...]
    shift_ref[1, :, 0] = top_ref[:, 0]
    shift_ref[1, :, rows + 1] = bot_ref[:, 0]
    gain_sum = jnp.zeros((cols, feats), F32)
    for b in range(batches):

        def step(h, gain_sum, b=b):
            d_normed = dn[pl.ds(pl.multiple_of((b * rows + h) * cols, cols), cols), :]
            d_mixed, nhat = norm_back(d_normed, mixed_ref[b, h], grad_ref[b, h], gain)
            shift_ref[1, b, h + 1] = d_mixed
            return gain_sum + d_normed * nhat

        gain_sum = lax.fori_loop(0, rows, step, gain_sum, unroll=2)
    sums_ref[9:10, :] = jnp.sum(gain_sum, axis=0, keepdims=True)
    sums_ref[10:, :] = jnp.zeros((sums_ref.shape[0] - 10, feats), F32)
    fill_shifts(shift_ref, left_ref, right_ref, side_l, side_r)
    kern = [[dw_ref[i, j : j + 1, :].astype(F32) for j in range(3)] for i in range(3)]
    for b in range(batches):

        def conv(h, carry, b=b):
            total = jnp.zeros((cols, feats), F32)
            for i in range(3):
                for j in range(3):
                    total = total + kern[i][j] * shift_ref[2 - j, b, h + 2 - i].astype(F32)
            out_ref[b, h] = (shift_ref[1, b, h + 1].astype(F32) + total).astype(BF16)
            return carry

        lax.fori_loop(0, rows, conv, 0, unroll=2)
    for j in range(3):
        sums = [jnp.zeros((cols, feats), F32) for _ in range(3)]
        for b in range(batches):

            def grads(h, sums, b=b, j=j):
                d_mixed = shift_ref[1, b, h + 1].astype(F32)
                return [s + d_mixed * x_ref[j, b, h + i].astype(F32) for i, s in enumerate(sums)]

            sums = lax.fori_loop(0, rows, grads, sums, unroll=2)
        for i in range(3):
            sums_ref[3 * i + j : 3 * i + j + 1, :] = jnp.sum(sums[i], axis=0, keepdims=True)


def call(body, outs, scratch, args, flops, name):
    moved = sum(int(np.prod(o.shape)) * o.dtype.itemsize for o in (*outs, *args))
    vmem = pl.BlockSpec(memory_space=pltpu.VMEM)
    return pl.pallas_call(
        body,
        out_shape=outs,
        in_specs=[vmem] * len(args),
        out_specs=[vmem] * len(outs),
        scratch_shapes=scratch,
        compiler_params=pltpu.CompilerParams(vmem_limit_bytes=LIMIT),
        cost_estimate=pl.CostEstimate(flops=flops, bytes_accessed=moved, transcendentals=0),
        name=name,
    )(*args)


def shape(dims, dtype):
    return jax.ShapeDtypeStruct(tuple(dims), dtype)


def shifted(cells, axis, step):
    count = lax.axis_size(axis)
    return lax.ppermute(cells, axis, [(n, n + step) for n in range(count) if 0 <= n + step < count])


def halos(top, bottom, left, right):
    above = shifted(bottom, "row", 1)
    below = shifted(top, "row", -1)

    def column(own, where):
        corner = lambda rows: rows[:, :, where : where + 1] if where == 0 else rows[:, :, -1:]
        return jnp.concatenate([corner(above), own, corner(below)], axis=1)

    from_left = shifted(column(right, -1), "col", 1)
    from_right = shifted(column(left, 0), "col", -1)
    flat = lambda c: c.reshape(c.shape[0], c.shape[1], c.shape[3])
    return above, below, flat(from_left), flat(from_right)


def bits(row_count, col_count):
    steps = [("col", 1)]
    steps += [("row", 1 << n) for n in range(row_count.bit_length() - 1)]
    steps += [("col", 1 << n) for n in range(1, col_count.bit_length() - 1)]
    return steps


def swap(x, axis, step):
    return lax.ppermute(x, axis, [(n, n ^ step) for n in range(lax.axis_size(axis))])


def halving(x, steps):
    for axis, step in steps:
        half = x.shape[0] // 2
        high = (lax.axis_index(axis) // step) % 2 == 1
        give = jnp.where(high, x[:half], x[half:])
        keep = jnp.where(high, x[half:], x[:half])
        got = swap(give, axis, step)
        x = keep.astype(F32) + got.astype(F32)
        if (axis, step) != steps[-1]:
            x = x.astype(BF16)
    return x


def cuts(slots, edge_slots):
    return [0, slots]


def shards(plan, latent, w_qkv, w_out, ln_gain, dw_kernel, grad_out):
    batches, rows, cols, feats = latent.shape
    row_count, col_count = lax.axis_size("row"), lax.axis_size("col")
    cells = batches * rows * cols
    parts = len(plan.rows)
    steps = bits(row_count, col_count)
    gain = ln_gain.reshape(1, feats)
    send = [jnp.asarray(m, BF16) for m in plan.send]
    back = [jnp.asarray(np.ascontiguousarray(m.T), BF16) for m in plan.send]
    sort = [jnp.asarray(m, BF16) for m in plan.sort]
    chunks = [shape((n, feats), BF16) for n in plan.rows]
    trade = lambda x: lax.all_to_all(x, AXES, split_axis=0, concat_axis=0, tiled=True)
    grad_flat = grad_out.reshape(cells, feats)

    grad_sent = call(send_kernel, chunks, [], [grad_flat, *send], 2 * cells * cells * feats, "grad_send")
    grad_win = [trade(x) for x in grad_sent]

    above, below, left, right = halos(latent[:, :1], latent[:, -1:], latent[:, :, :1], latent[:, :, -1:])
    padded = shape((3, batches, rows + 2, cols, feats), BF16)
    side = pltpu.VMEM((batches, rows + 2, feats), F32)
    *normed, mixed, x_shift = call(
        functools.partial(mix_kernel, parts),
        [*chunks, shape(latent.shape, BF16), padded],
        [pltpu.VMEM((cells, feats), BF16), side, side],
        [latent, above, below, left, right, dw_kernel, gain, *send],
        2 * cells * cells * feats,
        "mix",
    )
    normed_win = [trade(x) for x in normed]

    places = []
    for i in range(row_count):
        for j in range(col_count):
            place = 0
            for axis, step in steps:
                place = 2 * place + (((i if axis == "row" else j) // step) & 1)
            places.append(place)
    weights = None
    d_parts = []
    for n in range(parts):
        count = plan.rows[n]
        last = n == parts - 1
        args = [normed_win[n], grad_win[n], sort[n], w_qkv, w_out]
        if weights is not None:
            args.append(weights)
        d_chunk, weights = call(
            functools.partial(window_kernel, weights is None, last, places),
            [chunks[n], shape((feats, 4 * feats), BF16 if last else F32)],
            [
                pltpu.VMEM((count, feats), BF16),
                pltpu.VMEM((count, feats), BF16),
                pltpu.VMEM((count, 3 * feats), BF16),
                pltpu.VMEM((count, feats), BF16),
                pltpu.VMEM((count, feats), BF16),
                pltpu.VMEM((count, 3 * feats), BF16),
                pltpu.VMEM((4 * CELLS, 256), BF16),
                pltpu.VMEM((2 * CELLS, 256), BF16),
                pltpu.VMEM((feats, 4 * feats), F32),
            ],
            args,
            count * feats * feats * 40,
            "windows",
        )
        d_parts.append(trade(d_chunk))

    pick = plan.border_tile
    pick_dn = jnp.asarray(pick @ plan.send[0].T, BF16)
    (border,) = call(
        border_kernel,
        [shape((pick.shape[0], feats), BF16)],
        [],
        [d_parts[0], mixed.reshape(cells, feats), grad_flat, pick_dn, jnp.asarray(pick, BF16), gain],
        6 * cells * pick.shape[0] * feats,
        "border",
    )
    tops, sides = batches * cols, batches * rows
    d_top = border[:tops].reshape(batches, 1, cols, feats)
    d_bottom = border[tops : 2 * tops].reshape(batches, 1, cols, feats)
    d_left = border[2 * tops : 2 * tops + sides].reshape(batches, rows, 1, feats)
    d_right = border[2 * tops + sides :].reshape(batches, rows, 1, feats)
    above, below, left, right = halos(d_top, d_bottom, d_left, d_right)

    grad_latent, sums = call(
        functools.partial(final_kernel, parts),
        [shape(latent.shape, BF16), shape((16, feats), F32)],
        [
            pltpu.VMEM(padded.shape, BF16),
            pltpu.VMEM((cells, feats), F32),
            side,
            side,
        ],
        [*d_parts, *back, mixed, grad_out, x_shift, above, below, left, right, dw_kernel, gain],
        2 * cells * cells * feats,
        "final",
    )
    weights = halving(weights, steps)
    for axis, step in steps:
        sums = sums + swap(sums, axis, step)
    return (
        grad_latent,
        weights[:, : 3 * feats],
        weights[:, 3 * feats :],
        sums[9],
        sums[:9].reshape(3, 3, feats),
    )


def solution(mesh):
    row_count, col_count = mesh.shape["row"], mesh.shape["col"]

    def run(latent, w_qkv, w_out, ln_gain, dw_kernel, grad_out):
        batches, rows, cols, _ = latent.shape
        plan = Plan(batches, rows // row_count, cols // col_count, row_count, col_count, cuts)
        in_specs = (P(None, "row", "col", None), P(), P(), P(), P(), P(None, "row", "col", None))
        out_specs = (
            P(None, "row", "col", None),
            P(AXES, None),
            P(AXES, None),
            P(),
            P(),
        )
        return jax.shard_map(
            functools.partial(shards, plan),
            mesh=mesh,
            in_specs=in_specs,
            out_specs=out_specs,
            check_vma=False,
        )(latent, w_qkv, w_out, ln_gain, dw_kernel, grad_out)

    return run
```

time: 474 us -> 216 us (0.46); the launches traced: 466 us -> 216 us
  local copies, waits for them, and re-layouts: 97.1 us -> 12.3 us
  waiting for transfers between devices: 152 us -> 78.1 us
  Pallas kernels: 0 us -> 72 us
  matrix products: 69.7 us -> 0 us
  blocking collectives: 40.7 us -> 0 us
  other arithmetic: 43.4 us -> 5.01 us
  between operations: 14.8 us -> 1 us
    reduce_scatter x2 -> x0, waiting for transfers between devices: 99.3 us -> none  [the longest x1 99.3 us: shards(): lax.psum_scatter(contract_rows(piece, d_packed), ('row', 'col'), scatter_...]
    pallas_call x0 -> x5, Pallas kernels: none -> 72 us  [call(): pl.pallas_call(body, out_shape=outs, in_specs=[vmem] * len(args), out_spe...]
    dot_general x11 -> x0, matrix products: 69.7 us -> none  [the longest x1 15.7 us: shards(): jnp.einsum('whqk,wkhd->wqhd', d_scores, key_b, preferred_element_type=jnp...]
    ppermute x8 -> x18, waiting for transfers between devices: 2.51 us -> 48.8 us  [the longest x10 37.6 us: swap(): lax.ppermute(x, axis, [(n, n ^ step) for n in range(lax.axis_size(axis))])]
    psum x1 -> x0, blocking collectives: 40.7 us -> none  [shards(): lax.psum((gain_local, kernel_local), ('row', 'col'))]
    another operation x8 -> x0, local copies, waits for them, and re-layouts: 32.9 us -> none  [the longest x2 11.7 us: shards(): d_att = to_windows(d_att_seven).reshape(count, GRID * GRID, HEADS, HEAD)]
    reshape x7 -> x3, local copies, waits for them, and re-layouts: 28.3 us -> 0.72 us  [the longest x1 0.62 us: shards(): sums[:9].reshape(3, 3, feats)]
    all_to_all x4 -> x3, waiting for transfers between devices: 49.9 us -> 29.4 us  [shards(): lax.all_to_all(x, AXES, split_axis=0, concat_axis=0, tiled=True)]
  transfers between devices with their start and end apart: 14 -> 21, of which waited for: 6 -> 13; matrix products, arithmetic and copies ran while one was open for 29% -> 4% of each run, Pallas kernels for 0% -> 15%
where the time goes in v1:
time: 216 us
  waiting for transfers between devices  78.1 us (36%)
  Pallas kernels  72 us (33%)
  starting transfers between devices  47 us (22%)
  local copies, waits for them, and re-layouts  12.3 us (6%)
  other arithmetic  5.01 us (2%)
    pallas_call x5, Pallas kernels, call(): pl.pallas_call(body, out_shape=outs, in_specs=[vmem] * len(args), out_spe...  72 us
    ppermute x10, waiting for transfers between devices, swap(): lax.ppermute(x, axis, [(n, n ^ step) for n in range(lax.axis_size(axis))])  37.6 us
    all_to_all x3, waiting for transfers between devices, shards(): lax.all_to_all(x, AXES, split_axis=0, concat_axis=0, tiled=True)  29.4 us
    all_to_all x3, starting transfers between devices, shards(): lax.all_to_all(x, AXES, split_axis=0, concat_axis=0, tiled=True)  21.1 us
    ppermute x8, starting transfers between devices, shifted(): lax.ppermute(cells, axis, [(n, n + step) for n in range(count) if 0 <= n...  16.5 us
    ppermute x8, waiting for transfers between devices, shifted(): lax.ppermute(cells, axis, [(n, n + step) for n in range(count) if 0 <= n...  11.1 us
    ppermute x10, starting transfers between devices, swap(): lax.ppermute(x, axis, [(n, n ^ step) for n in range(lax.axis_size(axis))])  9.47 us
  transfers between devices with their start and end apart: 21, of which 13 were waited for; matrix products, arithmetic and copies ran while one was open for 4% of the time, Pallas kernels for 15%

profile of v1, /device:TPU:0, one launch (start us, length us, event | category | flops | bytes accessed | tf_op | source)
XLA Modules:
  0.0 215.5 jit_solution(2728956477422638264)
XLA Ops:
  0.6 4.1 %grad_send.1 = bf16[1024,512]{1,0:T(8,128)(2,1)} custom-call(bf16[1024,512]{1,0:T(8,128)(2,1)} %bitcast.21, bf16[1024,1024]{1,0:T(8,128)(2,1)} %constant.91.clone.refs_0_), custom_call_target="tpu_custom_call" | custom-call | flops 1073741824 | bytes 4194304 | tf_op jit(solution)/shard_map/grad_send/pallas_call | solution.py:323
  4.8 7.3 %all-to-all-start.1 = ((bf16[32,32,512]{2,1,0:T(8,128)(2,1)}), bf16[32,32,512]{2,1,0:T(8,128)(2,1)S(1)}, u32[]{:S(2)}, u32[]{:S(2)}) async-start(bf16[32,32,512]{2,1,0:T(8,128)(2,1)} %bitcast.23), calls=%async_computation.1 | async-start | bytes 2097152 | tf_op jit(solution)/shard_map/all_to_all | solution.py:397
  12.1 0.8 fusion.1
  12.9 0.1 copy.34
  12.9 3.7 %collective-permute-start = (bf16[2,1,16,512]{3,1,0,2:T(2,128)(2,1)S(1)}, bf16[2,1,16,512]{3,1,0,2:T(2,128)(2,1)S(1)}, u32[]{:S(2)}, u32[]{:S(2)}) collective-permute-start(bf16[2,1,16,512]{3,1,0,2:T(2,128)(2,1)S(1)} %copy.34), channel_id=1, source_target_pairs={{0,8},{8,16},{16,24},{1,9},{9,17},{17,25},{2,10},{10,18},{18,26},{... | collective-permute-start | bytes 98312 | tf_op jit(solution)/shard_map/ppermute | solution.py:341
  16.6 0.1 copy.35
  16.7 1.3 collective-permute-start.1
  18.0 1.4 fusion
  19.4 0.8 collective-permute-done
  20.3 4.8 %collective-permute-done.1 = bf16[2,1,16,512]{3,1,0,2:T(2,128)(2,1)S(1)} collective-permute-done((bf16[2,1,16,512]{3,1,0,2:T(2,128)(2,1)S(1)}, bf16[2,1,16,512]{3,1,0,2:T(2,128)(2,1)S(1)}, u32[]{:S(2)}, u32[]{:S(2)}) %collective-permute-start.1) | collective-permute-done | bytes 32800 | tf_op jit(solution)/shard_map/ppermute | solution.py:341
  25.1 1.3 collective-permute-start.3
  26.5 3.0 %collective-permute-start.2 = (bf16[2,34,1,512]{3,1,0,2:T(8,128)(2,1)S(1)}, bf16[2,34,1,512]{3,1,0,2:T(8,128)(2,1)S(1)}, u32[]{:S(2)}, u32[]{:S(2)}) collective-permute-start(bf16[2,34,1,512]{3,1,0,2:T(8,128)(2,1)S(1)} %pad_maximum_fusion), channel_id=1, source_target_pairs={{0,1},{1,2},{2,3},{3,4},{4,5},{5,6},{6,7},{8,9},{9,10},{10,11},{11... | collective-permute-start | bytes 208904 | tf_op jit(solution)/shard_map/ppermute | solution.py:341
  29.5 0.6 copy.28.top_ref
  30.1 0.6 copy.29.bot_ref
  30.8 0.6 copy-done.6
  31.4 12.9 %mix.1 = (bf16[1024,512]{1,0:T(8,128)(2,1)}, bf16[2,32,16,512]{3,2,1,0:T(8,128)(2,1)}, bf16[3,2,34,16,512]{4,3,2,1,0:T(8,128)(2,1)}) custom-call(bf16[2,32,16,512]{3,2,1,0:T(8,128)(2,1)} %lat_ref.1, bf16[2,1,16,512]{3,2,1,0:T(8,128)(2,1)} %copy.28.top_ref, bf16[2,1,16,512]{3,2,1,0:T(8,128)(2,1)} %copy.29.bot_ref, bf16[2,34,512]{2,1,0:T(8,128)(2,1)} %bitcast.41, ...), custom_call_target="tpu_custom_call" | custom-call | flops 1073741824 | bytes 8801280 | tf_op jit(solution)/shard_map/mix/pallas_call | solution.py:323
  44.3 11.1 %all-to-all-start = ((bf16[32,32,512]{2,1,0:T(8,128)(2,1)}), bf16[32,32,512]{2,1,0:T(8,128)(2,1)S(1)}, u32[]{:S(2)}, u32[]{:S(2)}) async-start(bf16[32,32,512]{2,1,0:T(8,128)(2,1)} %bitcast.27), calls=%async_computation | async-start | bytes 2097152 | tf_op jit(solution)/shard_map/all_to_all | solution.py:397
  55.4 27.6 %all-to-all-done = bf16[32,32,512]{2,1,0:T(8,128)(2,1)S(1)} async-done(((bf16[32,32,512]{2,1,0:T(8,128)(2,1)}), bf16[32,32,512]{2,1,0:T(8,128)(2,1)S(1)}, u32[]{:S(2)}, u32[]{:S(2)}) %all-to-all-start) | async-done | bytes 1048608 | tf_op jit(solution)/shard_map/all_to_all | solution.py:397
  83.0 1.0 copy-done.3
  84.0 31.3 %windows.1 = (bf16[1024,512]{1,0:T(8,128)(2,1)}, bf16[512,2048]{1,0:T(8,128)(2,1)}) custom-call(bf16[1024,512]{1,0:T(8,128)(2,1)} %bitcast.28, bf16[1024,512]{1,0:T(8,128)(2,1)} %bitcast.26, bf16[1024,1024]{1,0:T(8,128)(2,1)} %constant.93.clone.sort_ref, bf16[512,1536]{1,0:T(8,128)(2,1)} %wqkv_ref.1, bf16[512,512]{1,0:T(8,128)(2,1)} %wout_ref.1), custom_call_target="tpu_custom_call" | custom-call | flops 10737418240 | bytes 9437184 | tf_op jit(solution)/shard_map/windows/pallas_call | solution.py:323
  115.3 1.8 broadcast_select_fusion
  117.1 0.1 collective-permute-start.8
  117.2 2.8 %collective-permute-done.8 = bf16[256,2048]{1,0:T(8,128)(2,1)} collective-permute-done((bf16[256,2048]{1,0:T(8,128)(2,1)S(1)}, bf16[256,2048]{1,0:T(8,128)(2,1)}, u32[]{:S(2)}, u32[]{:S(2)}) %collective-permute-start.8) | collective-permute-done | bytes 1048608 | tf_op jit(solution)/shard_map/ppermute | solution.py:366
  119.9 1.8 add_convert_fusion
  121.7 0.1 broadcast_select_fusion.1
  121.8 0.6 collective-permute-start.9
  122.4 2.6 %all-to-all-start.2 = ((bf16[32,32,512]{2,1,0:T(8,128)(2,1)}), bf16[32,32,512]{2,1,0:T(8,128)(2,1)S(1)}, u32[]{:S(2)}, u32[]{:S(2)}) async-start(bf16[32,32,512]{2,1,0:T(8,128)(2,1)} %bitcast.25), calls=%async_computation.2 | async-start | bytes 2097152 | tf_op jit(solution)/shard_map/all_to_all | solution.py:397
  125.0 17.1 %collective-permute-done.9 = bf16[128,2048]{1,0:T(8,128)(2,1)S(1)} collective-permute-done((bf16[128,2048]{1,0:T(8,128)(2,1)S(1)}, bf16[128,2048]{1,0:T(8,128)(2,1)S(1)}, u32[]{:S(2)}, u32[]{:S(2)}) %collective-permute-start.9) | collective-permute-done | bytes 524320 | tf_op jit(solution)/shard_map/ppermute | solution.py:366
  142.1 0.2 add_convert_fusion.1
  142.4 0.2 collective-permute-start.10
  142.5 8.1 %collective-permute-done.10 = bf16[64,2048]{1,0:T(8,128)(2,1)S(1)} collective-permute-done((bf16[64,2048]{1,0:T(8,128)(2,1)S(1)}, bf16[64,2048]{1,0:T(8,128)(2,1)S(1)}, u32[]{:S(2)}, u32[]{:S(2)}) %collective-permute-start.10) | collective-permute-done | bytes 262176 | tf_op jit(solution)/shard_map/ppermute | solution.py:366
  150.7 0.1 add_convert_fusion.2
  150.8 1.8 all-to-all-done.2
  152.6 1.0 copy-done
  153.6 3.6 %border.1 = bf16[192,512]{1,0:T(8,128)(2,1)} custom-call(bf16[1024,512]{1,0:T(8,128)(2,1)} %bitcast.19, bf16[1024,512]{1,0:T(8,128)(2,1)} %bitcast.24, bf16[1024,512]{1,0:T(8,128)(2,1)} %bitcast.22, bf16[192,1024]{1,0:T(8,128)(2,1)} %constant.94.clone.pick_dn_ref, bf16[192,1024]{1,0:T(8,128)(2,1)} %constant.95.clone.pick_ref, f32[1,512]{1,0:T(1,128)} %bitcast.37), custom_call_target="tpu_custom_call" | custom-call | flops 603979776 | bytes 4130816 | tf_op jit(solution)/shard_map/border/pallas_call | solution.py:323
  157.2 0.8 fusion.3
  158.0 1.6 collective-permute-start.4
  159.6 0.9 fusion.2
  160.5 0.1 copy.31
  160.5 1.3 collective-permute-start.5
  161.8 5.5 %collective-permute-done.5 = bf16[2,1,16,512]{3,1,0,2:T(2,128)(2,1)S(1)} collective-permute-done((bf16[2,1,16,512]{3,1,0,2:T(2,128)(2,1)S(1)}, bf16[2,1,16,512]{3,1,0,2:T(2,128)(2,1)S(1)}, u32[]{:S(2)}, u32[]{:S(2)}) %collective-permute-start.5) | collective-permute-done | bytes 32800 | tf_op jit(solution)/shard_map/ppermute | solution.py:341
  167.4 1.3 collective-permute-start.7
  168.7 3.0 %collective-permute-start.6 = (bf16[2,34,1,512]{3,1,0,2:T(8,128)(2,1)S(1)}, bf16[2,34,1,512]{3,1,0,2:T(8,128)(2,1)S(1)}, u32[]{:S(2)}, u32[]{:S(2)}) collective-permute-start(bf16[2,34,1,512]{3,1,0,2:T(8,128)(2,1)S(1)} %pad_maximum_fusion.2), channel_id=1, source_target_pairs={{0,1},{1,2},{2,3},{3,4},{4,5},{5,6},{6,7},{8,9},{9,10},{10,11},{11... | collective-permute-start | bytes 208904 | tf_op jit(solution)/shard_map/ppermute | solution.py:341
  171.8 1.0 collective-permute-start.11
  172.8 0.6 copy.32.refs_5_
  173.5 0.6 copy.33.refs_6_
  174.1 0.6 copy-done.4
  174.7 20.2 %final.1 = (bf16[2,32,16,512]{3,2,1,0:T(8,128)(2,1)}, f32[16,512]{1,0:T(8,128)}) custom-call(bf16[1024,512]{1,0:T(8,128)(2,1)} %bitcast.20, bf16[1024,1024]{1,0:T(8,128)(2,1)} %constant.92.clone.refs_1_, bf16[2,32,16,512]{3,2,1,0:T(8,128)(2,1)} %get-tuple-element.14.refs_2_, bf16[2,32,16,512]{3,2,1,0:T(8,128)(2,1)} %refs_3_.1, ...), custom_call_target="tpu_custom_call" | custom-call | flops 1073741824 | bytes 9882624 | tf_op jit(solution)/shard_map/final/pallas_call | solution.py:323
  194.9 0.2 collective-permute-start.13
  195.1 1.2 collective-permute-done.13
  196.3 0.8 add.61
  197.1 1.6 collective-permute-start.14
  198.8 2.2 %collective-permute-done.14 = f32[16,512]{1,0:T(8,128)S(1)} collective-permute-done((f32[16,512]{1,0:T(8,128)S(1)}, f32[16,512]{1,0:T(8,128)S(1)}, u32[]{:S(2)}, u32[]{:S(2)}) %collective-permute-start.14) | collective-permute-done | bytes 32800 | tf_op jit(solution)/shard_map/ppermute | solution.py:366
  201.0 0.1 collective-permute-start.15
  201.2 2.1 collective-permute-start.12
  203.2 1.7 collective-permute-done.15
  204.9 2.7 %collective-permute-start.16 = (f32[16,512]{1,0:T(8,128)S(1)}, f32[16,512]{1,0:T(8,128)S(1)}, u32[]{:S(2)}, u32[]{:S(2)}) collective-permute-start(f32[16,512]{1,0:T(8,128)S(1)} %add.63), channel_id=1, source_target_pairs={{0,2},{1,3},{2,0},{3,1},{4,6},{5,7},{6,4},{7,5},{8,10},{9,11},{10,... | collective-permute-start | bytes 98312 | tf_op jit(solution)/shard_map/ppermute | solution.py:366
  207.6 1.9 collective-permute-done.16
  209.5 0.9 collective-permute-start.17
  210.4 0.6 slice.150
  211.1 0.6 slice.151
  211.7 2.7 %collective-permute-done.17 = f32[16,512]{1,0:T(8,128)S(1)} collective-permute-done((f32[16,512]{1,0:T(8,128)S(1)}, f32[16,512]{1,0:T(8,128)S(1)}, u32[]{:S(2)}, u32[]{:S(2)}) %collective-permute-start.17) | collective-permute-done | bytes 32800 | tf_op jit(solution)/shard_map/ppermute | solution.py:366
  214.3 0.6 slice.152
  214.9 0.6 reshape.63
  (40 shorter events, 0.5 us)
Async XLA Ops:
  4.8 39.5 %all-to-all-start.1 = ((bf16[32,32,512]{2,1,0:T(8,128)(2,1)}), bf16[32,32,512]{2,1,0:T(8,128)(2,1)S(1)}, u32[]{:S(2)}, u32[]{:S(2)}) async-start(bf16[32,32,512]{2,1,0:T(8,128)(2,1)} %bitcast.23), calls=%async_computation.1 | async-start | bytes 2097152 | tf_op jit(solution)/shard_map/all_to_all | solution.py:397
  12.9 7.3 %collective-permute-start = (bf16[2,1,16,512]{3,1,0,2:T(2,128)(2,1)S(1)}, bf16[2,1,16,512]{3,1,0,2:T(2,128)(2,1)S(1)}, u32[]{:S(2)}, u32[]{:S(2)}) collective-permute-start(bf16[2,1,16,512]{3,1,0,2:T(2,128)(2,1)S(1)} %copy.34), channel_id=1, source_target_pairs={{0,8},{8,16},{16,24},{1,9},{9,17},{17,25},{2,10},{10,18},{18,26},{... | collective-permute-start | bytes 98312 | tf_op jit(solution)/shard_map/ppermute | solution.py:341
  16.7 8.4 %collective-permute-start.1 = (bf16[2,1,16,512]{3,1,0,2:T(2,128)(2,1)S(1)}, bf16[2,1,16,512]{3,1,0,2:T(2,128)(2,1)S(1)}, u32[]{:S(2)}, u32[]{:S(2)}) collective-permute-start(bf16[2,1,16,512]{3,1,0,2:T(2,128)(2,1)S(1)} %copy.35), channel_id=1, source_target_pairs={{8,0},{16,8},{24,16},{9,1},{17,9},{25,17},{10,2},{18,10},{26,18},{... | collective-permute-start | bytes 98312 | tf_op jit(solution)/shard_map/ppermute | solution.py:341
  25.1 5.6 %collective-permute-start.3 = (bf16[2,34,1,512]{3,1,0,2:T(8,128)(2,1)S(1)}, bf16[2,34,1,512]{3,1,0,2:T(8,128)(2,1)S(1)}, u32[]{:S(2)}, u32[]{:S(2)}) collective-permute-start(bf16[2,34,1,512]{3,1,0,2:T(8,128)(2,1)S(1)} %pad_maximum_fusion.1), channel_id=1, source_target_pairs={{1,0},{2,1},{3,2},{4,3},{5,4},{6,5},{7,6},{9,8},{10,9},{11,10},{12... | collective-permute-start | bytes 208904 | tf_op jit(solution)/shard_map/ppermute | solution.py:341
  26.5 4.3 %collective-permute-start.2 = (bf16[2,34,1,512]{3,1,0,2:T(8,128)(2,1)S(1)}, bf16[2,34,1,512]{3,1,0,2:T(8,128)(2,1)S(1)}, u32[]{:S(2)}, u32[]{:S(2)}) collective-permute-start(bf16[2,34,1,512]{3,1,0,2:T(8,128)(2,1)S(1)} %pad_maximum_fusion), channel_id=1, source_target_pairs={{0,1},{1,2},{2,3},{3,4},{4,5},{5,6},{6,7},{8,9},{9,10},{10,11},{11... | collective-permute-start | bytes 208904 | tf_op jit(solution)/shard_map/ppermute | solution.py:341
  30.7 0.6 copy-start.6
  30.8 0.7 copy-start.7
  44.3 38.8 %copy-start.2 = (bf16[32,32,512]{2,1,0:T(8,128)(2,1)}, bf16[32,32,512]{2,1,0:T(8,128)(2,1)S(1)}, u32[]{:S(2)}) copy-start(bf16[32,32,512]{2,1,0:T(8,128)(2,1)S(1)} %all-to-all-done.1) | copy-start | bytes 3145732
  44.3 38.7 %all-to-all-start = ((bf16[32,32,512]{2,1,0:T(8,128)(2,1)}), bf16[32,32,512]{2,1,0:T(8,128)(2,1)S(1)}, u32[]{:S(2)}, u32[]{:S(2)}) async-start(bf16[32,32,512]{2,1,0:T(8,128)(2,1)} %bitcast.27), calls=%async_computation | async-start | bytes 2097152 | tf_op jit(solution)/shard_map/all_to_all | solution.py:397
  83.0 1.0 copy-start.3
  115.3 4.7 %copy-start.1 = (bf16[512,2048]{1,0:T(8,128)(2,1)S(1)}, bf16[512,2048]{1,0:T(8,128)(2,1)}, u32[]{:S(2)}) copy-start(bf16[512,2048]{1,0:T(8,128)(2,1)} %get-tuple-element.17) | copy-start | bytes 6291460
  117.1 2.9 %collective-permute-start.8 = (bf16[256,2048]{1,0:T(8,128)(2,1)S(1)}, bf16[256,2048]{1,0:T(8,128)(2,1)}, u32[]{:S(2)}, u32[]{:S(2)}) collective-permute-start(bf16[256,2048]{1,0:T(8,128)(2,1)S(1)} %broadcast_select_fusion), channel_id=1, source_target_pairs={{0,1},{1,0},{2,3},{3,2},{4,5},{5,4},{6,7},{7,6},{8,9},{9,8},{10,11... | collective-permute-start | bytes 3145736 | tf_op jit(solution)/shard_map/ppermute | solution.py:366
  121.8 20.3 %collective-permute-start.9 = (bf16[128,2048]{1,0:T(8,128)(2,1)S(1)}, bf16[128,2048]{1,0:T(8,128)(2,1)S(1)}, u32[]{:S(2)}, u32[]{:S(2)}) collective-permute-start(bf16[128,2048]{1,0:T(8,128)(2,1)S(1)} %broadcast_select_fusion.1), channel_id=1, source_target_pairs={{0,8},{8,0},{16,24},{24,16},{1,9},{9,1},{17,25},{25,17},{2,10},{10... | collective-permute-start | bytes 1572872 | tf_op jit(solution)/shard_map/ppermute | solution.py:366
  122.4 30.2 %all-to-all-start.2 = ((bf16[32,32,512]{2,1,0:T(8,128)(2,1)}), bf16[32,32,512]{2,1,0:T(8,128)(2,1)S(1)}, u32[]{:S(2)}, u32[]{:S(2)}) async-start(bf16[32,32,512]{2,1,0:T(8,128)(2,1)} %bitcast.25), calls=%async_computation.2 | async-start | bytes 2097152 | tf_op jit(solution)/shard_map/all_to_all | solution.py:397
  142.4 8.3 %collective-permute-start.10 = (bf16[64,2048]{1,0:T(8,128)(2,1)S(1)}, bf16[64,2048]{1,0:T(8,128)(2,1)S(1)}, u32[]{:S(2)}, u32[]{:S(2)}) collective-permute-start(bf16[64,2048]{1,0:T(8,128)(2,1)S(1)} %broadcast_select_fusion.2), channel_id=1, source_target_pairs={{0,16},{8,24},{16,0},{24,8},{1,17},{9,25},{17,1},{25,9},{2,18},{10... | collective-permute-start | bytes 786440 | tf_op jit(solution)/shard_map/ppermute | solution.py:366
  152.6 1.0 copy-start
  158.0 3.8 %collective-permute-start.4 = (bf16[2,1,16,512]{3,1,0,2:T(2,128)(2,1)S(1)}, bf16[2,1,16,512]{3,1,0,2:T(2,128)(2,1)S(1)}, u32[]{:S(2)}, u32[]{:S(2)}) collective-permute-start(bf16[2,1,16,512]{3,1,0,2:T(2,128)(2,1)S(1)} %copy.30), channel_id=1, source_target_pairs={{0,8},{8,16},{16,24},{1,9},{9,17},{17,25},{2,10},{10,18},{18,26},{... | collective-permute-start | bytes 98312 | tf_op jit(solution)/shard_map/ppermute | solution.py:341
  160.5 6.8 %collective-permute-start.5 = (bf16[2,1,16,512]{3,1,0,2:T(2,128)(2,1)S(1)}, bf16[2,1,16,512]{3,1,0,2:T(2,128)(2,1)S(1)}, u32[]{:S(2)}, u32[]{:S(2)}) collective-permute-start(bf16[2,1,16,512]{3,1,0,2:T(2,128)(2,1)S(1)} %copy.31), channel_id=1, source_target_pairs={{8,0},{16,8},{24,16},{9,1},{17,9},{25,17},{10,2},{18,10},{26,18},{... | collective-permute-start | bytes 98312 | tf_op jit(solution)/shard_map/ppermute | solution.py:341
  167.4 6.7 %collective-permute-start.7 = (bf16[2,34,1,512]{3,1,0,2:T(8,128)(2,1)S(1)}, bf16[2,34,1,512]{3,1,0,2:T(8,128)(2,1)S(1)}, u32[]{:S(2)}, u32[]{:S(2)}) collective-permute-start(bf16[2,34,1,512]{3,1,0,2:T(8,128)(2,1)S(1)} %pad_maximum_fusion.3), channel_id=1, source_target_pairs={{1,0},{2,1},{3,2},{4,3},{5,4},{6,5},{7,6},{9,8},{10,9},{11,10},{12... | collective-permute-start | bytes 208904 | tf_op jit(solution)/shard_map/ppermute | solution.py:341
  168.7 5.4 %collective-permute-start.6 = (bf16[2,34,1,512]{3,1,0,2:T(8,128)(2,1)S(1)}, bf16[2,34,1,512]{3,1,0,2:T(8,128)(2,1)S(1)}, u32[]{:S(2)}, u32[]{:S(2)}) collective-permute-start(bf16[2,34,1,512]{3,1,0,2:T(8,128)(2,1)S(1)} %pad_maximum_fusion.2), channel_id=1, source_target_pairs={{0,1},{1,2},{2,3},{3,4},{4,5},{5,6},{6,7},{8,9},{9,10},{10,11},{11... | collective-permute-start | bytes 208904 | tf_op jit(solution)/shard_map/ppermute | solution.py:341
  171.8 26.9 %collective-permute-start.11 = (bf16[32,2048]{1,0:T(8,128)(2,1)S(1)}, bf16[32,2048]{1,0:T(8,128)(2,1)S(1)}, u32[]{:S(2)}, u32[]{:S(2)}) collective-permute-start(bf16[32,2048]{1,0:T(8,128)(2,1)S(1)} %broadcast_select_fusion.3), channel_id=1, source_target_pairs={{0,2},{1,3},{2,0},{3,1},{4,6},{5,7},{6,4},{7,5},{8,10},{9,11},{10,... | collective-permute-start | bytes 393224 | tf_op jit(solution)/shard_map/ppermute | solution.py:366
  174.1 0.6 copy-start.4
  174.1 0.7 copy-start.5
  194.9 1.4 collective-permute-start.13
  197.1 3.9 %collective-permute-start.14 = (f32[16,512]{1,0:T(8,128)S(1)}, f32[16,512]{1,0:T(8,128)S(1)}, u32[]{:S(2)}, u32[]{:S(2)}) collective-permute-start(f32[16,512]{1,0:T(8,128)S(1)} %add.61), channel_id=1, source_target_pairs={{0,8},{8,0},{16,24},{24,16},{1,9},{9,1},{17,25},{25,17},{2,10},{10... | collective-permute-start | bytes 98312 | tf_op jit(solution)/shard_map/ppermute | solution.py:366
  201.0 3.9 %collective-permute-start.15 = (f32[16,512]{1,0:T(8,128)S(1)}, f32[16,512]{1,0:T(8,128)S(1)}, u32[]{:S(2)}, u32[]{:S(2)}) collective-permute-start(f32[16,512]{1,0:T(8,128)S(1)} %add.62), channel_id=1, source_target_pairs={{0,16},{8,24},{16,0},{24,8},{1,17},{9,25},{17,1},{25,9},{2,18},{10... | collective-permute-start | bytes 98312 | tf_op jit(solution)/shard_map/ppermute | solution.py:366
  201.2 9.2 %collective-permute-start.12 = (bf16[16,2048]{1,0:T(8,128)(2,1)S(1)}, bf16[16,2048]{1,0:T(8,128)(2,1)S(1)}, u32[]{:S(2)}, u32[]{:S(2)}) collective-permute-start(bf16[16,2048]{1,0:T(8,128)(2,1)S(1)} %broadcast_select_fusion.4), channel_id=1, source_target_pairs={{0,4},{1,5},{2,6},{3,7},{4,0},{5,1},{6,2},{7,3},{8,12},{9,13},{10,... | collective-permute-start | bytes 196616 | tf_op jit(solution)/shard_map/ppermute | solution.py:366
  204.9 4.6 %collective-permute-start.16 = (f32[16,512]{1,0:T(8,128)S(1)}, f32[16,512]{1,0:T(8,128)S(1)}, u32[]{:S(2)}, u32[]{:S(2)}) collective-permute-start(f32[16,512]{1,0:T(8,128)S(1)} %add.63), channel_id=1, source_target_pairs={{0,2},{1,3},{2,0},{3,1},{4,6},{5,7},{6,4},{7,5},{8,10},{9,11},{10,... | collective-permute-start | bytes 98312 | tf_op jit(solution)/shard_map/ppermute | solution.py:366
  209.5 4.8 %collective-permute-start.17 = (f32[16,512]{1,0:T(8,128)S(1)}, f32[16,512]{1,0:T(8,128)S(1)}, u32[]{:S(2)}, u32[]{:S(2)}) collective-permute-start(f32[16,512]{1,0:T(8,128)S(1)} %add.64), channel_id=1, source_target_pairs={{0,4},{1,5},{2,6},{3,7},{4,0},{5,1},{6,2},{7,3},{8,12},{9,13},{10,... | collective-permute-start | bytes 98312 | tf_op jit(solution)/shard_map/ppermute | solution.py:366

commit v2 on v1

v2 whole, which is shorter than its diff:
```python
import functools

import jax
import jax.numpy as jnp
import numpy as np
from jax import lax
from jax.experimental import pallas as pl
from jax.experimental.pallas import tpu as pltpu
from jax.sharding import PartitionSpec as P

HEADS = 16
HEAD = 32
GRID = 8
CELLS = GRID * GRID
AXES = ("row", "col")
F32 = jnp.float32
BF16 = jnp.bfloat16
LIMIT = 56 * 1024 * 1024
UNROLL = 2
GROUP = 16


def dot(left, right, dims=((1,), (0,))):
    return lax.dot_general(left, right, (dims, ((), ())), preferred_element_type=F32)


def moves(pairs, sems):
    copies = [pltpu.make_async_copy(a, b, sems.at[n]) for n, (a, b) in enumerate(pairs)]
    for copy in copies:
        copy.start()
    return copies


class Plan:
    def __init__(self, batches, tile_rows, tile_cols, row_count, col_count):
        devices = row_count * col_count
        high = tile_rows * row_count // GRID
        full = tile_cols * col_count // GRID
        wide = min(full, tile_cols)
        groups = full // wide
        reps_r = tile_rows // high
        reps_s = tile_cols // wide
        reps = reps_r * reps_s
        share = devices // batches
        spots = [(a, e) for a in range(high) for e in range(wide)]
        edge = [c for c in spots if c[0] in (0, high - 1) or c[1] in (0, wide - 1)]
        rest = [c for c in spots if c not in set(edge)]
        place = {c: (n % share, n // share) for n, c in enumerate(edge + rest)}
        slots = len(spots) // share
        edge_slots = -(-len(edge) // share)
        bounds = [0, edge_slots, slots] if edge_slots < slots else [0, slots]
        cells = tile_rows * tile_cols

        def build(first, last):
            size = (last - first) * reps
            send = np.zeros((share * size, cells), np.float32)
            for h in range(tile_rows):
                for w in range(tile_cols):
                    owner, slot = place[(h % high, w % wide)]
                    if first <= slot < last:
                        rep = (h // high) * reps_s + w // wide
                        send[owner * size + (slot - first) * reps + rep, h * tile_cols + w] = 1
            count = (last - first) * groups
            seen = np.zeros((count,), np.int64)
            sort = np.zeros((devices * size, devices * size), np.float32)
            for source in range(devices):
                j = source % col_count
                for slot in range(last - first):
                    for r in range(reps_r):
                        for s in range(reps_s):
                            window = slot * groups + ((j * tile_cols + s * wide) % full) // wide
                            position = int(seen[window])
                            seen[window] += 1
                            chunk, lane = divmod(position, GROUP)
                            row = chunk * GROUP * count + window * GROUP + lane
                            sort[row, source * size + slot * reps + r * reps_s + s] = 1
            step = GROUP * count
            block = sort[:step, :step]
            assert (sort == np.kron(np.eye(CELLS // GROUP), block)).all()
            return send, block

        self.send_all, sort_all = build(0, slots)
        self.send, self.sort, self.take = [], [], []
        for first, last in zip(bounds[:-1], bounds[1:]):
            send, block = build(first, last)
            self.send.append(send)
            self.sort.append(block)
            self.take.append(sort_all[first * groups * GROUP : last * groups * GROUP])
        self.rows = [batches * m.shape[0] for m in self.send]
        spots = []
        for h in (0, tile_rows - 1):
            spots += [(b, h, w) for b in range(batches) for w in range(tile_cols)]
        for w in (0, tile_cols - 1):
            spots += [(b, h, w) for b in range(batches) for h in range(tile_rows)]
        self.pick = np.zeros((len(spots), batches * cells), np.float32)
        for n, (b, h, w) in enumerate(spots):
            self.pick[n, b * cells + h * tile_cols + w] = 1
        self.pick_sent = self.pick @ np.kron(np.eye(batches), self.send[0]).T


def send_kernel(batches, x_ref, order, out):
    cells = x_ref.shape[0] // batches
    for b in range(batches):
        at = slice(b * cells, (b + 1) * cells)
        out[at, :] = dot(order[...], x_ref[at, :]).astype(BF16)


def convolve(pad, left_ref, right_ref, kern, side_l, side_r, out_ref):
    batches, rows, cols, feats = pad.shape
    rows -= 2
    four = 4
    width = 256
    for b in range(batches):
        left, right = left_ref[b].astype(F32), right_ref[b].astype(F32)
        side_l[b] = sum(kern[i][0] * left[i : i + rows] for i in range(3))
        side_r[b] = sum(kern[i][2] * right[i : i + rows] for i in range(3))
    spot = lax.broadcasted_iota(jnp.int32, (cols, width), 0)
    for c in range(feats // width):
        at = slice(c * width, (c + 1) * width)
        taps = [[kern[i][j][:, at] for j in range(3)] for i in range(3)]
        for b in range(batches):

            def step(n, carry, b=b, at=at, taps=taps):
                first = n * four
                x = [pad[b, first + r, :, at].astype(F32) for r in range(four + 2)]
                for r in range(four):
                    low, mid, high = (
                        taps[0][j] * x[r] + taps[1][j] * x[r + 1] + taps[2][j] * x[r + 2]
                        for j in range(3)
                    )
                    h = first + r
                    low = jnp.where(spot == 0, side_l[b, pl.ds(h, 1), at], pltpu.roll(low, 1, 0))
                    high = jnp.where(
                        spot == cols - 1, side_r[b, pl.ds(h, 1), at], pltpu.roll(high, cols - 1, 0)
                    )
                    where = pl.ds(pl.multiple_of((b * rows + h) * cols, cols), cols)
                    out_ref[where, at] = (x[r + 1] + (low + mid + high)).astype(BF16)
                return carry

            lax.fori_loop(0, rows // four, step, 0)


def taps_of(dw_ref, flipped):
    side = lambda n: 2 - n if flipped else n
    return [
        [dw_ref[side(i), side(j) : side(j) + 1, :].astype(F32) for j in range(3)] for i in range(3)
    ]


def mix_kernel(lat_ref, top_ref, bot_ref, left_ref, right_ref, dw_ref, gain_ref, order, *refs):
    out, mixed_out, stat_out, pad_out = refs[:4]
    mixed_ref, stat_ref, pad_ref, normed_ref, side_l, side_r, sems = refs[4:]
    batches, rows, cols, feats = lat_ref.shape
    pad_ref[:, 1 : rows + 1] = lat_ref[...]
    pad_ref[:, 0] = top_ref[...]
    pad_ref[:, rows + 1] = bot_ref[...]
    copies = moves([(pad_ref, pad_out)], sems)
    convolve(pad_ref, left_ref, right_ref, taps_of(dw_ref, False), side_l, side_r, mixed_ref)
    copies += moves([(mixed_ref, mixed_out)], sems.at[1:2])
    block = 64

    def norm(n, carry):
        at = pl.ds(pl.multiple_of(n * block, block), block)
        mixed = mixed_ref[at, :].astype(F32)
        mean = jnp.mean(mixed, axis=-1, keepdims=True)
        centred = mixed - mean
        rstd = lax.rsqrt(jnp.mean(centred * centred, axis=-1, keepdims=True) + 1e-05)
        stat_ref[at, 0:1] = mean
        stat_ref[at, 1:2] = rstd
        normed_ref[at, :] = (centred * rstd * gain_ref[...]).astype(BF16)
        return carry

    lax.fori_loop(0, batches * rows * cols // block, norm, 0, unroll=2)
    copies += moves([(stat_ref, stat_out)], sems.at[2:3])
    send_kernel(batches, normed_ref, order, out)
    for copy in copies:
        copy.wait()


def gather_rows(source, take_ref, target):
    count = target.shape[0] // CELLS
    whole = source.shape[0] * GROUP // CELLS
    for p in range(CELLS // GROUP):
        ordered = dot(take_ref[...], source[p * whole : (p + 1) * whole, :]).astype(BF16)
        for w in range(count):
            target[w * CELLS + p * GROUP : w * CELLS + (p + 1) * GROUP, :] = ordered[
                w * GROUP : (w + 1) * GROUP
            ]


def grads_kernel(parts, g_ref, wout_ref, *refs):
    for n in range(parts):
        gw, datt = refs[parts + 2 * n : parts + 2 * n + 2]
        gather_rows(g_ref, refs[n], gw)
        rows = gw.shape[0]
        for first in range(0, rows, 256):
            at = slice(first, min(first + 256, rows))
            datt[at, :] = dot(gw[at, :], wout_ref[...], ((1,), (1,))).astype(BF16)


def window_kernel(counts, before, n_hbm, datt_hbm, take_ref, sort_ref, wqkv_hbm, *refs):
    n_ref, wqkv_ref, nw, packed, datt, att, dpacked, head_mask, half_mask, in_sems = refs[-10:]
    if counts is None:
        dn_ref, *results, out_sems = refs[:5]
    else:
        mine_ref, gw_hbm, *old = refs[: 4 * before + 2]
        dn_ref, keep_hbm, give_hbm, gw, acc, keep_ref, give_ref, out_sems, old_sems, *old_refs = refs[
            4 * before + 2 : -10
        ]
        late = moves([(gw_hbm, gw), *zip(old, old_refs)], old_sems)
    loads = moves([(n_hbm, n_ref), (wqkv_hbm, wqkv_ref), (datt_hbm, datt)], in_sems)
    rows, feats = dn_ref.shape
    count = rows // CELLS
    part = GROUP * count
    tiles = feats // 256
    scale = HEAD ** (-0.5)
    block = 256 if rows % 256 == 0 else CELLS

    head_mask[...] = (
        (lax.broadcasted_iota(jnp.int32, (4 * CELLS, 256), 1) // HEAD) % 4
        == lax.broadcasted_iota(jnp.int32, (4 * CELLS, 256), 0) // CELLS
    ).astype(F32).astype(BF16)
    half_mask[...] = (
        lax.broadcasted_iota(jnp.int32, (2 * CELLS, 256), 1) // 128
        == lax.broadcasted_iota(jnp.int32, (2 * CELLS, 256), 0) // CELLS
    ).astype(F32).astype(BF16)

    loads[0].wait()
    gather_rows(n_ref, take_ref, nw)
    loads[1].wait()

    def project(n, carry):
        at = pl.ds(pl.multiple_of(n * block, block), block)
        packed[at, :] = dot(nw[at, :], wqkv_ref[...]).astype(BF16)
        return carry

    lax.fori_loop(0, rows // block, project, 0)
    loads[2].wait()

    lane = lax.broadcasted_iota(jnp.int32, (CELLS, 256), 1)
    lane_half = lane < 128
    lane_head = (lane // HEAD) % 4

    def fold_heads(full):
        out = full[3 * CELLS :]
        for h in (2, 1, 0):
            out = jnp.where(lane_head == h, full[h * CELLS : (h + 1) * CELLS], out)
        return out

    def one(n, carry):
        at = pl.ds(pl.multiple_of(n * CELLS, CELLS), CELLS)
        for t in range(tiles):
            cols = [slice(p * feats + t * 256, p * feats + (t + 1) * 256) for p in range(3)]
            query = packed[at, cols[0]]
            key = packed[at, cols[1]]
            value = packed[at, cols[2]]
            grad = datt[at, t * 256 : (t + 1) * 256]
            key_big = jnp.concatenate([key] * 4, axis=0) * head_mask[...]
            value_big = jnp.concatenate([value] * 4, axis=0) * head_mask[...]
            query_two = jnp.concatenate([query] * 2, axis=0) * half_mask[...]
            grad_two = jnp.concatenate([grad] * 2, axis=0) * half_mask[...]
            scores = (dot(key_big, query_two, ((1,), (1,))) * scale).reshape(4, CELLS, 2 * CELLS)
            d_probs = dot(value_big, grad_two, ((1,), (1,))).reshape(4, CELLS, 2 * CELLS)
            raised = jnp.exp(scores - jnp.max(scores, axis=1, keepdims=True))
            probs = raised * (1.0 / jnp.sum(raised, axis=1, keepdims=True))
            probs_b = probs.astype(BF16).reshape(4 * CELLS, 2 * CELLS)
            inner = jnp.sum(probs * d_probs, axis=1, keepdims=True)
            d_scores = (
                (probs * (d_probs - inner) * scale).astype(BF16).reshape(4 * CELLS, 2 * CELLS)
            )
            out = dot(probs_b, value_big, ((0,), (0,)))
            att[at, t * 256 : (t + 1) * 256] = jnp.where(
                lane_half, out[:CELLS], out[CELLS:]
            ).astype(BF16)
            d_query = dot(d_scores, key_big, ((0,), (0,)))
            dpacked[at, cols[0]] = jnp.where(
                lane_half, d_query[:CELLS], d_query[CELLS:]
            ).astype(BF16)
            dpacked[at, cols[1]] = fold_heads(dot(d_scores, query_two)).astype(BF16)
            dpacked[at, cols[2]] = fold_heads(dot(probs_b, grad_two)).astype(BF16)
        return carry

    lax.fori_loop(0, count, one, 0, unroll=UNROLL)
    if counts is None:
        stores = moves(list(zip((nw, att, dpacked), results)), out_sems)
    else:
        for copy in late:
            copy.wait()
        parts = [old_refs[4 * n : 4 * n + 4] for n in range(before)] + [(nw, att, dpacked, gw)]
        weight_sums(parts, counts, mine_ref[0], acc, keep_ref, give_ref)
        stores = moves([(give_ref, give_hbm), (keep_ref, keep_hbm)], out_sems)

    def back(n, carry):
        at = pl.ds(pl.multiple_of(n * block, block), block)
        datt[at, :] = dot(dpacked[at, :], wqkv_ref[...], ((1,), (1,))).astype(BF16)
        return carry

    lax.fori_loop(0, rows // block, back, 0)
    for p in range(CELLS // GROUP):
        ordered = jnp.concatenate(
            [
                datt[w * CELLS + p * GROUP : w * CELLS + (p + 1) * GROUP, :]
                for w in range(count)
            ],
            axis=0,
        )
        dn_ref[p * part : (p + 1) * part, :] = dot(
            sort_ref[...], ordered, ((0,), (0,))
        ).astype(BF16)
    for copy in stores:
        copy.wait()


def place_of(i, j, row_count, chips):
    return (j % 2) * row_count * chips + i * chips + j // 2


def weight_sums(parts, counts, mine, acc, keep_ref, give_ref):
    feats = acc.shape[0]
    row_count, chips = counts
    devices = 2 * row_count * chips
    size = feats // devices
    half = devices // 2
    for left, right, start in ((0, 2, 0), (1, 3, 3 * feats)):
        turned = [part[left][...].T for part in parts]
        for t in range(parts[0][right].shape[1] // 256):
            at = slice(t * 256, (t + 1) * 256)
            acc[:, start + t * 256 : start + (t + 1) * 256] = sum(
                dot(x, part[right][:, at]) for x, part in zip(turned, parts)
            ).astype(BF16)
    if size % 16:
        source = lax.broadcasted_iota(jnp.int32, (feats, feats), 1)
        device = source // size
        place = place_of(device // (2 * chips), device % (2 * chips), row_count, chips)
        target = jnp.bitwise_xor(mine, place) * size + source % size
        order = (lax.broadcasted_iota(jnp.int32, (feats, feats), 0) == target).astype(F32).astype(BF16)
        keep_ref[...] = dot(order[: feats // 2], acc[...]).astype(BF16)
        give_ref[...] = dot(order[feats // 2 :], acc[...]).astype(BF16)
        return
    for n in range(devices):
        place = place_of(n // (2 * chips), n % (2 * chips), row_count, chips)
        block = jnp.bitwise_xor(mine, place)
        rows = acc[n * size : (n + 1) * size, :]
        at = pl.ds(pl.multiple_of((block % half) * size, size), size)

        @pl.when(block < half)
        def _(rows=rows, at=at):
            keep_ref[at, :] = rows

        @pl.when(block >= half)
        def _(rows=rows, at=at):
            give_ref[at, :] = rows


def norm_back(d_normed, nhat, rstd, grad, gain):
    scaled = d_normed * gain
    return (
        grad.astype(F32)
        + rstd
        * (
            scaled
            - jnp.mean(scaled, axis=-1, keepdims=True)
            - nhat * jnp.mean(scaled * nhat, axis=-1, keepdims=True)
        )
    ).astype(BF16)


def border_kernel(dn_ref, mixed_ref, grad_ref, pick_sent_ref, pick_ref, gain_ref, *outs):
    d_normed = dot(pick_sent_ref[...], dn_ref[...])
    mixed = dot(pick_ref[...], mixed_ref[...])
    grad = dot(pick_ref[...], grad_ref[...])
    centred = mixed - jnp.mean(mixed, axis=-1, keepdims=True)
    rstd = lax.rsqrt(jnp.mean(centred * centred, axis=-1, keepdims=True) + 1e-05)
    d_mixed = norm_back(d_normed, centred * rstd, rstd, grad, gain_ref[...])
    start = 0
    for out in outs:
        out[...] = d_mixed[start : start + out.shape[0]]
        start += out.shape[0]


def sums_kernel(count, *refs):
    parts, orders, refs = refs[:count], refs[count : 2 * count], refs[2 * count :]
    hbm, (left_ref, right_ref, gain_ref) = refs[:4], refs[4:7]
    out_ref, sums_ref, dn, side_l, side_r = refs[7:12]
    here, sems = refs[12:16], refs[16]
    stat_ref, mixed_ref, grad_ref, pad_ref = here
    loads = moves(list(zip(hbm, here)), sems)
    batches, rows, cols, feats = pad_ref.shape
    rows -= 2
    cells = rows * cols
    for b in range(batches):
        total = None
        for order, part in zip(orders, parts):
            size = part.shape[0] // batches
            term = dot(order[...], part[b * size : (b + 1) * size, :])
            total = term if total is None else total + term
        dn[b * cells : (b + 1) * cells, :] = total
    block = 64
    for copy in loads[:3]:
        copy.wait()

    def norm(n, gain_sum):
        at = pl.ds(pl.multiple_of(n * block, block), block)
        d_normed = dn[at, :]
        rstd = stat_ref[at, 1:2]
        nhat = (mixed_ref[at, :].astype(F32) - stat_ref[at, 0:1]) * rstd
        out_ref[at, :] = norm_back(d_normed, nhat, rstd, grad_ref[at, :], gain_ref[...])
        return gain_sum + jnp.sum((d_normed * nhat).reshape(block // 8, 8, feats), axis=0)

    gain_sum = lax.fori_loop(
        0, batches * cells // block, norm, jnp.zeros((8, feats), F32), unroll=2
    )
    sums_ref[9:10, :] = jnp.sum(gain_sum, axis=0, keepdims=True)
    sums_ref[10:, :] = jnp.zeros((sums_ref.shape[0] - 10, feats), F32)
    loads[3].wait()

    four = 4
    width = 256
    spot = lax.broadcasted_iota(jnp.int32, (cols, width), 0)
    fold = lambda v: jnp.sum(v.reshape(cols // 8, 8, width), axis=0)
    for c in range(feats // width):
        lanes = slice(c * width, (c + 1) * width)
        sums = [jnp.zeros((8, width), F32) for _ in range(9)]
        for b in range(batches):

            def step(n, sums, b=b, lanes=lanes):
                start = n * four
                x = [pad_ref[b, start + r, :, lanes].astype(F32) for r in range(four + 2)]
                sums = list(sums)
                for r in range(four):
                    h = start + r
                    at = pl.ds(pl.multiple_of((b * rows + h) * cols, cols), cols)
                    d_mixed = out_ref[at, lanes].astype(F32)
                    side_l[b, pl.ds(h, 1), lanes] = d_mixed[:1]
                    side_r[b, pl.ds(h, 1), lanes] = d_mixed[cols - 1 :]
                    moved = (
                        jnp.where(spot == cols - 1, 0.0, pltpu.roll(d_mixed, cols - 1, 0)),
                        d_mixed,
                        jnp.where(spot == 0, 0.0, pltpu.roll(d_mixed, 1, 0)),
                    )
                    for i in range(3):
                        for j in range(3):
                            sums[3 * i + j] = sums[3 * i + j] + fold(moved[j] * x[r + i])
                return tuple(sums)

            sums = lax.fori_loop(0, rows // four, step, tuple(sums))
        for n in range(9):
            sums_ref[n : n + 1, lanes] = jnp.sum(sums[n], axis=0, keepdims=True)
    for i in range(3):
        for b in range(batches):
            left, right = left_ref[b].astype(F32), right_ref[b].astype(F32)
            sums_ref[3 * i : 3 * i + 1, :] += jnp.sum(
                side_l[b] * left[i : i + rows], axis=0, keepdims=True
            )
            sums_ref[3 * i + 2 : 3 * i + 3, :] += jnp.sum(
                side_r[b] * right[i : i + rows], axis=0, keepdims=True
            )


def spread_kernel(d_ref, top_ref, bot_ref, left_ref, right_ref, dw_ref, out_ref, pad, side_l, side_r):
    batches, rows, cols, feats = pad.shape
    rows -= 2
    for b in range(batches):
        for h in range(rows):
            pad[b, h + 1] = d_ref[(b * rows + h) * cols : (b * rows + h + 1) * cols, :]
    pad[:, 0] = top_ref[...]
    pad[:, rows + 1] = bot_ref[...]
    convolve(pad, left_ref, right_ref, taps_of(dw_ref, True), side_l, side_r, out_ref)


def call(body, outs, scratch, args, micros, name, hbm_ins=(), hbm_outs=(), scalars=()):
    moved = sum(int(np.prod(o.shape)) * o.dtype.itemsize for o in (*outs, *args))
    vmem = pl.BlockSpec(memory_space=pltpu.VMEM)
    hbm = pl.BlockSpec(memory_space=pl.ANY)
    smem = pl.BlockSpec(memory_space=pltpu.SMEM)
    return pl.pallas_call(
        body,
        out_shape=outs,
        in_specs=[
            smem if n in scalars else hbm if n in hbm_ins else vmem for n in range(len(args))
        ],
        out_specs=[hbm if n in hbm_outs else vmem for n in range(len(outs))],
        scratch_shapes=scratch,
        compiler_params=pltpu.CompilerParams(vmem_limit_bytes=LIMIT),
        cost_estimate=pl.CostEstimate(
            flops=micros * 10**9, bytes_accessed=moved, transcendentals=0
        ),
        name=name,
    )(*args)


def shape(dims, dtype):
    return jax.ShapeDtypeStruct(tuple(dims), dtype)


def shifted(cells, axis, step):
    count = lax.axis_size(axis)
    return lax.ppermute(cells, axis, [(n, n + step) for n in range(count) if 0 <= n + step < count])


def halos(top, bottom, left, right):
    above = shifted(bottom, "row", 1)
    below = shifted(top, "row", -1)
    last = above.shape[1] - 1
    column = lambda own, at: jnp.concatenate(
        [above[:, at : at + 1], own, below[:, at : at + 1]], axis=1
    )
    from_left = shifted(column(right, last), "col", 1)
    from_right = shifted(column(left, 0), "col", -1)
    return above, below, from_left, from_right


def swap(x, axis, step):
    return lax.ppermute(x, axis, [(n, n ^ step) for n in range(lax.axis_size(axis))])


def total(values):
    while len(values) > 1:
        values = [a + b for a, b in zip(values[::2], values[1::2])]
    return values[0]


def scatter(blocks, sums, axis, unit, count):
    size = blocks.shape[0] // count
    sums = sums.reshape(size, -1)
    load = lambda n: jnp.concatenate([blocks[n * size : (n + 1) * size], sums], axis=1).astype(BF16)
    own = jnp.concatenate([blocks[:size], sums], axis=1)
    return [own, *(swap(load(n), axis, unit * n).astype(F32) for n in range(1, count))]


def shards(plan, latent, w_qkv, w_out, ln_gain, dw_kernel, grad_out):
    batches, rows, cols, feats = latent.shape
    row_count, col_count = lax.axis_size("row"), lax.axis_size("col")
    cells = batches * rows * cols
    parts = len(plan.rows)
    gain = ln_gain.reshape(1, feats)
    send = jnp.asarray(plan.send_all, BF16)
    back = [jnp.asarray(np.ascontiguousarray(m.T), BF16) for m in plan.send]
    sort = [jnp.asarray(m, BF16) for m in plan.sort]
    take = [jnp.asarray(m, BF16) for m in plan.take]
    chunks = [shape((n, feats), BF16) for n in plan.rows]
    trade = lambda x: lax.all_to_all(x, AXES, split_axis=0, concat_axis=0, tiled=True)
    grad_flat = grad_out.reshape(cells, feats)

    flat = shape((cells, feats), BF16)
    (grad_sent,) = call(
        functools.partial(send_kernel, batches), [flat], [], [grad_flat, send], 3, "grad_send"
    )
    grad_win = trade(grad_sent)

    above, below, left, right = halos(latent[:, 0], latent[:, -1], latent[:, :, 0], latent[:, :, -1])
    padded = (batches, rows + 2, cols, feats)
    side = pltpu.VMEM((batches, rows, feats), F32)
    stat_shape = (cells, 2)
    normed, mixed, stat, pad = call(
        mix_kernel,
        [flat, flat, shape(stat_shape, F32), shape(padded, BF16)],
        [
            pltpu.VMEM((cells, feats), BF16),
            pltpu.VMEM(stat_shape, F32),
            pltpu.VMEM(padded, BF16),
            pltpu.VMEM((cells, feats), BF16),
            side,
            side,
            pltpu.SemaphoreType.DMA((3,)),
        ],
        [latent, above, below, left, right, dw_kernel, gain, send],
        6,
        "mix",
        hbm_outs=(1, 2, 3),
    )
    normed_win = trade(normed)

    chips = col_count // 2
    ahead = call(
        functools.partial(grads_kernel, parts),
        [chunks[n // 2] for n in range(2 * parts)],
        [],
        [grad_win, w_out, *take],
        4,
        "grads",
    )
    mine = place_of(lax.axis_index("row"), lax.axis_index("col"), row_count, chips).astype(jnp.int32).reshape(1)
    half = shape((feats // 2, 4 * feats), BF16)
    d_parts, kept = [], []
    for n in range(parts):
        count = plan.rows[n]
        last = n == parts - 1
        mat = lambda width: pltpu.VMEM((count, width), BF16)
        args = [normed_win, ahead[2 * n + 1], take[n], sort[n], w_qkv]
        if last:
            outs = [chunks[n], half, half]
            args += [mine, ahead[2 * n], *kept]
            scratch = [
                mat(feats),
                pltpu.VMEM((feats, 4 * feats), BF16),
                pltpu.VMEM(half.shape, BF16),
                pltpu.VMEM(half.shape, BF16),
                pltpu.SemaphoreType.DMA((2,)),
                pltpu.SemaphoreType.DMA((1 + len(kept),)),
                *(pltpu.VMEM(x.shape, BF16) for x in kept),
            ]
        else:
            outs = [chunks[n], chunks[n], chunks[n], shape((count, 3 * feats), BF16)]
            scratch = [pltpu.SemaphoreType.DMA((3,))]
        d_chunk, *saved = call(
            functools.partial(window_kernel, (row_count, chips) if last else None, n),
            outs,
            [
                *scratch,
                pltpu.VMEM((cells, feats), BF16),
                pltpu.VMEM((feats, 3 * feats), BF16),
                mat(feats),
                mat(3 * feats),
                mat(feats),
                mat(feats),
                mat(3 * feats),
                pltpu.VMEM((4 * CELLS, 256), BF16),
                pltpu.VMEM((2 * CELLS, 256), BF16),
                pltpu.SemaphoreType.DMA((3,)),
            ],
            args,
            2 + 20 * count // sum(plan.rows),
            "windows",
            hbm_ins=(0, 1, 4, *range(6, len(args))),
            hbm_outs=tuple(range(1, len(outs))),
            scalars=(5,),
        )
        kept += [*saved, ahead[2 * n]]
        d_parts.append(trade(d_chunk))
    keep, give = saved

    tops, sides = batches * cols, batches * rows
    borders = call(
        border_kernel,
        [shape((n, feats), BF16) for n in (tops, tops, sides, sides)],
        [],
        [
            d_parts[0],
            mixed,
            grad_flat,
            jnp.asarray(plan.pick_sent, BF16),
            jnp.asarray(plan.pick, BF16),
            gain,
        ],
        3,
        "border",
    )
    d_halos = halos(*(x.reshape(batches, -1, feats) for x in borders))

    weights = (keep.astype(F32) + swap(give, "col", 1).astype(F32)).astype(BF16)
    *d_parts, above, below, from_left, from_right = lax.optimization_barrier((*d_parts, *d_halos))
    d_halos = (above, below, from_left, from_right)
    d_mixed, sums = call(
        functools.partial(sums_kernel, parts),
        [flat, shape((16, feats), F32)],
        [
            pltpu.VMEM((cells, feats), F32),
            side,
            side,
            pltpu.VMEM(stat_shape, F32),
            pltpu.VMEM((cells, feats), BF16),
            pltpu.VMEM((cells, feats), BF16),
            pltpu.VMEM(padded, BF16),
            pltpu.SemaphoreType.DMA((4,)),
        ],
        [*d_parts, *back, stat, mixed, grad_flat, pad, left, right, gain],
        7,
        "sums",
        hbm_ins=tuple(range(2 * parts, 2 * parts + 4)),
    )
    (grad_latent,) = call(
        spread_kernel,
        [flat],
        [pltpu.VMEM(padded, BF16), side, side],
        [d_mixed, *d_halos, dw_kernel],
        5,
        "spread",
    )
    wide = 4 * feats
    size = weights.shape[0] // row_count
    gives = [
        swap(weights[n * size : (n + 1) * size], "row", n).astype(F32) for n in range(1, row_count)
    ]
    weights = total([weights[:size].astype(F32), *gives])
    sums = sums + swap(sums, "col", 1)
    sums = total([sums, *(swap(sums, "row", n) for n in range(1, row_count))])
    level = scatter(weights, sums, "col", 2, chips)
    part = lambda first, last: total([x[:, first:last] for x in level])
    sums = part(wide, None).reshape(16, feats)
    return (
        grad_latent.reshape(latent.shape),
        part(0, 3 * feats),
        part(3 * feats, wide),
        sums[9],
        sums[:9].reshape(3, 3, feats),
    )


def solution(mesh):
    row_count, col_count = mesh.shape["row"], mesh.shape["col"]

    def run(latent, w_qkv, w_out, ln_gain, dw_kernel, grad_out):
        batches, rows, cols, _ = latent.shape
        plan = Plan(batches, rows // row_count, cols // col_count, row_count, col_count)
        in_specs = (P(None, "row", "col", None), P(), P(), P(), P(), P(None, "row", "col", None))
        out_specs = (
            P(None, "row", "col", None),
            P(AXES, None),
            P(AXES, None),
            P(),
            P(),
        )
        return jax.shard_map(
            functools.partial(shards, plan),
            mesh=mesh,
            in_specs=in_specs,
            out_specs=out_specs,
            check_vma=False,
        )(latent, w_qkv, w_out, ln_gain, dw_kernel, grad_out)

    return run
```

time: 216 us -> 173 us (0.80)
  waiting for transfers between devices: 78.1 us -> 46.4 us
  Pallas kernels: 72 us -> 59.1 us
  starting transfers between devices: 47 us -> 57.1 us
  local copies, waits for them, and re-layouts: 12.3 us -> 5.88 us
  other arithmetic: 5.01 us -> 2.03 us
    ppermute x10 -> x11, waiting for transfers between devices: 37.6 us -> 3.99 us  [swap(): lax.ppermute(x, axis, [(n, n ^ step) for n in range(lax.axis_size(axis))])]
    pallas_call x5 -> x8, Pallas kernels: 72 us -> 59.1 us  [call(): pl.pallas_call(body, out_shape=outs, in_specs=[smem if n in scalars else...]
    all_to_all x3 -> x4, waiting for transfers between devices: 29.4 us -> 37.2 us  [shards(): lax.all_to_all(x, AXES, split_axis=0, concat_axis=0, tiled=True)]
    all_to_all x3 -> x4, starting transfers between devices: 21.1 us -> 27.1 us  [shards(): lax.all_to_all(x, AXES, split_axis=0, concat_axis=0, tiled=True)]
    ppermute x8, waiting for transfers between devices: 11.1 us -> 5.23 us  [shifted(): lax.ppermute(cells, axis, [(n, n + step) for n in range(count) if 0 <= n...]
    ppermute x10 -> x11, starting transfers between devices: 9.47 us -> 13.4 us  [swap(): lax.ppermute(x, axis, [(n, n ^ step) for n in range(lax.axis_size(axis))])]
    slice x10 -> x7, local copies, waits for them, and re-layouts: 5.16 us -> 1.54 us  [the longest x1 1.41 us: shards(): latent[:, :, 0]]
    ppermute x4 -> x0, local copies, waits for them, and re-layouts: 2.48 us -> none  [shifted(): lax.ppermute(cells, axis, [(n, n + step) for n in range(count) if 0 <= n...]
  transfers between devices with their start and end apart: 21 -> 23, of which waited for: 13 -> 10; matrix products, arithmetic and copies ran while one was open for 4% -> 2% of each run, Pallas kernels for 15% -> 28%
where the time goes in v2:
time: 173 us; the launch traced here: 172 us
  Pallas kernels  59.1 us (34%)
  starting transfers between devices  57.1 us (33%)
  waiting for transfers between devices  46.4 us (27%)
  local copies, waits for them, and re-layouts  5.88 us (3%)
  other arithmetic  2.03 us (1%)
    pallas_call x8, Pallas kernels, call(): pl.pallas_call(body, out_shape=outs, in_specs=[smem if n in scalars else...  59.1 us
    all_to_all x4, waiting for transfers between devices, shards(): lax.all_to_all(x, AXES, split_axis=0, concat_axis=0, tiled=True)  37.2 us
    all_to_all x4, starting transfers between devices, shards(): lax.all_to_all(x, AXES, split_axis=0, concat_axis=0, tiled=True)  27.1 us
    ppermute x8, starting transfers between devices, shifted(): lax.ppermute(cells, axis, [(n, n + step) for n in range(count) if 0 <= n...  16.6 us
    ppermute x11, starting transfers between devices, swap(): lax.ppermute(x, axis, [(n, n ^ step) for n in range(lax.axis_size(axis))])  13.4 us
    ppermute x8, waiting for transfers between devices, shifted(): lax.ppermute(cells, axis, [(n, n + step) for n in range(count) if 0 <= n...  5.23 us
    ppermute x11, waiting for transfers between devices, swap(): lax.ppermute(x, axis, [(n, n ^ step) for n in range(lax.axis_size(axis))])  3.99 us
  transfers between devices with their start and end apart: 23, of which 10 were waited for; matrix products, arithmetic and copies ran while one was open for 2% of the time, Pallas kernels for 28%

profile of v2, /device:TPU:0, one launch (start us, length us, event | category | flops | bytes accessed | tf_op | source)
XLA Modules:
  0.0 171.6 jit_solution(8085616047987658087)
XLA Ops:
  0.6 3.1 %grad_send.1 = bf16[1024,512]{1,0:T(8,128)(2,1)} custom-call(bf16[1024,512]{1,0:T(8,128)(2,1)} %bitcast.46, bf16[512,512]{1,0:T(8,128)(2,1)} %constant.54.clone.order), custom_call_target="tpu_custom_call" | custom-call | flops 3000000000 | bytes 2621440 | tf_op jit(solution)/shard_map/grad_send/pallas_call | solution.py:476
  3.7 7.3 %all-to-all-start.1 = ((bf16[32,32,512]{2,1,0:T(8,128)(2,1)}), bf16[32,32,512]{2,1,0:T(8,128)(2,1)S(1)}, u32[]{:S(2)}, u32[]{:S(2)}) async-start(bf16[32,32,512]{2,1,0:T(8,128)(2,1)} %bitcast.36), calls=%async_computation.1 | async-start | bytes 2097152 | tf_op jit(solution)/shard_map/all_to_all | solution.py:542
  11.0 0.8 slice_bitcast_fusion
  11.8 1.3 collective-permute-start.1
  13.1 4.5 %collective-permute-start = (bf16[2,16,512]{2,1,0:T(8,128)(2,1)S(1)}, bf16[2,16,512]{2,1,0:T(8,128)(2,1)S(1)}, u32[]{:S(2)}, u32[]{:S(2)}) collective-permute-start(bf16[2,16,512]{2,1,0:T(8,128)(2,1)S(1)} %get-tuple-element.69), channel_id=1, source_target_pairs={{0,8},{8,16},{16,24},{1,9},{9,17},{17,25},{2,10},{10,18},{18,26},{... | collective-permute-start | bytes 98312 | tf_op jit(solution)/shard_map/ppermute | solution.py:498
  17.6 1.4 fusion.6
  19.1 0.0 collective-permute-done.1.bot_ref
  19.1 0.3 collective-permute-done.top_ref
  19.5 1.6 collective-permute-start.2
  21.2 1.3 collective-permute-start.3
  22.5 0.0 collective-permute-done.2.left_ref.refs_8_
  22.5 0.0 copy-start.11
  22.5 3.4 %collective-permute-done.3.right_ref.refs_9_ = bf16[2,34,512]{2,1,0:T(8,128)(2,1)S(1)} collective-permute-done((bf16[2,34,512]{2,1,0:T(8,128)(2,1)S(1)}, bf16[2,34,512]{2,1,0:T(8,128)(2,1)S(1)}, u32[]{:S(2)}, u32[]{:S(2)}) %collective-permute-start.3) | collective-permute-done | bytes 69664 | tf_op jit(solution)/shard_map/ppermute | solution.py:498
  25.9 0.6 copy-done.12
  26.5 7.1 %mix.1 = (bf16[1024,512]{1,0:T(8,128)(2,1)}, bf16[1024,512]{1,0:T(8,128)(2,1)}, f32[1024,2]{1,0:T(8,128)}, bf16[2,34,16,512]{3,2,1,0:T(8,128)(2,1)}) custom-call(bf16[2,32,16,512]{3,2,1,0:T(8,128)(2,1)} %lat_ref.1, bf16[2,16,512]{2,1,0:T(8,128)(2,1)} %copy-done.10, bf16[2,16,512]{2,1,0:T(8,128)(2,1)} %copy-done.9, bf16[2,34,512]{2,1,0:T(8,128)(2,1)} %copy-done.11, ...), custom_call_target="tpu_custom_call" | custom-call | flops 6000000000 | bytes 5008384 | tf_op jit(solution)/shard_map/mix/pallas_call | solution.py:476
  33.6 5.0 %all-to-all-done.1 = bf16[32,32,512]{2,1,0:T(8,128)(2,1)S(1)} async-done(((bf16[32,32,512]{2,1,0:T(8,128)(2,1)}), bf16[32,32,512]{2,1,0:T(8,128)(2,1)S(1)}, u32[]{:S(2)}, u32[]{:S(2)}) %all-to-all-start.1) | async-done | bytes 1048608 | tf_op jit(solution)/shard_map/all_to_all | solution.py:542
  38.6 10.0 %all-to-all-start = ((bf16[32,32,512]{2,1,0:T(8,128)(2,1)}), bf16[32,32,512]{2,1,0:T(8,128)(2,1)S(1)}, u32[]{:S(2)}, u32[]{:S(2)}) async-start(bf16[32,32,512]{2,1,0:T(8,128)(2,1)} %bitcast.35), calls=%async_computation | async-start | bytes 2097152 | tf_op jit(solution)/shard_map/all_to_all | solution.py:542
  48.7 3.6 %grads.1 = (bf16[256,512]{1,0:T(8,128)(2,1)}, bf16[256,512]{1,0:T(8,128)(2,1)}, bf16[768,512]{1,0:T(8,128)(2,1)}, bf16[768,512]{1,0:T(8,128)(2,1)}) custom-call(bf16[1024,512]{1,0:T(8,128)(2,1)} %bitcast.32, bf16[512,512]{1,0:T(8,128)(2,1)} %wout_ref.1, bf16[64,256]{1,0:T(8,128)(2,1)} %constant.59.clone.refs_0_.take_ref, ...), custom_call_target="tpu_custom_call" | custom-call | flops 4000000000 | bytes 3801088 | tf_op jit(solution)/shard_map/grads/pallas_call | solution.py:476
  52.2 24.0 %all-to-all-done = bf16[32,32,512]{2,1,0:T(8,128)(2,1)S(1)} async-done(((bf16[32,32,512]{2,1,0:T(8,128)(2,1)}), bf16[32,32,512]{2,1,0:T(8,128)(2,1)S(1)}, u32[]{:S(2)}, u32[]{:S(2)}) %all-to-all-start) | async-done | bytes 1048608 | tf_op jit(solution)/shard_map/all_to_all | solution.py:542
  76.2 1.0 copy-done.2
  77.2 8.2 %windows.2 = (bf16[256,512]{1,0:T(8,128)(2,1)}, bf16[256,512]{1,0:T(8,128)(2,1)}, bf16[256,512]{1,0:T(8,128)(2,1)}, bf16[256,1536]{1,0:T(8,128)(2,1)}) custom-call(bf16[1024,512]{1,0:T(8,128)(2,1)} %bitcast.33, bf16[256,512]{1,0:T(8,128)(2,1)} %get-tuple-element.33.datt_hbm, bf16[64,256]{1,0:T(8,128)(2,1)} %constant.59.clone.refs_0_.take_ref, ...), custom_call_target="tpu_custom_call" | custom-call | flops 7000000000 | bytes 4497408 | tf_op jit(solution)/shard_map/windows/pallas_call | solution.py:476
  85.4 2.6 %all-to-all-start.2 = ((bf16[32,8,512]{2,1,0:T(8,128)(2,1)}), bf16[32,8,512]{2,1,0:T(8,128)(2,1)S(1)}, u32[]{:S(2)}, u32[]{:S(2)}) async-start(bf16[32,8,512]{2,1,0:T(8,128)(2,1)} %bitcast.41), calls=%async_computation.2 | async-start | bytes 524288 | tf_op jit(solution)/shard_map/all_to_all | solution.py:542
  88.0 21.5 %windows.3 = (bf16[768,512]{1,0:T(8,128)(2,1)}, bf16[256,2048]{1,0:T(8,128)(2,1)}, bf16[256,2048]{1,0:T(8,128)(2,1)}) custom-call(bf16[1024,512]{1,0:T(8,128)(2,1)} %bitcast.34, bf16[768,512]{1,0:T(8,128)(2,1)} %get-tuple-element.35.datt_hbm, bf16[192,256]{1,0:T(8,128)(2,1)} %constant.60.clone.refs_1_.take_ref, bf16[192,192]{1,0:T(8,128)(2,1)} %constant.58.clone.sort_ref, ...), custom_call_target="tpu_custom_call" | custom-call | flops 16999999488 | bytes 8822788 | tf_op jit(solution)/shard_map/windows/pallas_call | solution.py:476
  109.5 0.2 collective-permute-start.8
  109.7 0.0 all-to-all-done.2
  109.7 0.7 copy-done.3
  110.4 3.1 %border.1 = (bf16[32,512]{1,0:T(8,128)(2,1)}, bf16[32,512]{1,0:T(8,128)(2,1)}, bf16[64,512]{1,0:T(8,128)(2,1)}, bf16[64,512]{1,0:T(8,128)(2,1)}) custom-call(bf16[256,512]{1,0:T(8,128)(2,1)} %bitcast.39, bf16[1024,512]{1,0:T(8,128)(2,1)} %get-tuple-element.42.mixed_ref.refs_5_, bf16[1024,512]{1,0:T(8,128)(2,1)} %bitcast.47, ...), custom_call_target="tpu_custom_call" | custom-call | flops 3000000000 | bytes 3049472 | tf_op jit(solution)/shard_map/border/pallas_call | solution.py:476
  113.5 1.4 collective-permute-start.5
  114.9 7.2 %all-to-all-start.3 = ((bf16[32,24,512]{2,1,0:T(8,128)(2,1)}), bf16[32,24,512]{2,1,0:T(8,128)(2,1)}, u32[]{:S(2)}, u32[]{:S(2)}) async-start(bf16[32,24,512]{2,1,0:T(8,128)(2,1)} %bitcast.13), calls=%async_computation.3 | async-start | bytes 1572864 | tf_op jit(solution)/shard_map/all_to_all | solution.py:542
  122.1 3.6 %collective-permute-start.4 = (bf16[2,16,512]{2,1,0:T(8,128)(2,1)S(1)}, bf16[2,16,512]{2,1,0:T(8,128)(2,1)S(1)}, u32[]{:S(2)}, u32[]{:S(2)}) collective-permute-start(bf16[2,16,512]{2,1,0:T(8,128)(2,1)S(1)} %bitcast.49), channel_id=1, source_target_pairs={{0,8},{8,16},{16,24},{1,9},{9,17},{17,25},{2,10},{10,18},{18,26},{... | collective-permute-start | bytes 98312 | tf_op jit(solution)/shard_map/ppermute | solution.py:498
  125.7 0.0 collective-permute-done.5.bot_ref
  125.8 1.5 collective-permute-done.4.top_ref
  127.4 1.6 collective-permute-start.6
  129.0 1.3 collective-permute-start.7
  130.3 0.0 collective-permute-done.8
  130.3 0.4 add_convert_fusion
  130.7 0.1 fusion.5
  130.8 2.7 %collective-permute-start.9 = (bf16[64,2048]{1,0:T(8,128)(2,1)S(1)}, bf16[64,2048]{1,0:T(8,128)(2,1)S(1)}, u32[]{:S(2)}, u32[]{:S(2)}) collective-permute-start(bf16[64,2048]{1,0:T(8,128)(2,1)S(1)} %get-tuple-element.63), channel_id=1, source_target_pairs={{0,8},{8,0},{16,24},{24,16},{1,9},{9,1},{17,25},{25,17},{2,10},{10... | collective-permute-start | bytes 786440 | tf_op jit(solution)/shard_map/ppermute | solution.py:514
  133.5 2.4 %collective-permute-start.11 = (bf16[64,2048]{1,0:T(8,128)(2,1)S(1)}, bf16[64,2048]{1,0:T(8,128)(2,1)S(1)}, u32[]{:S(2)}, u32[]{:S(2)}) collective-permute-start(bf16[64,2048]{1,0:T(8,128)(2,1)S(1)} %get-tuple-element.64), channel_id=1, source_target_pairs={{0,24},{8,16},{16,8},{24,0},{1,25},{9,17},{17,9},{25,1},{2,26},{10... | collective-permute-start | bytes 786440 | tf_op jit(solution)/shard_map/ppermute | solution.py:514
  135.9 0.0 collective-permute-start.10
  135.9 0.0 collective-permute-done.6.left_ref
  135.9 0.0 collective-permute-done.7.right_ref
  136.0 8.2 %all-to-all-done.3 = bf16[32,24,512]{2,1,0:T(8,128)(2,1)} async-done(((bf16[32,24,512]{2,1,0:T(8,128)(2,1)}), bf16[32,24,512]{2,1,0:T(8,128)(2,1)}, u32[]{:S(2)}, u32[]{:S(2)}) %all-to-all-start.3) | async-done | bytes 786464 | tf_op jit(solution)/shard_map/all_to_all | solution.py:542
  144.1 8.1 %sums.1 = (bf16[1024,512]{1,0:T(8,128)(2,1)}, f32[16,512]{1,0:T(8,128)}) custom-call(bf16[256,512]{1,0:T(8,128)(2,1)} %bitcast.40, bf16[768,512]{1,0:T(8,128)(2,1)} %bitcast.14.refs_1_, bf16[512,128]{1,0:T(8,128)(2,1)} %constant.55.clone.refs_2_, bf16[512,384]{1,0:T(8,128)(2,1)} %constant.56.clone.refs_3_, f32[1024,2]{1,0:T(8,128)} %get-tuple-element.49.refs_4_, ...), custom_call_target="tpu_custom_call" | custom-call | flops 7000000000 | bytes 6014976 | tf_op jit(solution)/shard_map/sums/pallas_call | solution.py:476
  152.3 0.0 copy-start.6
  152.3 0.1 collective-permute-start.12
  152.4 0.0 collective-permute-done.9
  152.4 0.0 collective-permute-done.10
  152.4 0.1 fusion.3
  152.6 1.2 collective-permute-done.12
  153.8 0.7 collective-permute-start.15
  154.6 1.5 collective-permute-start.14
  156.0 1.3 collective-permute-start.13
  157.4 1.6 collective-permute-done.15
  159.0 0.9 collective-permute-done.13
  160.0 0.6 collective-permute-start.16
  160.6 2.2 %collective-permute-start.17 = (bf16[16,2560]{1,0:T(8,128)(2,1)S(1)}, bf16[16,2560]{1,0:T(8,128)(2,1)S(1)}, u32[]{:S(2)}, u32[]{:S(2)}) collective-permute-start(bf16[16,2560]{1,0:T(8,128)(2,1)S(1)} %get-tuple-element.84), channel_id=1, source_target_pairs={{0,4},{1,5},{2,6},{3,7},{4,0},{5,1},{6,2},{7,3},{8,12},{9,13},{10,... | collective-permute-start | bytes 245768 | tf_op jit(solution)/shard_map/ppermute | solution.py:514
  162.8 1.7 collective-permute-start.18
  164.4 4.4 %spread.1 = bf16[1024,512]{1,0:T(8,128)(2,1)} custom-call(bf16[1024,512]{1,0:T(8,128)(2,1)} %get-tuple-element.51.d_ref, bf16[2,16,512]{2,1,0:T(8,128)(2,1)} %copy-done.8, bf16[2,16,512]{2,1,0:T(8,128)(2,1)} %copy-done.7, bf16[2,34,512]{2,1,0:T(8,128)(2,1)} %copy-done.13, bf16[2,34,512]{2,1,0:T(8,128)(2,1)} %copy-done.14, bf16[3,3,512]{2,1,0:T(4,128)(2,1)} %dw_ref.3), custom_call_target="tpu_custom_call" | custom-call | flops 5000000000 | bytes 2311168 | tf_op jit(solution)/shard_map/spread/pallas_call | solution.py:476
  168.9 0.2 collective-permute-done.18
  169.1 0.7 fusion
  169.8 0.6 fusion.1
  170.4 0.6 slice.160
  171.0 0.6 reshape.53
  (48 shorter events, 0.3 us)
Async XLA Ops:
  3.7 34.9 %all-to-all-start.1 = ((bf16[32,32,512]{2,1,0:T(8,128)(2,1)}), bf16[32,32,512]{2,1,0:T(8,128)(2,1)S(1)}, u32[]{:S(2)}, u32[]{:S(2)}) async-start(bf16[32,32,512]{2,1,0:T(8,128)(2,1)} %bitcast.36), calls=%async_computation.1 | async-start | bytes 2097152 | tf_op jit(solution)/shard_map/all_to_all | solution.py:542
  11.8 7.3 %collective-permute-start.1 = (bf16[2,16,512]{2,1,0:T(8,128)(2,1)S(1)}, bf16[2,16,512]{2,1,0:T(8,128)(2,1)S(1)}, u32[]{:S(2)}, u32[]{:S(2)}) collective-permute-start(bf16[2,16,512]{2,1,0:T(8,128)(2,1)S(1)} %get-tuple-element.68), channel_id=1, source_target_pairs={{8,0},{16,8},{24,16},{9,1},{17,9},{25,17},{10,2},{18,10},{26,18},{... | collective-permute-start | bytes 98312 | tf_op jit(solution)/shard_map/ppermute | solution.py:498
  13.1 6.4 %collective-permute-start = (bf16[2,16,512]{2,1,0:T(8,128)(2,1)S(1)}, bf16[2,16,512]{2,1,0:T(8,128)(2,1)S(1)}, u32[]{:S(2)}, u32[]{:S(2)}) collective-permute-start(bf16[2,16,512]{2,1,0:T(8,128)(2,1)S(1)} %get-tuple-element.69), channel_id=1, source_target_pairs={{0,8},{8,16},{16,24},{1,9},{9,17},{17,25},{2,10},{10,18},{18,26},{... | collective-permute-start | bytes 98312 | tf_op jit(solution)/shard_map/ppermute | solution.py:498
  19.1 6.8 %copy-start.9 = (bf16[2,16,512]{2,1,0:T(8,128)(2,1)}, bf16[2,16,512]{2,1,0:T(8,128)(2,1)S(1)}, u32[]{:S(2)}) copy-start(bf16[2,16,512]{2,1,0:T(8,128)(2,1)S(1)} %collective-permute-done.1.bot_ref) | copy-start | bytes 98308
  19.4 6.4 %copy-start.10 = (bf16[2,16,512]{2,1,0:T(8,128)(2,1)}, bf16[2,16,512]{2,1,0:T(8,128)(2,1)S(1)}, u32[]{:S(2)}) copy-start(bf16[2,16,512]{2,1,0:T(8,128)(2,1)S(1)} %collective-permute-done.top_ref) | copy-start | bytes 98308
  19.5 3.0 %collective-permute-start.2 = (bf16[2,34,512]{2,1,0:T(8,128)(2,1)S(1)}, bf16[2,34,512]{2,1,0:T(8,128)(2,1)S(1)}, u32[]{:S(2)}, u32[]{:S(2)}) collective-permute-start(bf16[2,34,512]{2,1,0:T(8,128)(2,1)S(1)} %pad_maximum_fusion.3), channel_id=1, source_target_pairs={{0,1},{1,2},{2,3},{3,4},{4,5},{5,6},{6,7},{8,9},{9,10},{10,11},{11... | collective-permute-start | bytes 208904 | tf_op jit(solution)/shard_map/ppermute | solution.py:498
  21.2 4.7 %collective-permute-start.3 = (bf16[2,34,512]{2,1,0:T(8,128)(2,1)S(1)}, bf16[2,34,512]{2,1,0:T(8,128)(2,1)S(1)}, u32[]{:S(2)}, u32[]{:S(2)}) collective-permute-start(bf16[2,34,512]{2,1,0:T(8,128)(2,1)S(1)} %pad_maximum_fusion.4), channel_id=1, source_target_pairs={{1,0},{2,1},{3,2},{4,3},{5,4},{6,5},{7,6},{9,8},{10,9},{11,10},{12... | collective-permute-start | bytes 208904 | tf_op jit(solution)/shard_map/ppermute | solution.py:498
  22.5 3.4 %copy-start.11 = (bf16[2,34,512]{2,1,0:T(8,128)(2,1)}, bf16[2,34,512]{2,1,0:T(8,128)(2,1)S(1)}, u32[]{:S(2)}) copy-start(bf16[2,34,512]{2,1,0:T(8,128)(2,1)S(1)} %collective-permute-done.2.left_ref.refs_8_) | copy-start | bytes 208900
  25.9 0.6 copy-start.12
  38.6 10.1 %copy-start.1 = (bf16[32,32,512]{2,1,0:T(8,128)(2,1)}, bf16[32,32,512]{2,1,0:T(8,128)(2,1)S(1)}, u32[]{:S(2)}) copy-start(bf16[32,32,512]{2,1,0:T(8,128)(2,1)S(1)} %all-to-all-done.1) | copy-start | bytes 3145732
  38.6 37.6 %all-to-all-start = ((bf16[32,32,512]{2,1,0:T(8,128)(2,1)}), bf16[32,32,512]{2,1,0:T(8,128)(2,1)S(1)}, u32[]{:S(2)}, u32[]{:S(2)}) async-start(bf16[32,32,512]{2,1,0:T(8,128)(2,1)} %bitcast.35), calls=%async_computation | async-start | bytes 2097152 | tf_op jit(solution)/shard_map/all_to_all | solution.py:542
  76.2 1.0 copy-start.2
  85.4 24.3 %all-to-all-start.2 = ((bf16[32,8,512]{2,1,0:T(8,128)(2,1)}), bf16[32,8,512]{2,1,0:T(8,128)(2,1)S(1)}, u32[]{:S(2)}, u32[]{:S(2)}) async-start(bf16[32,8,512]{2,1,0:T(8,128)(2,1)} %bitcast.41), calls=%async_computation.2 | async-start | bytes 524288 | tf_op jit(solution)/shard_map/all_to_all | solution.py:542
  109.5 20.8 %collective-permute-start.8 = (bf16[256,2048]{1,0:T(8,128)(2,1)}, bf16[256,2048]{1,0:T(8,128)(2,1)S(1)}, u32[]{:S(2)}, u32[]{:S(2)}) collective-permute-start(bf16[256,2048]{1,0:T(8,128)(2,1)} %get-tuple-element.57), channel_id=1, source_target_pairs={{0,1},{1,0},{2,3},{3,2},{4,5},{5,4},{6,7},{7,6},{8,9},{9,8},{10,11... | collective-permute-start | bytes 3145736 | tf_op jit(solution)/shard_map/ppermute | solution.py:514
  109.7 0.7 copy-start.3
  113.5 8.6 %copy-start.15 = (bf16[32,512]{1,0:T(8,128)(2,1)S(1)}, bf16[32,512]{1,0:T(8,128)(2,1)}, u32[]{:S(2)}) copy-start(bf16[32,512]{1,0:T(8,128)(2,1)} %get-tuple-element.43) | copy-start | bytes 98308
  113.5 13.8 %copy-start.5 = (bf16[64,512]{1,0:T(8,128)(2,1)S(1)}, bf16[64,512]{1,0:T(8,128)(2,1)}, u32[]{:S(2)}) copy-start(bf16[64,512]{1,0:T(8,128)(2,1)} %get-tuple-element.45) | copy-start | bytes 196612
  113.5 15.4 %copy-start.4 = (bf16[64,512]{1,0:T(8,128)(2,1)S(1)}, bf16[64,512]{1,0:T(8,128)(2,1)}, u32[]{:S(2)}) copy-start(bf16[64,512]{1,0:T(8,128)(2,1)} %get-tuple-element.46) | copy-start | bytes 196612
  113.5 16.8 %copy-start = (bf16[256,2048]{1,0:T(8,128)(2,1)S(1)}, bf16[256,2048]{1,0:T(8,128)(2,1)}, u32[]{:S(2)}) copy-start(bf16[256,2048]{1,0:T(8,128)(2,1)} %get-tuple-element.56) | copy-start | bytes 3145732
  113.5 12.2 %collective-permute-start.5 = (bf16[2,16,512]{2,1,0:T(8,128)(2,1)}, bf16[2,16,512]{2,1,0:T(8,128)(2,1)S(1)}, u32[]{:S(2)}, u32[]{:S(2)}) collective-permute-start(bf16[2,16,512]{2,1,0:T(8,128)(2,1)} %bitcast.50), channel_id=1, source_target_pairs={{8,0},{16,8},{24,16},{9,1},{17,9},{25,17},{10,2},{18,10},{26,18},{... | collective-permute-start | bytes 98312 | tf_op jit(solution)/shard_map/ppermute | solution.py:498
  114.9 29.2 %all-to-all-start.3 = ((bf16[32,24,512]{2,1,0:T(8,128)(2,1)}), bf16[32,24,512]{2,1,0:T(8,128)(2,1)}, u32[]{:S(2)}, u32[]{:S(2)}) async-start(bf16[32,24,512]{2,1,0:T(8,128)(2,1)} %bitcast.13), calls=%async_computation.3 | async-start | bytes 1572864 | tf_op jit(solution)/shard_map/all_to_all | solution.py:542
  122.1 5.2 %collective-permute-start.4 = (bf16[2,16,512]{2,1,0:T(8,128)(2,1)S(1)}, bf16[2,16,512]{2,1,0:T(8,128)(2,1)S(1)}, u32[]{:S(2)}, u32[]{:S(2)}) collective-permute-start(bf16[2,16,512]{2,1,0:T(8,128)(2,1)S(1)} %bitcast.49), channel_id=1, source_target_pairs={{0,8},{8,16},{16,24},{1,9},{9,17},{17,25},{2,10},{10,18},{18,26},{... | collective-permute-start | bytes 98312 | tf_op jit(solution)/shard_map/ppermute | solution.py:498
  125.8 5.0 %copy-start.7 = (bf16[2,16,512]{2,1,0:T(8,128)(2,1)}, bf16[2,16,512]{2,1,0:T(8,128)(2,1)S(1)}, u32[]{:S(2)}) copy-start(bf16[2,16,512]{2,1,0:T(8,128)(2,1)S(1)} %collective-permute-done.5.bot_ref) | copy-start | bytes 98308
  127.3 3.4 %copy-start.8 = (bf16[2,16,512]{2,1,0:T(8,128)(2,1)}, bf16[2,16,512]{2,1,0:T(8,128)(2,1)S(1)}, u32[]{:S(2)}) copy-start(bf16[2,16,512]{2,1,0:T(8,128)(2,1)S(1)} %collective-permute-done.4.top_ref) | copy-start | bytes 98308
  127.4 8.5 %collective-permute-start.6 = (bf16[2,34,512]{2,1,0:T(8,128)(2,1)S(1)}, bf16[2,34,512]{2,1,0:T(8,128)(2,1)S(1)}, u32[]{:S(2)}, u32[]{:S(2)}) collective-permute-start(bf16[2,34,512]{2,1,0:T(8,128)(2,1)S(1)} %pad_maximum_fusion.5), channel_id=1, source_target_pairs={{0,1},{1,2},{2,3},{3,4},{4,5},{5,6},{6,7},{8,9},{9,10},{10,11},{11... | collective-permute-start | bytes 208904 | tf_op jit(solution)/shard_map/ppermute | solution.py:498
  129.0 6.9 %collective-permute-start.7 = (bf16[2,34,512]{2,1,0:T(8,128)(2,1)S(1)}, bf16[2,34,512]{2,1,0:T(8,128)(2,1)S(1)}, u32[]{:S(2)}, u32[]{:S(2)}) collective-permute-start(bf16[2,34,512]{2,1,0:T(8,128)(2,1)S(1)} %pad_maximum_fusion.6), channel_id=1, source_target_pairs={{1,0},{2,1},{3,2},{4,3},{5,4},{6,5},{7,6},{9,8},{10,9},{11,10},{12... | collective-permute-start | bytes 208904 | tf_op jit(solution)/shard_map/ppermute | solution.py:498
  130.8 21.6 %collective-permute-start.9 = (bf16[64,2048]{1,0:T(8,128)(2,1)S(1)}, bf16[64,2048]{1,0:T(8,128)(2,1)S(1)}, u32[]{:S(2)}, u32[]{:S(2)}) collective-permute-start(bf16[64,2048]{1,0:T(8,128)(2,1)S(1)} %get-tuple-element.63), channel_id=1, source_target_pairs={{0,8},{8,0},{16,24},{24,16},{1,9},{9,1},{17,25},{25,17},{2,10},{10... | collective-permute-start | bytes 786440 | tf_op jit(solution)/shard_map/ppermute | solution.py:514
  133.5 18.9 %collective-permute-start.11 = (bf16[64,2048]{1,0:T(8,128)(2,1)S(1)}, bf16[64,2048]{1,0:T(8,128)(2,1)S(1)}, u32[]{:S(2)}, u32[]{:S(2)}) collective-permute-start(bf16[64,2048]{1,0:T(8,128)(2,1)S(1)} %get-tuple-element.64), channel_id=1, source_target_pairs={{0,24},{8,16},{16,8},{24,0},{1,25},{9,17},{17,9},{25,1},{2,26},{10... | collective-permute-start | bytes 786440 | tf_op jit(solution)/shard_map/ppermute | solution.py:514
  135.9 16.5 %collective-permute-start.10 = (bf16[64,2048]{1,0:T(8,128)(2,1)S(1)}, bf16[64,2048]{1,0:T(8,128)(2,1)S(1)}, u32[]{:S(2)}, u32[]{:S(2)}) collective-permute-start(bf16[64,2048]{1,0:T(8,128)(2,1)S(1)} %get-tuple-element.65), channel_id=1, source_target_pairs={{0,16},{8,24},{16,0},{24,8},{1,17},{9,25},{17,1},{25,9},{2,18},{10... | collective-permute-start | bytes 786440 | tf_op jit(solution)/shard_map/ppermute | solution.py:514
  135.9 16.4 %copy-start.13 = (bf16[2,34,512]{2,1,0:T(8,128)(2,1)}, bf16[2,34,512]{2,1,0:T(8,128)(2,1)S(1)}, u32[]{:S(2)}) copy-start(bf16[2,34,512]{2,1,0:T(8,128)(2,1)S(1)} %collective-permute-done.6.left_ref) | copy-start | bytes 208900
  135.9 16.4 %copy-start.14 = (bf16[2,34,512]{2,1,0:T(8,128)(2,1)}, bf16[2,34,512]{2,1,0:T(8,128)(2,1)S(1)}, u32[]{:S(2)}) copy-start(bf16[2,34,512]{2,1,0:T(8,128)(2,1)S(1)} %collective-permute-done.7.right_ref) | copy-start | bytes 208900
  152.3 1.5 copy-start.6
  152.3 1.5 collective-permute-start.12
  153.8 5.2 %collective-permute-start.15 = (f32[16,512]{1,0:T(8,128)S(1)}, f32[16,512]{1,0:T(8,128)S(1)}, u32[]{:S(2)}, u32[]{:S(2)}) collective-permute-start(f32[16,512]{1,0:T(8,128)S(1)} %add.69), channel_id=1, source_target_pairs={{0,24},{8,16},{16,8},{24,0},{1,25},{9,17},{17,9},{25,1},{2,26},{10... | collective-permute-start | bytes 98312 | tf_op jit(solution)/shard_map/ppermute | solution.py:514
  154.6 4.5 %collective-permute-start.14 = (f32[16,512]{1,0:T(8,128)S(1)}, f32[16,512]{1,0:T(8,128)S(1)}, u32[]{:S(2)}, u32[]{:S(2)}) collective-permute-start(f32[16,512]{1,0:T(8,128)S(1)} %add.69), channel_id=1, source_target_pairs={{0,16},{8,24},{16,0},{24,8},{1,17},{9,25},{17,1},{25,9},{2,18},{10... | collective-permute-start | bytes 98312 | tf_op jit(solution)/shard_map/ppermute | solution.py:514
  156.0 3.9 %collective-permute-start.13 = (f32[16,512]{1,0:T(8,128)S(1)}, f32[16,512]{1,0:T(8,128)S(1)}, u32[]{:S(2)}, u32[]{:S(2)}) collective-permute-start(f32[16,512]{1,0:T(8,128)S(1)} %add.69), channel_id=1, source_target_pairs={{0,8},{8,0},{16,24},{24,16},{1,9},{9,1},{17,25},{25,17},{2,10},{10... | collective-permute-start | bytes 98312 | tf_op jit(solution)/shard_map/ppermute | solution.py:514
  160.0 8.9 %collective-permute-start.16 = (bf16[16,2560]{1,0:T(8,128)(2,1)S(1)}, bf16[16,2560]{1,0:T(8,128)(2,1)S(1)}, u32[]{:S(2)}, u32[]{:S(2)}) collective-permute-start(bf16[16,2560]{1,0:T(8,128)(2,1)S(1)} %get-tuple-element.83), channel_id=1, source_target_pairs={{0,2},{1,3},{2,0},{3,1},{4,6},{5,7},{6,4},{7,5},{8,10},{9,11},{10,... | collective-permute-start | bytes 245768 | tf_op jit(solution)/shard_map/ppermute | solution.py:514
  160.6 8.3 %collective-permute-start.17 = (bf16[16,2560]{1,0:T(8,128)(2,1)S(1)}, bf16[16,2560]{1,0:T(8,128)(2,1)S(1)}, u32[]{:S(2)}, u32[]{:S(2)}) collective-permute-start(bf16[16,2560]{1,0:T(8,128)(2,1)S(1)} %get-tuple-element.84), channel_id=1, source_target_pairs={{0,4},{1,5},{2,6},{3,7},{4,0},{5,1},{6,2},{7,3},{8,12},{9,13},{10,... | collective-permute-start | bytes 245768 | tf_op jit(solution)/shard_map/ppermute | solution.py:514
  162.8 6.3 %collective-permute-start.18 = (bf16[16,2560]{1,0:T(8,128)(2,1)S(1)}, bf16[16,2560]{1,0:T(8,128)(2,1)S(1)}, u32[]{:S(2)}, u32[]{:S(2)}) collective-permute-start(bf16[16,2560]{1,0:T(8,128)(2,1)S(1)} %get-tuple-element.85), channel_id=1, source_target_pairs={{0,6},{1,7},{2,4},{3,5},{4,2},{5,3},{6,0},{7,1},{8,14},{9,15},{10,... | collective-permute-start | bytes 245768 | tf_op jit(solution)/shard_map/ppermute | solution.py:514

commit v3 on v2

--- a/solution.py
+++ b/solution.py
@@ -43,13 +43,39 @@
         reps = reps_r * reps_s
         share = devices // batches
         spots = [(a, e) for a in range(high) for e in range(wide)]
-        edge = [c for c in spots if c[0] in (0, high - 1) or c[1] in (0, wide - 1)]
-        rest = [c for c in spots if c not in set(edge)]
-        place = {c: (n % share, n // share) for n, c in enumerate(edge + rest)}
+        cells = tile_rows * tile_cols
+        ring = [
+            [(-1, w) for w in range(tile_cols)],
+            [(tile_rows, w) for w in range(tile_cols)],
+            [(h, -1) for h in range(-1, tile_rows + 1)],
+            [(h, tile_cols) for h in range(-1, tile_rows + 1)],
+        ]
+
+        def home(h, w):
+            down, right = h // tile_rows, w // tile_cols
+            h, w = h % tile_rows, w % tile_cols
+            return down, right, (h % high, w % wide), (h // high) * reps_s + w // wide
+
+        wanted = {c: [] for c in spots}
+        for piece, members in enumerate(ring):
+            for n, cell in enumerate(members):
+                wanted[home(*cell)[2]].append((piece, n))
+        edge = sorted((c for c in spots if wanted[c]), key=lambda c: -len(wanted[c]))
         slots = len(spots) // share
         edge_slots = -(-len(edge) // share)
-        bounds = [0, edge_slots, slots] if edge_slots < slots else [0, slots]
-        cells = tile_rows * tile_cols
+        assert edge_slots < slots
+        bounds = [0, edge_slots, slots]
+        place, filled, load = {}, [0] * share, [0] * share
+        for c in edge:
+            owner = min((n for n in range(share) if filled[n] < edge_slots), key=lambda n: load[n])
+            place[c] = (owner, filled[owner])
+            filled[owner] += 1
+            load[owner] += len(wanted[c])
+        for c in spots:
+            if c not in place:
+                owner = min(range(share), key=lambda n: filled[n])
+                place[c] = (owner, filled[owner])
+                filled[owner] += 1
 
         def build(first, last):
             size = (last - first) * reps
@@ -62,6 +88,7 @@
                         send[owner * size + (slot - first) * reps + rep, h * tile_cols + w] = 1
             count = (last - first) * groups
             seen = np.zeros((count,), np.int64)
+            where = {}
             sort = np.zeros((devices * size, devices * size), np.float32)
             for source in range(devices):
                 j = source % col_count
@@ -73,29 +100,49 @@
                             seen[window] += 1
                             chunk, lane = divmod(position, GROUP)
                             row = chunk * GROUP * count + window * GROUP + lane
+                            where[source, slot, r * reps_s + s] = window * CELLS + position
                             sort[row, source * size + slot * reps + r * reps_s + s] = 1
             step = GROUP * count
             block = sort[:step, :step]
             assert (sort == np.kron(np.eye(CELLS // GROUP), block)).all()
-            return send, block
-
-        self.send_all, sort_all = build(0, slots)
+            return send, block, where
+
+        self.send_all, sort_all, _ = build(0, slots)
         self.send, self.sort, self.take = [], [], []
         for first, last in zip(bounds[:-1], bounds[1:]):
-            send, block = build(first, last)
+            send, block, where = build(first, last)
+            if first == 0:
+                around = where
             self.send.append(send)
             self.sort.append(block)
             self.take.append(sort_all[first * groups * GROUP : last * groups * GROUP])
+        own = edge_slots * reps
+        size = own + -(-max(load) // 8) * 8
+        size = -(-size // 8) * 8
+        back = np.zeros((share * size, cells), np.float32)
+        for n in range(share):
+            back[n * size : n * size + own] = self.send[0][n * own : (n + 1) * own]
+        self.send[0] = back
+        self.pieces = [np.zeros((len(members), share * size), np.float32) for members in ring]
+        self.index = np.full((share, 1, devices * size), -1, np.int32)
+        used = [own] * share
+        for source, slot, rep in around:
+            self.index[:, 0, source * size + slot * reps + rep] = around[source, slot, rep]
+        for c in edge:
+            owner, slot = place[c]
+            for piece, n in wanted[c]:
+                down, right, _, rep = home(*ring[piece][n])
+                self.pieces[piece][n, owner * size + used[owner]] = 1
+                for i in range(row_count):
+                    for j in range(col_count):
+                        if 0 <= i + down < row_count and 0 <= j + right < col_count:
+                            source = (i + down) * col_count + j + right
+                            target = (i * col_count + j) * size + used[owner]
+                            self.index[owner, 0, target] = around[source, slot, rep]
+                used[owner] += 1
+        self.share = share
+        self.windows = [m.shape[0] // GROUP for m in self.sort]
         self.rows = [batches * m.shape[0] for m in self.send]
-        spots = []
-        for h in (0, tile_rows - 1):
-            spots += [(b, h, w) for b in range(batches) for w in range(tile_cols)]
-        for w in (0, tile_cols - 1):
-            spots += [(b, h, w) for b in range(batches) for h in range(tile_rows)]
-        self.pick = np.zeros((len(spots), batches * cells), np.float32)
-        for n, (b, h, w) in enumerate(spots):
-            self.pick[n, b * cells + h * tile_cols + w] = 1
-        self.pick_sent = self.pick @ np.kron(np.eye(batches), self.send[0]).T
 
 
 def send_kernel(batches, x_ref, order, out):
@@ -198,7 +245,7 @@
             datt[at, :] = dot(gw[at, :], wout_ref[...], ((1,), (1,))).astype(BF16)
 
 
-def window_kernel(counts, before, n_hbm, datt_hbm, take_ref, sort_ref, wqkv_hbm, *refs):
+def window_kernel(counts, before, n_hbm, datt_hbm, take_ref, back_ref, wqkv_hbm, *refs):
     n_ref, wqkv_ref, nw, packed, datt, att, dpacked, head_mask, half_mask, in_sems = refs[-10:]
     if counts is None:
         dn_ref, *results, out_sems = refs[:5]
@@ -209,7 +256,7 @@
         ]
         late = moves([(gw_hbm, gw), *zip(old, old_refs)], old_sems)
     loads = moves([(n_hbm, n_ref), (wqkv_hbm, wqkv_ref), (datt_hbm, datt)], in_sems)
-    rows, feats = dn_ref.shape
+    rows, feats = nw.shape
     count = rows // CELLS
     part = GROUP * count
     tiles = feats // 256
@@ -296,17 +343,23 @@
         return carry
 
     lax.fori_loop(0, rows // block, back, 0)
-    for p in range(CELLS // GROUP):
-        ordered = jnp.concatenate(
-            [
-                datt[w * CELLS + p * GROUP : w * CELLS + (p + 1) * GROUP, :]
-                for w in range(count)
-            ],
-            axis=0,
-        )
-        dn_ref[p * part : (p + 1) * part, :] = dot(
-            sort_ref[...], ordered, ((0,), (0,))
-        ).astype(BF16)
+    if back_ref.shape[0] == 1:
+        order = (
+            lax.broadcasted_iota(jnp.int32, (rows, dn_ref.shape[0]), 0) == back_ref[...]
+        ).astype(F32).astype(BF16)
+        dn_ref[...] = dot(order, datt[...], ((0,), (0,))).astype(BF16)
+    else:
+        for p in range(CELLS // GROUP):
+            ordered = jnp.concatenate(
+                [
+                    datt[w * CELLS + p * GROUP : w * CELLS + (p + 1) * GROUP, :]
+                    for w in range(count)
+                ],
+                axis=0,
+            )
+            dn_ref[p * part : (p + 1) * part, :] = dot(
+                back_ref[...], ordered, ((0,), (0,))
+            ).astype(BF16)
     for copy in stores:
         copy.wait()
 
@@ -365,17 +418,17 @@
     ).astype(BF16)
 
 
-def border_kernel(dn_ref, mixed_ref, grad_ref, pick_sent_ref, pick_ref, gain_ref, *outs):
-    d_normed = dot(pick_sent_ref[...], dn_ref[...])
-    mixed = dot(pick_ref[...], mixed_ref[...])
-    grad = dot(pick_ref[...], grad_ref[...])
-    centred = mixed - jnp.mean(mixed, axis=-1, keepdims=True)
-    rstd = lax.rsqrt(jnp.mean(centred * centred, axis=-1, keepdims=True) + 1e-05)
-    d_mixed = norm_back(d_normed, centred * rstd, rstd, grad, gain_ref[...])
-    start = 0
-    for out in outs:
-        out[...] = d_mixed[start : start + out.shape[0]]
-        start += out.shape[0]
+def border_kernel(dn_ref, gain_ref, *refs):
+    batches = refs[4].shape[0]
+    feats = dn_ref.shape[1]
+    size = dn_ref.shape[0] // batches
+    for pick, pair, out in zip(refs[:4], refs[4:8], refs[8:]):
+        for b in range(batches):
+            d_normed = dot(pick[...], dn_ref[b * size : (b + 1) * size, :])
+            mixed = pair[b, :, :feats].astype(F32)
+            centred = mixed - jnp.mean(mixed, axis=-1, keepdims=True)
+            rstd = lax.rsqrt(jnp.mean(centred * centred, axis=-1, keepdims=True) + 1e-05)
+            out[b] = norm_back(d_normed, centred * rstd, rstd, pair[b, :, feats:], gain_ref[...])
 
 
 def sums_kernel(count, *refs):
@@ -535,8 +588,11 @@
     parts = len(plan.rows)
     gain = ln_gain.reshape(1, feats)
     send = jnp.asarray(plan.send_all, BF16)
+    owner = lax.axis_index("row") * col_count + lax.axis_index("col")
+    index = lax.dynamic_index_in_dim(jnp.asarray(plan.index), owner % plan.share, keepdims=False)
     back = [jnp.asarray(np.ascontiguousarray(m.T), BF16) for m in plan.send]
-    sort = [jnp.asarray(m, BF16) for m in plan.sort]
+    sort = [index, *(jnp.asarray(m, BF16) for m in plan.sort[1:])]
+    grouped = [shape((n * CELLS, feats), BF16) for n in plan.windows]
     take = [jnp.asarray(m, BF16) for m in plan.take]
     chunks = [shape((n, feats), BF16) for n in plan.rows]
     trade = lambda x: lax.all_to_all(x, AXES, split_axis=0, concat_axis=0, tiled=True)
@@ -570,11 +626,19 @@
         hbm_outs=(1, 2, 3),
     )
     normed_win = trade(normed)
+    pair = lambda pick: jnp.concatenate([pick(mixed.reshape(latent.shape)), pick(grad_out)], axis=-1)
+    pairs = halos(
+        pair(lambda x: x[:, 0]),
+        pair(lambda x: x[:, -1]),
+        pair(lambda x: x[:, :, 0]),
+        pair(lambda x: x[:, :, -1]),
+    )
+    normed_win, *pairs = lax.optimization_barrier((normed_win, *pairs))
 
     chips = col_count // 2
     ahead = call(
         functools.partial(grads_kernel, parts),
-        [chunks[n // 2] for n in range(2 * parts)],
+        [grouped[n // 2] for n in range(2 * parts)],
         [],
         [grad_win, w_out, *take],
         4,
@@ -584,7 +648,7 @@
     half = shape((feats // 2, 4 * feats), BF16)
     d_parts, kept = [], []
     for n in range(parts):
-        count = plan.rows[n]
+        count = plan.windows[n] * CELLS
         last = n == parts - 1
         mat = lambda width: pltpu.VMEM((count, width), BF16)
         args = [normed_win, ahead[2 * n + 1], take[n], sort[n], w_qkv]
@@ -601,7 +665,7 @@
                 *(pltpu.VMEM(x.shape, BF16) for x in kept),
             ]
         else:
-            outs = [chunks[n], chunks[n], chunks[n], shape((count, 3 * feats), BF16)]
+            outs = [chunks[n], grouped[n], grouped[n], shape((count, 3 * feats), BF16)]
             scratch = [pltpu.SemaphoreType.DMA((3,))]
         d_chunk, *saved = call(
             functools.partial(window_kernel, (row_count, chips) if last else None, n),
@@ -620,7 +684,7 @@
                 pltpu.SemaphoreType.DMA((3,)),
             ],
             args,
-            2 + 20 * count // sum(plan.rows),
+            2 + 20 * count // cells,
             "windows",
             hbm_ins=(0, 1, 4, *range(6, len(args))),
             hbm_outs=tuple(range(1, len(outs))),
@@ -630,27 +694,15 @@
         d_parts.append(trade(d_chunk))
     keep, give = saved
 
-    tops, sides = batches * cols, batches * rows
-    borders = call(
+    d_halos = call(
         border_kernel,
-        [shape((n, feats), BF16) for n in (tops, tops, sides, sides)],
+        [shape((*x.shape[:2], feats), BF16) for x in pairs],
         [],
-        [
-            d_parts[0],
-            mixed,
-            grad_flat,
-            jnp.asarray(plan.pick_sent, BF16),
-            jnp.asarray(plan.pick, BF16),
-            gain,
-        ],
+        [d_parts[0], gain, *(jnp.asarray(m, BF16) for m in plan.pieces), *pairs],
         3,
         "border",
     )
-    d_halos = halos(*(x.reshape(batches, -1, feats) for x in borders))
-
     weights = (keep.astype(F32) + swap(give, "col", 1).astype(F32)).astype(BF16)
-    *d_parts, above, below, from_left, from_right = lax.optimization_barrier((*d_parts, *d_halos))
-    d_halos = (above, below, from_left, from_right)
     d_mixed, sums = call(
         functools.partial(sums_kernel, parts),
         [flat, shape((16, feats), F32)],

time: 173 us -> 168 us (0.971)
  waiting for transfers between devices: 46.4 us -> 38.2 us
  local copies, waits for them, and re-layouts: 5.88 us -> 11.8 us
  starting transfers between devices: 57.1 us -> 54.8 us
    all_to_all x4, waiting for transfers between devices: 37.2 us -> 26.5 us  [shards(): lax.all_to_all(x, AXES, split_axis=0, concat_axis=0, tiled=True)]
    ppermute x8, waiting for transfers between devices: 5.23 us -> 8.14 us  [shifted(): lax.ppermute(cells, axis, [(n, n + step) for n in range(count) if 0 <= n...]
    squeeze x0 -> x3, local copies, waits for them, and re-layouts: none -> 2.83 us  [the longest x2 1.57 us: shards(): x[:, 0]]
    slice x0 -> x2, local copies, waits for them, and re-layouts: none -> 2.82 us  [shards(): x[:, :, 0]]
  transfers between devices with their start and end apart: 23 -> 23, of which waited for: 10 -> 10; matrix products, arithmetic and copies ran while one was open for 2% -> 5% of each run, Pallas kernels for 28% -> 28%
where the time goes in v3:
time: 168 us; the launch traced here: 167 us
  Pallas kernels  59 us (35%)
  starting transfers between devices  54.8 us (33%)
  waiting for transfers between devices  38.2 us (23%)
  local copies, waits for them, and re-layouts  11.8 us (7%)
  other arithmetic  2.1 us (1%)
    pallas_call x8, Pallas kernels, call(): pl.pallas_call(body, out_shape=outs, in_specs=[smem if n in scalars else...  59 us
    all_to_all x4, waiting for transfers between devices, shards(): lax.all_to_all(x, AXES, split_axis=0, concat_axis=0, tiled=True)  26.5 us
    all_to_all x4, starting transfers between devices, shards(): lax.all_to_all(x, AXES, split_axis=0, concat_axis=0, tiled=True)  26.3 us
    ppermute x8, starting transfers between devices, shifted(): lax.ppermute(cells, axis, [(n, n + step) for n in range(count) if 0 <= n...  16.5 us
    ppermute x11, starting transfers between devices, swap(): lax.ppermute(x, axis, [(n, n ^ step) for n in range(lax.axis_size(axis))])  12 us
    ppermute x8, waiting for transfers between devices, shifted(): lax.ppermute(cells, axis, [(n, n + step) for n in range(count) if 0 <= n...  8.14 us
    ppermute x11, waiting for transfers between devices, swap(): lax.ppermute(x, axis, [(n, n ^ step) for n in range(lax.axis_size(axis))])  3.55 us
  transfers between devices with their start and end apart: 23, of which 10 were waited for; matrix products, arithmetic and copies ran while one was open for 5% of the time, Pallas kernels for 28%

profile of v3, /device:TPU:0, one launch (start us, length us, event | category | flops | bytes accessed | tf_op | source)
XLA Modules:
  0.0 167.0 jit_solution(17557617876218989725)
XLA Ops:
  0.6 3.0 %grad_send.1 = bf16[1024,512]{1,0:T(8,128)(2,1)} custom-call(bf16[1024,512]{1,0:T(8,128)(2,1)} %bitcast.76, bf16[512,512]{1,0:T(8,128)(2,1)} %constant.73.clone.order), custom_call_target="tpu_custom_call" | custom-call | flops 3000000000 | bytes 2621440 | tf_op jit(solution)/shard_map/grad_send/pallas_call | solution.py:529
  3.7 7.3 %all-to-all-start.1 = ((bf16[32,32,512]{2,1,0:T(8,128)(2,1)}), bf16[32,32,512]{2,1,0:T(8,128)(2,1)S(1)}, u32[]{:S(2)}, u32[]{:S(2)}) async-start(bf16[32,32,512]{2,1,0:T(8,128)(2,1)} %bitcast.63), calls=%async_computation.1 | async-start | bytes 2097152 | tf_op jit(solution)/shard_map/all_to_all | solution.py:598
  11.0 0.8 slice_bitcast_fusion.4
  11.8 1.3 collective-permute-start.1
  13.1 4.5 %collective-permute-start = (bf16[2,16,512]{2,1,0:T(8,128)(2,1)S(1)}, bf16[2,16,512]{2,1,0:T(8,128)(2,1)S(1)}, u32[]{:S(2)}, u32[]{:S(2)}) collective-permute-start(bf16[2,16,512]{2,1,0:T(8,128)(2,1)S(1)} %get-tuple-element.75), channel_id=1, source_target_pairs={{0,8},{8,16},{16,24},{1,9},{9,17},{17,25},{2,10},{10,18},{18,26},{... | collective-permute-start | bytes 98312 | tf_op jit(solution)/shard_map/ppermute | solution.py:551
  17.6 1.4 fusion.8
  19.1 0.3 collective-permute-done.top_ref
  19.5 1.6 collective-permute-start.2
  21.2 1.3 collective-permute-start.3
  22.5 1.4 fusion.7
  23.9 0.0 collective-permute-done.2.left_ref.refs_8_
  23.9 0.0 copy-start.12
  23.9 1.9 %collective-permute-done.3.right_ref.refs_9_ = bf16[2,34,512]{2,1,0:T(8,128)(2,1)S(1)} collective-permute-done((bf16[2,34,512]{2,1,0:T(8,128)(2,1)S(1)}, bf16[2,34,512]{2,1,0:T(8,128)(2,1)S(1)}, u32[]{:S(2)}, u32[]{:S(2)}) %collective-permute-start.3) | collective-permute-done | bytes 69664 | tf_op jit(solution)/shard_map/ppermute | solution.py:551
  25.9 0.6 copy-done.13
  26.5 7.1 %mix.1 = (bf16[1024,512]{1,0:T(8,128)(2,1)}, bf16[1024,512]{1,0:T(8,128)(2,1)}, f32[1024,2]{1,0:T(8,128)}, bf16[2,34,16,512]{3,2,1,0:T(8,128)(2,1)}) custom-call(bf16[2,32,16,512]{3,2,1,0:T(8,128)(2,1)} %lat_ref.1, bf16[2,16,512]{2,1,0:T(8,128)(2,1)} %copy-done.9, bf16[2,16,512]{2,1,0:T(8,128)(2,1)} %copy-done.8, bf16[2,34,512]{2,1,0:T(8,128)(2,1)} %copy-done.12, ...), custom_call_target="tpu_custom_call" | custom-call | flops 6000000000 | bytes 5008384 | tf_op jit(solution)/shard_map/mix/pallas_call | solution.py:529
  33.6 5.0 %all-to-all-done.1 = bf16[32,32,512]{2,1,0:T(8,128)(2,1)S(1)} async-done(((bf16[32,32,512]{2,1,0:T(8,128)(2,1)}), bf16[32,32,512]{2,1,0:T(8,128)(2,1)S(1)}, u32[]{:S(2)}, u32[]{:S(2)}) %all-to-all-start.1) | async-done | bytes 1048608 | tf_op jit(solution)/shard_map/all_to_all | solution.py:598
  38.6 10.1 %all-to-all-start = ((bf16[32,32,512]{2,1,0:T(8,128)(2,1)}), bf16[32,32,512]{2,1,0:T(8,128)(2,1)S(1)}, u32[]{:S(2)}, u32[]{:S(2)}) async-start(bf16[32,32,512]{2,1,0:T(8,128)(2,1)} %bitcast.62), calls=%async_computation | async-start | bytes 2097152 | tf_op jit(solution)/shard_map/all_to_all | solution.py:598
  48.6 1.3 dynamic-slice_bitcast_fusion.back_ref
  50.0 0.8 slice_bitcast_fusion.2
  50.7 0.8 slice_bitcast_fusion
  51.5 3.7 %collective-permute-start.4 = (bf16[2,16,1024]{2,1,0:T(8,128)(2,1)S(1)}, bf16[2,16,1024]{2,1,0:T(8,128)(2,1)S(1)}, u32[]{:S(2)}, u32[]{:S(2)}) collective-permute-start(bf16[2,16,1024]{2,1,0:T(8,128)(2,1)S(1)} %pad_maximum_fusion.7), channel_id=1, source_target_pairs={{0,8},{8,16},{16,24},{1,9},{9,17},{17,25},{2,10},{10,18},{18,26},{... | collective-permute-start | bytes 196616 | tf_op jit(solution)/shard_map/ppermute | solution.py:551
  55.2 1.4 fusion.6
  56.7 1.3 collective-permute-start.5
  58.0 5.0 %collective-permute-done.5.refs_5_ = bf16[2,16,1024]{2,1,0:T(8,128)(2,1)S(1)} collective-permute-done((bf16[2,16,1024]{2,1,0:T(8,128)(2,1)S(1)}, bf16[2,16,1024]{2,1,0:T(8,128)(2,1)S(1)}, u32[]{:S(2)}, u32[]{:S(2)}) %collective-permute-start.5) | collective-permute-done | bytes 65568 | tf_op jit(solution)/shard_map/ppermute | solution.py:551
  63.1 0.1 pad_maximum_fusion
  63.2 1.5 collective-permute-start.6
  64.7 0.1 pad_maximum_fusion.1
  64.7 1.3 collective-permute-start.7
  66.0 3.6 %grads.1 = (bf16[256,512]{1,0:T(8,128)(2,1)}, bf16[256,512]{1,0:T(8,128)(2,1)}, bf16[768,512]{1,0:T(8,128)(2,1)}, bf16[768,512]{1,0:T(8,128)(2,1)}) custom-call(bf16[1024,512]{1,0:T(8,128)(2,1)} %bitcast.59, bf16[512,512]{1,0:T(8,128)(2,1)} %wout_ref.1, bf16[64,256]{1,0:T(8,128)(2,1)} %constant.78.clone.refs_0_.take_ref, ...), custom_call_target="tpu_custom_call" | custom-call | flops 4000000000 | bytes 3801088 | tf_op jit(solution)/shard_map/grads/pallas_call | solution.py:529
  69.6 0.8 collective-permute-done.7.refs_7_
  70.5 5.8 %all-to-all-done = bf16[32,32,512]{2,1,0:T(8,128)(2,1)S(1)} async-done(((bf16[32,32,512]{2,1,0:T(8,128)(2,1)}), bf16[32,32,512]{2,1,0:T(8,128)(2,1)S(1)}, u32[]{:S(2)}, u32[]{:S(2)}) %all-to-all-start) | async-done | bytes 1048608 | tf_op jit(solution)/shard_map/all_to_all | solution.py:598
  76.2 1.0 copy-done.2
  77.2 8.4 %windows.2 = (bf16[512,512]{1,0:T(8,128)(2,1)}, bf16[256,512]{1,0:T(8,128)(2,1)}, bf16[256,512]{1,0:T(8,128)(2,1)}, bf16[256,1536]{1,0:T(8,128)(2,1)}) custom-call(bf16[1024,512]{1,0:T(8,128)(2,1)} %bitcast.60, bf16[256,512]{1,0:T(8,128)(2,1)} %get-tuple-element.34.datt_hbm, bf16[64,256]{1,0:T(8,128)(2,1)} %constant.78.clone.refs_0_.take_ref, ...), custom_call_target="tpu_custom_call" | custom-call | flops 7000000000 | bytes 4753408 | tf_op jit(solution)/shard_map/windows/pallas_call | solution.py:529
  85.6 3.2 %all-to-all-start.2 = ((bf16[32,16,512]{2,1,0:T(8,128)(2,1)}), bf16[32,16,512]{2,1,0:T(8,128)(2,1)S(1)}, u32[]{:S(2)}, u32[]{:S(2)}) async-start(bf16[32,16,512]{2,1,0:T(8,128)(2,1)} %bitcast.68), calls=%async_computation.2 | async-start | bytes 1048576 | tf_op jit(solution)/shard_map/all_to_all | solution.py:598
  88.8 21.7 %windows.3 = (bf16[768,512]{1,0:T(8,128)(2,1)}, bf16[256,2048]{1,0:T(8,128)(2,1)}, bf16[256,2048]{1,0:T(8,128)(2,1)}) custom-call(bf16[1024,512]{1,0:T(8,128)(2,1)} %bitcast.61, bf16[768,512]{1,0:T(8,128)(2,1)} %get-tuple-element.36.datt_hbm, bf16[192,256]{1,0:T(8,128)(2,1)} %constant.79.clone.refs_1_.take_ref, bf16[192,192]{1,0:T(8,128)(2,1)} %constant.77.clone.back_ref, ...), custom_call_target="tpu_custom_call" | custom-call | flops 16999999488 | bytes 8822788 | tf_op jit(solution)/shard_map/windows/pallas_call | solution.py:529
  110.5 0.3 collective-permute-start.8
  110.8 5.7 %all-to-all-start.3 = ((bf16[32,24,512]{2,1,0:T(8,128)(2,1)}), bf16[32,24,512]{2,1,0:T(8,128)(2,1)S(1)}, u32[]{:S(2)}, u32[]{:S(2)}) async-start(bf16[32,24,512]{2,1,0:T(8,128)(2,1)} %bitcast.64), calls=%async_computation.3 | async-start | bytes 1572864 | tf_op jit(solution)/shard_map/all_to_all | solution.py:598
  116.6 2.5 %border.1 = (bf16[2,16,512]{2,1,0:T(8,128)(2,1)}, bf16[2,16,512]{2,1,0:T(8,128)(2,1)}, bf16[2,34,512]{2,1,0:T(8,128)(2,1)}, bf16[2,34,512]{2,1,0:T(8,128)(2,1)}) custom-call(bf16[512,512]{1,0:T(8,128)(2,1)} %bitcast.66, f32[1,512]{1,0:T(1,128)} %bitcast.82, bf16[16,256]{1,0:T(8,128)(2,1)} %constant.80.clone.refs_0_, bf16[16,256]{1,0:T(8,128)(2,1)} %constant.81.clone.refs_1_, ...), custom_call_target="tpu_custom_call" | custom-call | flops 3000000000 | bytes 1191936 | tf_op jit(solution)/shard_map/border/pallas_call | solution.py:529
  119.1 0.0 collective-permute-done.8
  119.1 0.4 add_convert_fusion
  119.5 0.1 fusion.5
  119.6 1.8 %collective-permute-start.9 = (bf16[64,2048]{1,0:T(8,128)(2,1)S(1)}, bf16[64,2048]{1,0:T(8,128)(2,1)S(1)}, u32[]{:S(2)}, u32[]{:S(2)}) collective-permute-start(bf16[64,2048]{1,0:T(8,128)(2,1)S(1)} %get-tuple-element.61), channel_id=1, source_target_pairs={{0,8},{8,0},{16,24},{24,16},{1,9},{9,1},{17,25},{25,17},{2,10},{10... | collective-permute-start | bytes 786440 | tf_op jit(solution)/shard_map/ppermute | solution.py:567
  121.4 1.5 collective-permute-start.11
  122.9 0.3 collective-permute-start.10
  123.1 15.8 %all-to-all-done.3 = bf16[32,24,512]{2,1,0:T(8,128)(2,1)S(1)} async-done(((bf16[32,24,512]{2,1,0:T(8,128)(2,1)}), bf16[32,24,512]{2,1,0:T(8,128)(2,1)S(1)}, u32[]{:S(2)}, u32[]{:S(2)}) %all-to-all-start.3) | async-done | bytes 786464 | tf_op jit(solution)/shard_map/all_to_all | solution.py:598
  138.9 0.9 copy-done.3
  139.8 8.2 %sums.1 = (bf16[1024,512]{1,0:T(8,128)(2,1)}, f32[16,512]{1,0:T(8,128)}) custom-call(bf16[512,512]{1,0:T(8,128)(2,1)} %bitcast.67, bf16[768,512]{1,0:T(8,128)(2,1)} %bitcast.65, bf16[512,256]{1,0:T(8,128)(2,1)} %constant.75.clone.refs_2_, bf16[512,384]{1,0:T(8,128)(2,1)} %constant.76.clone.refs_3_, f32[1024,2]{1,0:T(8,128)} %get-tuple-element.43.refs_4_, ...), custom_call_target="tpu_custom_call" | custom-call | flops 7000000000 | bytes 6408192 | tf_op jit(solution)/shard_map/sums/pallas_call | solution.py:529
  148.1 0.0 copy-start.5
  148.1 0.1 collective-permute-start.12
  148.2 0.1 fusion.3
  148.3 1.2 collective-permute-done.12
  149.6 0.5 collective-permute-start.15
  150.0 1.5 collective-permute-start.14
  151.5 1.6 collective-permute-start.13
  153.1 1.5 collective-permute-done.15
  154.6 0.8 collective-permute-done.13
  155.5 0.1 collective-permute-start.16
  155.6 1.5 collective-permute-start.17
  157.1 2.9 %collective-permute-start.18 = (bf16[16,2560]{1,0:T(8,128)(2,1)S(1)}, bf16[16,2560]{1,0:T(8,128)(2,1)S(1)}, u32[]{:S(2)}, u32[]{:S(2)}) collective-permute-start(bf16[16,2560]{1,0:T(8,128)(2,1)S(1)} %get-tuple-element.91), channel_id=1, source_target_pairs={{0,6},{1,7},{2,4},{3,5},{4,2},{5,3},{6,0},{7,1},{8,14},{9,15},{10,... | collective-permute-start | bytes 245768 | tf_op jit(solution)/shard_map/ppermute | solution.py:567
  159.9 4.4 %spread.1 = bf16[1024,512]{1,0:T(8,128)(2,1)} custom-call(bf16[1024,512]{1,0:T(8,128)(2,1)} %get-tuple-element.45.d_ref, bf16[2,16,512]{2,1,0:T(8,128)(2,1)} %get-tuple-element.50.top_ref, bf16[2,16,512]{2,1,0:T(8,128)(2,1)} %get-tuple-element.51.bot_ref, bf16[2,34,512]{2,1,0:T(8,128)(2,1)} %get-tuple-element.52.left_ref, ...), custom_call_target="tpu_custom_call" | custom-call | flops 5000000000 | bytes 2311168 | tf_op jit(solution)/shard_map/spread/pallas_call | solution.py:529
  164.5 0.7 fusion
  165.1 0.6 fusion.1
  165.8 0.6 slice.196
  166.3 0.6 reshape.44
  (55 shorter events, 0.4 us)
Async XLA Ops:
  3.7 34.9 %all-to-all-start.1 = ((bf16[32,32,512]{2,1,0:T(8,128)(2,1)}), bf16[32,32,512]{2,1,0:T(8,128)(2,1)S(1)}, u32[]{:S(2)}, u32[]{:S(2)}) async-start(bf16[32,32,512]{2,1,0:T(8,128)(2,1)} %bitcast.63), calls=%async_computation.1 | async-start | bytes 2097152 | tf_op jit(solution)/shard_map/all_to_all | solution.py:598
  11.8 7.3 %collective-permute-start.1 = (bf16[2,16,512]{2,1,0:T(8,128)(2,1)S(1)}, bf16[2,16,512]{2,1,0:T(8,128)(2,1)S(1)}, u32[]{:S(2)}, u32[]{:S(2)}) collective-permute-start(bf16[2,16,512]{2,1,0:T(8,128)(2,1)S(1)} %get-tuple-element.74), channel_id=1, source_target_pairs={{8,0},{16,8},{24,16},{9,1},{17,9},{25,17},{10,2},{18,10},{26,18},{... | collective-permute-start | bytes 98312 | tf_op jit(solution)/shard_map/ppermute | solution.py:551
  13.1 6.4 %collective-permute-start = (bf16[2,16,512]{2,1,0:T(8,128)(2,1)S(1)}, bf16[2,16,512]{2,1,0:T(8,128)(2,1)S(1)}, u32[]{:S(2)}, u32[]{:S(2)}) collective-permute-start(bf16[2,16,512]{2,1,0:T(8,128)(2,1)S(1)} %get-tuple-element.75), channel_id=1, source_target_pairs={{0,8},{8,16},{16,24},{1,9},{9,17},{17,25},{2,10},{10,18},{18,26},{... | collective-permute-start | bytes 98312 | tf_op jit(solution)/shard_map/ppermute | solution.py:551
  19.1 6.8 %copy-start.8 = (bf16[2,16,512]{2,1,0:T(8,128)(2,1)}, bf16[2,16,512]{2,1,0:T(8,128)(2,1)S(1)}, u32[]{:S(2)}) copy-start(bf16[2,16,512]{2,1,0:T(8,128)(2,1)S(1)} %collective-permute-done.1.bot_ref) | copy-start | bytes 98308
  19.4 6.4 %copy-start.9 = (bf16[2,16,512]{2,1,0:T(8,128)(2,1)}, bf16[2,16,512]{2,1,0:T(8,128)(2,1)S(1)}, u32[]{:S(2)}) copy-start(bf16[2,16,512]{2,1,0:T(8,128)(2,1)S(1)} %collective-permute-done.top_ref) | copy-start | bytes 98308
  19.5 4.4 %collective-permute-start.2 = (bf16[2,34,512]{2,1,0:T(8,128)(2,1)S(1)}, bf16[2,34,512]{2,1,0:T(8,128)(2,1)S(1)}, u32[]{:S(2)}, u32[]{:S(2)}) collective-permute-start(bf16[2,34,512]{2,1,0:T(8,128)(2,1)S(1)} %pad_maximum_fusion.5), channel_id=1, source_target_pairs={{0,1},{1,2},{2,3},{3,4},{4,5},{5,6},{6,7},{8,9},{9,10},{10,11},{11... | collective-permute-start | bytes 208904 | tf_op jit(solution)/shard_map/ppermute | solution.py:551
  21.2 4.7 %collective-permute-start.3 = (bf16[2,34,512]{2,1,0:T(8,128)(2,1)S(1)}, bf16[2,34,512]{2,1,0:T(8,128)(2,1)S(1)}, u32[]{:S(2)}, u32[]{:S(2)}) collective-permute-start(bf16[2,34,512]{2,1,0:T(8,128)(2,1)S(1)} %pad_maximum_fusion.6), channel_id=1, source_target_pairs={{1,0},{2,1},{3,2},{4,3},{5,4},{6,5},{7,6},{9,8},{10,9},{11,10},{12... | collective-permute-start | bytes 208904 | tf_op jit(solution)/shard_map/ppermute | solution.py:551
  23.9 1.9 %copy-start.12 = (bf16[2,34,512]{2,1,0:T(8,128)(2,1)}, bf16[2,34,512]{2,1,0:T(8,128)(2,1)S(1)}, u32[]{:S(2)}) copy-start(bf16[2,34,512]{2,1,0:T(8,128)(2,1)S(1)} %collective-permute-done.2.left_ref.refs_8_) | copy-start | bytes 208900
  25.8 0.6 copy-start.13
  38.6 18.1 %copy-start.1 = (bf16[32,32,512]{2,1,0:T(8,128)(2,1)}, bf16[32,32,512]{2,1,0:T(8,128)(2,1)S(1)}, u32[]{:S(2)}) copy-start(bf16[32,32,512]{2,1,0:T(8,128)(2,1)S(1)} %all-to-all-done.1) | copy-start | bytes 3145732
  38.6 37.7 %all-to-all-start = ((bf16[32,32,512]{2,1,0:T(8,128)(2,1)}), bf16[32,32,512]{2,1,0:T(8,128)(2,1)S(1)}, u32[]{:S(2)}, u32[]{:S(2)}) async-start(bf16[32,32,512]{2,1,0:T(8,128)(2,1)} %bitcast.62), calls=%async_computation | async-start | bytes 2097152 | tf_op jit(solution)/shard_map/all_to_all | solution.py:598
  51.5 6.5 %collective-permute-start.4 = (bf16[2,16,1024]{2,1,0:T(8,128)(2,1)S(1)}, bf16[2,16,1024]{2,1,0:T(8,128)(2,1)S(1)}, u32[]{:S(2)}, u32[]{:S(2)}) collective-permute-start(bf16[2,16,1024]{2,1,0:T(8,128)(2,1)S(1)} %pad_maximum_fusion.7), channel_id=1, source_target_pairs={{0,8},{8,16},{16,24},{1,9},{9,17},{17,25},{2,10},{10,18},{18,26},{... | collective-permute-start | bytes 196616 | tf_op jit(solution)/shard_map/ppermute | solution.py:551
  56.7 6.4 %collective-permute-start.5 = (bf16[2,16,1024]{2,1,0:T(8,128)(2,1)S(1)}, bf16[2,16,1024]{2,1,0:T(8,128)(2,1)S(1)}, u32[]{:S(2)}, u32[]{:S(2)}) collective-permute-start(bf16[2,16,1024]{2,1,0:T(8,128)(2,1)S(1)} %pad_maximum_fusion.8), channel_id=1, source_target_pairs={{8,0},{16,8},{24,16},{9,1},{17,9},{25,17},{10,2},{18,10},{26,18},{... | collective-permute-start | bytes 196616 | tf_op jit(solution)/shard_map/ppermute | solution.py:551
  58.0 11.6 %copy-start.6 = (bf16[2,16,1024]{2,1,0:T(8,128)(2,1)}, bf16[2,16,1024]{2,1,0:T(8,128)(2,1)S(1)}, u32[]{:S(2)}) copy-start(bf16[2,16,1024]{2,1,0:T(8,128)(2,1)S(1)} %collective-permute-done.4.refs_4_) | copy-start | bytes 196612
  63.1 6.5 %copy-start.7 = (bf16[2,16,1024]{2,1,0:T(8,128)(2,1)}, bf16[2,16,1024]{2,1,0:T(8,128)(2,1)S(1)}, u32[]{:S(2)}) copy-start(bf16[2,16,1024]{2,1,0:T(8,128)(2,1)S(1)} %collective-permute-done.5.refs_5_) | copy-start | bytes 196612
  63.2 6.4 %collective-permute-start.6 = (bf16[2,34,1024]{2,1,0:T(8,128)(2,1)S(1)}, bf16[2,34,1024]{2,1,0:T(8,128)(2,1)S(1)}, u32[]{:S(2)}, u32[]{:S(2)}) collective-permute-start(bf16[2,34,1024]{2,1,0:T(8,128)(2,1)S(1)} %pad_maximum_fusion), channel_id=1, source_target_pairs={{0,1},{1,2},{2,3},{3,4},{4,5},{5,6},{6,7},{8,9},{9,10},{10,11},{11... | collective-permute-start | bytes 417800 | tf_op jit(solution)/shard_map/ppermute | solution.py:551
  64.7 5.7 %collective-permute-start.7 = (bf16[2,34,1024]{2,1,0:T(8,128)(2,1)S(1)}, bf16[2,34,1024]{2,1,0:T(8,128)(2,1)S(1)}, u32[]{:S(2)}, u32[]{:S(2)}) collective-permute-start(bf16[2,34,1024]{2,1,0:T(8,128)(2,1)S(1)} %pad_maximum_fusion.1), channel_id=1, source_target_pairs={{1,0},{2,1},{3,2},{4,3},{5,4},{6,5},{7,6},{9,8},{10,9},{11,10},{12... | collective-permute-start | bytes 417800 | tf_op jit(solution)/shard_map/ppermute | solution.py:551
  69.6 16.0 %copy-start.10 = (bf16[2,34,1024]{2,1,0:T(8,128)(2,1)}, bf16[2,34,1024]{2,1,0:T(8,128)(2,1)S(1)}, u32[]{:S(2)}) copy-start(bf16[2,34,1024]{2,1,0:T(8,128)(2,1)S(1)} %collective-permute-done.6.refs_6_) | copy-start | bytes 417796
  70.5 15.1 %copy-start.11 = (bf16[2,34,1024]{2,1,0:T(8,128)(2,1)}, bf16[2,34,1024]{2,1,0:T(8,128)(2,1)S(1)}, u32[]{:S(2)}) copy-start(bf16[2,34,1024]{2,1,0:T(8,128)(2,1)S(1)} %collective-permute-done.7.refs_7_) | copy-start | bytes 417796
  76.2 1.0 copy-start.2
  85.6 25.2 %all-to-all-start.2 = ((bf16[32,16,512]{2,1,0:T(8,128)(2,1)}), bf16[32,16,512]{2,1,0:T(8,128)(2,1)S(1)}, u32[]{:S(2)}, u32[]{:S(2)}) async-start(bf16[32,16,512]{2,1,0:T(8,128)(2,1)} %bitcast.68), calls=%async_computation.2 | async-start | bytes 1048576 | tf_op jit(solution)/shard_map/all_to_all | solution.py:598
  110.5 8.6 %collective-permute-start.8 = (bf16[256,2048]{1,0:T(8,128)(2,1)}, bf16[256,2048]{1,0:T(8,128)(2,1)S(1)}, u32[]{:S(2)}, u32[]{:S(2)}) collective-permute-start(bf16[256,2048]{1,0:T(8,128)(2,1)} %get-tuple-element.55), channel_id=1, source_target_pairs={{0,1},{1,0},{2,3},{3,2},{4,5},{5,4},{6,7},{7,6},{8,9},{9,8},{10,11... | collective-permute-start | bytes 3145736 | tf_op jit(solution)/shard_map/ppermute | solution.py:567
  110.8 5.7 %copy-start.4 = (bf16[32,16,512]{2,1,0:T(8,128)(2,1)}, bf16[32,16,512]{2,1,0:T(8,128)(2,1)S(1)}, u32[]{:S(2)}) copy-start(bf16[32,16,512]{2,1,0:T(8,128)(2,1)S(1)} %all-to-all-done.2) | copy-start | bytes 1572868
  110.8 28.1 %all-to-all-start.3 = ((bf16[32,24,512]{2,1,0:T(8,128)(2,1)}), bf16[32,24,512]{2,1,0:T(8,128)(2,1)S(1)}, u32[]{:S(2)}, u32[]{:S(2)}) async-start(bf16[32,24,512]{2,1,0:T(8,128)(2,1)} %bitcast.64), calls=%async_computation.3 | async-start | bytes 1572864 | tf_op jit(solution)/shard_map/all_to_all | solution.py:598
  116.6 2.5 %copy-start = (bf16[256,2048]{1,0:T(8,128)(2,1)S(1)}, bf16[256,2048]{1,0:T(8,128)(2,1)}, u32[]{:S(2)}) copy-start(bf16[256,2048]{1,0:T(8,128)(2,1)} %get-tuple-element.54) | copy-start | bytes 3145732
  119.6 28.6 %collective-permute-start.9 = (bf16[64,2048]{1,0:T(8,128)(2,1)S(1)}, bf16[64,2048]{1,0:T(8,128)(2,1)S(1)}, u32[]{:S(2)}, u32[]{:S(2)}) collective-permute-start(bf16[64,2048]{1,0:T(8,128)(2,1)S(1)} %get-tuple-element.61), channel_id=1, source_target_pairs={{0,8},{8,0},{16,24},{24,16},{1,9},{9,1},{17,25},{25,17},{2,10},{10... | collective-permute-start | bytes 786440 | tf_op jit(solution)/shard_map/ppermute | solution.py:567
  121.4 26.7 %collective-permute-start.11 = (bf16[64,2048]{1,0:T(8,128)(2,1)S(1)}, bf16[64,2048]{1,0:T(8,128)(2,1)S(1)}, u32[]{:S(2)}, u32[]{:S(2)}) collective-permute-start(bf16[64,2048]{1,0:T(8,128)(2,1)S(1)} %get-tuple-element.62), channel_id=1, source_target_pairs={{0,24},{8,16},{16,8},{24,0},{1,25},{9,17},{17,9},{25,1},{2,26},{10... | collective-permute-start | bytes 786440 | tf_op jit(solution)/shard_map/ppermute | solution.py:567
  122.9 25.3 %collective-permute-start.10 = (bf16[64,2048]{1,0:T(8,128)(2,1)S(1)}, bf16[64,2048]{1,0:T(8,128)(2,1)S(1)}, u32[]{:S(2)}, u32[]{:S(2)}) collective-permute-start(bf16[64,2048]{1,0:T(8,128)(2,1)S(1)} %get-tuple-element.63), channel_id=1, source_target_pairs={{0,16},{8,24},{16,0},{24,8},{1,17},{9,25},{17,1},{25,9},{2,18},{10... | collective-permute-start | bytes 786440 | tf_op jit(solution)/shard_map/ppermute | solution.py:567
  138.9 0.9 copy-start.3
  148.1 1.5 copy-start.5
  148.1 1.5 collective-permute-start.12
  149.6 5.0 %collective-permute-start.15 = (f32[16,512]{1,0:T(8,128)S(1)}, f32[16,512]{1,0:T(8,128)S(1)}, u32[]{:S(2)}, u32[]{:S(2)}) collective-permute-start(f32[16,512]{1,0:T(8,128)S(1)} %add.82), channel_id=1, source_target_pairs={{0,24},{8,16},{16,8},{24,0},{1,25},{9,17},{17,9},{25,1},{2,26},{10... | collective-permute-start | bytes 98312 | tf_op jit(solution)/shard_map/ppermute | solution.py:567
  150.0 4.5 %collective-permute-start.14 = (f32[16,512]{1,0:T(8,128)S(1)}, f32[16,512]{1,0:T(8,128)S(1)}, u32[]{:S(2)}, u32[]{:S(2)}) collective-permute-start(f32[16,512]{1,0:T(8,128)S(1)} %add.82), channel_id=1, source_target_pairs={{0,16},{8,24},{16,0},{24,8},{1,17},{9,25},{17,1},{25,9},{2,18},{10... | collective-permute-start | bytes 98312 | tf_op jit(solution)/shard_map/ppermute | solution.py:567
  151.5 3.9 %collective-permute-start.13 = (f32[16,512]{1,0:T(8,128)S(1)}, f32[16,512]{1,0:T(8,128)S(1)}, u32[]{:S(2)}, u32[]{:S(2)}) collective-permute-start(f32[16,512]{1,0:T(8,128)S(1)} %add.82), channel_id=1, source_target_pairs={{0,8},{8,0},{16,24},{24,16},{1,9},{9,1},{17,25},{25,17},{2,10},{10... | collective-permute-start | bytes 98312 | tf_op jit(solution)/shard_map/ppermute | solution.py:567
  155.5 8.9 %collective-permute-start.16 = (bf16[16,2560]{1,0:T(8,128)(2,1)S(1)}, bf16[16,2560]{1,0:T(8,128)(2,1)S(1)}, u32[]{:S(2)}, u32[]{:S(2)}) collective-permute-start(bf16[16,2560]{1,0:T(8,128)(2,1)S(1)} %get-tuple-element.89), channel_id=1, source_target_pairs={{0,2},{1,3},{2,0},{3,1},{4,6},{5,7},{6,4},{7,5},{8,10},{9,11},{10,... | collective-permute-start | bytes 245768 | tf_op jit(solution)/shard_map/ppermute | solution.py:567
  155.6 8.8 %collective-permute-start.17 = (bf16[16,2560]{1,0:T(8,128)(2,1)S(1)}, bf16[16,2560]{1,0:T(8,128)(2,1)S(1)}, u32[]{:S(2)}, u32[]{:S(2)}) collective-permute-start(bf16[16,2560]{1,0:T(8,128)(2,1)S(1)} %get-tuple-element.90), channel_id=1, source_target_pairs={{0,4},{1,5},{2,6},{3,7},{4,0},{5,1},{6,2},{7,3},{8,12},{9,13},{10,... | collective-permute-start | bytes 245768 | tf_op jit(solution)/shard_map/ppermute | solution.py:567
  157.1 7.4 %collective-permute-start.18 = (bf16[16,2560]{1,0:T(8,128)(2,1)S(1)}, bf16[16,2560]{1,0:T(8,128)(2,1)S(1)}, u32[]{:S(2)}, u32[]{:S(2)}) collective-permute-start(bf16[16,2560]{1,0:T(8,128)(2,1)S(1)} %get-tuple-element.91), channel_id=1, source_target_pairs={{0,6},{1,7},{2,4},{3,5},{4,2},{5,3},{6,0},{7,1},{8,14},{9,15},{10,... | collective-permute-start | bytes 245768 | tf_op jit(solution)/shard_map/ppermute | solution.py:567

commit v4 on v3

--- a/solution.py
+++ b/solution.py
@@ -16,7 +16,7 @@
 F32 = jnp.float32
 BF16 = jnp.bfloat16
 LIMIT = 56 * 1024 * 1024
-UNROLL = 2
+UNROLL = 4
 GROUP = 16
 
 
@@ -432,15 +432,19 @@
 
 
 def sums_kernel(count, *refs):
-    parts, orders, refs = refs[:count], refs[count : 2 * count], refs[2 * count :]
-    hbm, (left_ref, right_ref, gain_ref) = refs[:4], refs[4:7]
+    orders, refs = refs[:count], refs[count:]
+    hbm, refs = refs[:count], refs[count:]
+    hbm, (left_ref, right_ref, gain_ref) = hbm + refs[:4], refs[4:7]
     out_ref, sums_ref, dn, side_l, side_r = refs[7:12]
-    here, sems = refs[12:16], refs[16]
-    stat_ref, mixed_ref, grad_ref, pad_ref = here
+    here, sems = refs[12:-1], refs[-1]
+    parts = here[:count]
+    stat_ref, mixed_ref, grad_ref, pad_ref = here[count:]
     loads = moves(list(zip(hbm, here)), sems)
     batches, rows, cols, feats = pad_ref.shape
     rows -= 2
     cells = rows * cols
+    for copy in loads[:count]:
+        copy.wait()
     for b in range(batches):
         total = None
         for order, part in zip(orders, parts):
@@ -449,7 +453,7 @@
             total = term if total is None else total + term
         dn[b * cells : (b + 1) * cells, :] = total
     block = 64
-    for copy in loads[:3]:
+    for copy in loads[count : count + 3]:
         copy.wait()
 
     def norm(n, gain_sum):
@@ -465,7 +469,7 @@
     )
     sums_ref[9:10, :] = jnp.sum(gain_sum, axis=0, keepdims=True)
     sums_ref[10:, :] = jnp.zeros((sums_ref.shape[0] - 10, feats), F32)
-    loads[3].wait()
+    loads[count + 3].wait()
 
     four = 4
     width = 256
@@ -521,10 +525,22 @@
     convolve(pad, left_ref, right_ref, taps_of(dw_ref, True), side_l, side_r, out_ref)
 
 
-def call(body, outs, scratch, args, micros, name, hbm_ins=(), hbm_outs=(), scalars=()):
+def finish_kernel(*refs):
+    *parts, qkv_ref, wout_ref, gain_ref, kernel_ref = refs
+    feats = wout_ref.shape[1]
+    level = total([part[...].astype(F32) for part in parts])
+    qkv_ref[...] = level[:, : 3 * feats]
+    wout_ref[...] = level[:, 3 * feats : 4 * feats]
+    sums = level[:, 4 * feats :]
+    gain_ref[...] = sums[9:10]
+    for i in range(3):
+        kernel_ref[i] = sums[3 * i : 3 * i + 3]
+
+
+def call(body, outs, scratch, args, micros, name, hbm_ins=(), hbm_outs=(), scalars=(), limit=56 << 20):
     moved = sum(int(np.prod(o.shape)) * o.dtype.itemsize for o in (*outs, *args))
     vmem = pl.BlockSpec(memory_space=pltpu.VMEM)
-    hbm = pl.BlockSpec(memory_space=pl.ANY)
+    hbm = pl.BlockSpec(memory_space=pltpu.HBM)
     smem = pl.BlockSpec(memory_space=pltpu.SMEM)
     return pl.pallas_call(
         body,
@@ -534,7 +550,7 @@
         ],
         out_specs=[hbm if n in hbm_outs else vmem for n in range(len(outs))],
         scratch_shapes=scratch,
-        compiler_params=pltpu.CompilerParams(vmem_limit_bytes=LIMIT),
+        compiler_params=pltpu.CompilerParams(vmem_limit_bytes=limit),
         cost_estimate=pl.CostEstimate(
             flops=micros * 10**9, bytes_accessed=moved, transcendentals=0
         ),
@@ -578,7 +594,7 @@
     sums = sums.reshape(size, -1)
     load = lambda n: jnp.concatenate([blocks[n * size : (n + 1) * size], sums], axis=1).astype(BF16)
     own = jnp.concatenate([blocks[:size], sums], axis=1)
-    return [own, *(swap(load(n), axis, unit * n).astype(F32) for n in range(1, count))]
+    return [own, *(swap(load(n), axis, unit * n) for n in range(1, count))]
 
 
 def shards(plan, latent, w_qkv, w_out, ln_gain, dw_kernel, grad_out):
@@ -623,6 +639,7 @@
         [latent, above, below, left, right, dw_kernel, gain, send],
         6,
         "mix",
+        limit=50 << 20,
         hbm_outs=(1, 2, 3),
     )
     normed_win = trade(normed)
@@ -643,6 +660,7 @@
         [grad_win, w_out, *take],
         4,
         "grads",
+        limit=50 << 20,
     )
     mine = place_of(lax.axis_index("row"), lax.axis_index("col"), row_count, chips).astype(jnp.int32).reshape(1)
     half = shape((feats // 2, 4 * feats), BF16)
@@ -686,6 +704,7 @@
             args,
             2 + 20 * count // cells,
             "windows",
+        limit=56 << 20,
             hbm_ins=(0, 1, 4, *range(6, len(args))),
             hbm_outs=tuple(range(1, len(outs))),
             scalars=(5,),
@@ -701,6 +720,7 @@
         [d_parts[0], gain, *(jnp.asarray(m, BF16) for m in plan.pieces), *pairs],
         3,
         "border",
+        limit=50 << 20,
     )
     weights = (keep.astype(F32) + swap(give, "col", 1).astype(F32)).astype(BF16)
     d_mixed, sums = call(
@@ -710,17 +730,29 @@
             pltpu.VMEM((cells, feats), F32),
             side,
             side,
+            *(pltpu.VMEM((n, feats), BF16) for n in plan.rows),
             pltpu.VMEM(stat_shape, F32),
             pltpu.VMEM((cells, feats), BF16),
             pltpu.VMEM((cells, feats), BF16),
             pltpu.VMEM(padded, BF16),
-            pltpu.SemaphoreType.DMA((4,)),
+            pltpu.SemaphoreType.DMA((parts + 4,)),
         ],
-        [*d_parts, *back, stat, mixed, grad_flat, pad, left, right, gain],
+        [*back, *d_parts, stat, mixed, grad_flat, pad, left, right, gain],
         7,
         "sums",
-        hbm_ins=tuple(range(2 * parts, 2 * parts + 4)),
-    )
+        limit=50 << 20,
+        hbm_ins=tuple(range(parts, 2 * parts + 4)),
+    )
+    wide = 4 * feats
+    size = weights.shape[0] // row_count
+    gives = [
+        swap(weights[n * size : (n + 1) * size], "row", n) for n in range(1, row_count)
+    ]
+    sums, weights, *gives = lax.optimization_barrier((sums, weights, *gives))
+    weights = total([x.astype(F32) for x in (weights[:size], *gives)])
+    sums = sums + swap(sums, "col", 1)
+    sums = total([sums, *(swap(sums, "row", n) for n in range(1, row_count))])
+    sums, d_mixed = lax.optimization_barrier((sums, d_mixed))
     (grad_latent,) = call(
         spread_kernel,
         [flat],
@@ -728,22 +760,33 @@
         [d_mixed, *d_halos, dw_kernel],
         5,
         "spread",
-    )
-    wide = 4 * feats
-    size = weights.shape[0] // row_count
-    gives = [
-        swap(weights[n * size : (n + 1) * size], "row", n).astype(F32) for n in range(1, row_count)
-    ]
-    weights = total([weights[:size].astype(F32), *gives])
-    sums = sums + swap(sums, "col", 1)
-    sums = total([sums, *(swap(sums, "row", n) for n in range(1, row_count))])
+        limit=50 << 20,
+    )
     level = scatter(weights, sums, "col", 2, chips)
-    part = lambda first, last: total([x[:, first:last] for x in level])
-    sums = part(wide, None).reshape(16, feats)
+    grad_latent = grad_latent.reshape(latent.shape)
+    size = level[0].shape[0]
+    if size == 16:
+        qkv, wout, gain_sum, kernel_sum = call(
+            finish_kernel,
+            [
+                shape((size, 3 * feats), F32),
+                shape((size, feats), F32),
+                shape((1, feats), F32),
+                shape((3, 3, feats), F32),
+            ],
+            [],
+            level,
+            1,
+            "finish",
+            limit=50 << 20,
+        )
+        return grad_latent, qkv, wout, gain_sum.reshape(feats), kernel_sum
+    level = total([x.astype(F32) for x in level])
+    sums = level[:, wide:].reshape(16, feats)
     return (
-        grad_latent.reshape(latent.shape),
-        part(0, 3 * feats),
-        part(3 * feats, wide),
+        grad_latent,
+        level[:, : 3 * feats],
+        level[:, 3 * feats : wide],
         sums[9],
         sums[:9].reshape(3, 3, feats),
     )

time: 168 us -> 161 us (0.958)
  Pallas kernels: 59 us -> 50.7 us
    pallas_call x8 -> x9, Pallas kernels: 59 us -> 50.7 us  [call(): pl.pallas_call(body, out_shape=outs, in_specs=[smem if n in scalars else...]
    unnamed x34 -> x48, local copies, waits for them, and re-layouts: 2.59 us -> 4.1 us
  transfers between devices with their start and end apart: 23 -> 23, of which waited for: 10 -> 11; matrix products, arithmetic and copies ran while one was open for 5% -> 6% of each run, Pallas kernels for 28% -> 24%
where the time goes in v4:
time: 161 us; the launch traced here: 160 us
  starting transfers between devices  55 us (34%)
  Pallas kernels  50.7 us (31%)
  waiting for transfers between devices  38.8 us (24%)
  local copies, waits for them, and re-layouts  11 us (7%)
  other arithmetic  3.02 us (2%)
    pallas_call x9, Pallas kernels, call(): pl.pallas_call(body, out_shape=outs, in_specs=[smem if n in scalars else...  50.7 us
    all_to_all x4, starting transfers between devices, shards(): lax.all_to_all(x, AXES, split_axis=0, concat_axis=0, tiled=True)  26.4 us
    all_to_all x4, waiting for transfers between devices, shards(): lax.all_to_all(x, AXES, split_axis=0, concat_axis=0, tiled=True)  25.7 us
    ppermute x8, starting transfers between devices, shifted(): lax.ppermute(cells, axis, [(n, n + step) for n in range(count) if 0 <= n...  16.9 us
    ppermute x11, starting transfers between devices, swap(): lax.ppermute(x, axis, [(n, n ^ step) for n in range(lax.axis_size(axis))])  11.7 us
    ppermute x8, waiting for transfers between devices, shifted(): lax.ppermute(cells, axis, [(n, n + step) for n in range(count) if 0 <= n...  9.12 us
    unnamed x48, local copies, waits for them, and re-layouts  4.1 us
    ppermute x11, waiting for transfers between devices, swap(): lax.ppermute(x, axis, [(n, n ^ step) for n in range(lax.axis_size(axis))])  3.99 us
  transfers between devices with their start and end apart: 23, of which 11 were waited for; matrix products, arithmetic and copies ran while one was open for 6% of the time, Pallas kernels for 24%

profile of v4, /device:TPU:0, one launch (start us, length us, event | category | flops | bytes accessed | tf_op | source)
XLA Modules:
  0.0 159.8 jit_solution(17841837425263479147)
XLA Ops:
  0.6 3.1 %grad_send.1 = bf16[1024,512]{1,0:T(8,128)(2,1)} custom-call(bf16[1024,512]{1,0:T(8,128)(2,1)} %bitcast.76, bf16[512,512]{1,0:T(8,128)(2,1)} %constant.73.clone.order), custom_call_target="tpu_custom_call" | custom-call | flops 3000000000 | bytes 2621440 | tf_op jit(solution)/shard_map/grad_send/pallas_call | solution.py:545
  3.7 7.3 %all-to-all-start.1 = ((bf16[32,32,512]{2,1,0:T(8,128)(2,1)}), bf16[32,32,512]{2,1,0:T(8,128)(2,1)S(1)}, u32[]{:S(2)}, u32[]{:S(2)}) async-start(bf16[32,32,512]{2,1,0:T(8,128)(2,1)} %bitcast.67), calls=%async_computation.1 | async-start | bytes 2097152 | tf_op jit(solution)/shard_map/all_to_all | solution.py:614
  11.0 0.8 slice_bitcast_fusion.4
  11.8 1.3 collective-permute-start.1
  13.1 4.5 %collective-permute-start = (bf16[2,16,512]{2,1,0:T(8,128)(2,1)S(1)}, bf16[2,16,512]{2,1,0:T(8,128)(2,1)S(1)}, u32[]{:S(2)}, u32[]{:S(2)}) collective-permute-start(bf16[2,16,512]{2,1,0:T(8,128)(2,1)S(1)} %get-tuple-element.95), channel_id=1, source_target_pairs={{0,8},{8,16},{16,24},{1,9},{9,17},{17,25},{2,10},{10,18},{18,26},{... | collective-permute-start | bytes 98312 | tf_op jit(solution)/shard_map/ppermute | solution.py:567
  17.6 1.4 fusion.4
  19.1 0.3 collective-permute-done.top_ref
  19.5 1.6 %collective-permute-start.2 = (bf16[2,34,512]{2,1,0:T(8,128)(2,1)S(1)}, bf16[2,34,512]{2,1,0:T(8,128)(2,1)S(1)}, u32[]{:S(2)}, u32[]{:S(2)}) collective-permute-start(bf16[2,34,512]{2,1,0:T(8,128)(2,1)S(1)} %pad_maximum_fusion.6), channel_id=1, source_target_pairs={{0,1},{1,2},{2,3},{3,4},{4,5},{5,6},{6,7},{8,9},{9,10},{10,11},{11... | collective-permute-start | bytes 208904 | tf_op jit(solution)/shard_map/ppermute | solution.py:567
  21.2 1.3 collective-permute-start.3
  22.5 1.4 fusion.3
  23.9 1.9 %collective-permute-done.3.right_ref.refs_9_ = bf16[2,34,512]{2,1,0:T(8,128)(2,1)S(1)} collective-permute-done((bf16[2,34,512]{2,1,0:T(8,128)(2,1)S(1)}, bf16[2,34,512]{2,1,0:T(8,128)(2,1)S(1)}, u32[]{:S(2)}, u32[]{:S(2)}) %collective-permute-start.3) | collective-permute-done | bytes 69664 | tf_op jit(solution)/shard_map/ppermute | solution.py:567
  25.9 6.9 %mix.1 = (bf16[1024,512]{1,0:T(8,128)(2,1)}, bf16[1024,512]{1,0:T(8,128)(2,1)S(1)}, f32[1024,2]{1,0:T(8,128)S(1)}, bf16[2,34,16,512]{3,2,1,0:T(8,128)(2,1)}) custom-call(bf16[2,32,16,512]{3,2,1,0:T(8,128)(2,1)} %lat_ref.1, bf16[2,16,512]{2,1,0:T(8,128)(2,1)S(1)} %collective-permute-done.top_ref, bf16[2,16,512]{2,1,0:T(8,128)(2,1)S(1)} %collective-permute-done.1.bot_ref, ...), custom_call_target="tpu_custom_call" | custom-call | flops 6000000000 | bytes 5008384 | tf_op jit(solution)/shard_map/mix/pallas_call | solution.py:545
  32.7 0.8 copy-done.17
  33.6 5.0 %all-to-all-done.1 = bf16[32,32,512]{2,1,0:T(8,128)(2,1)S(1)} async-done(((bf16[32,32,512]{2,1,0:T(8,128)(2,1)}), bf16[32,32,512]{2,1,0:T(8,128)(2,1)S(1)}, u32[]{:S(2)}, u32[]{:S(2)}) %all-to-all-start.1) | async-done | bytes 1048608 | tf_op jit(solution)/shard_map/all_to_all | solution.py:614
  38.6 10.1 %all-to-all-start = ((bf16[32,32,512]{2,1,0:T(8,128)(2,1)}), bf16[32,32,512]{2,1,0:T(8,128)(2,1)}, u32[]{:S(2)}, u32[]{:S(2)}) async-start(bf16[32,32,512]{2,1,0:T(8,128)(2,1)} %bitcast.5), calls=%async_computation | async-start | bytes 2097152 | tf_op jit(solution)/shard_map/all_to_all | solution.py:614
  48.7 0.0 copy-start.7
  48.7 0.0 copy-start.8
  48.7 1.3 dynamic-slice_bitcast_fusion.back_ref
  50.1 0.8 slice_bitcast_fusion.2
  50.9 3.6 %collective-permute-start.4 = (bf16[2,16,1024]{2,1,0:T(8,128)(2,1)S(1)}, bf16[2,16,1024]{2,1,0:T(8,128)(2,1)S(1)}, u32[]{:S(2)}, u32[]{:S(2)}) collective-permute-start(bf16[2,16,1024]{2,1,0:T(8,128)(2,1)S(1)} %pad_maximum_fusion.8), channel_id=1, source_target_pairs={{0,8},{8,16},{16,24},{1,9},{9,17},{17,25},{2,10},{10,18},{18,26},{... | collective-permute-start | bytes 196616 | tf_op jit(solution)/shard_map/ppermute | solution.py:567
  54.5 0.2 fusion.2
  54.8 1.3 collective-permute-start.5
  56.1 1.6 collective-permute-done.4.refs_4_
  57.7 5.3 %collective-permute-done.5.refs_5_ = bf16[2,16,1024]{2,1,0:T(8,128)(2,1)S(1)} collective-permute-done((bf16[2,16,1024]{2,1,0:T(8,128)(2,1)S(1)}, bf16[2,16,1024]{2,1,0:T(8,128)(2,1)S(1)}, u32[]{:S(2)}, u32[]{:S(2)}) %collective-permute-start.5) | collective-permute-done | bytes 65568 | tf_op jit(solution)/shard_map/ppermute | solution.py:567
  63.0 0.1 pad_maximum_fusion
  63.1 2.0 %collective-permute-start.6 = (bf16[2,34,1024]{2,1,0:T(8,128)(2,1)S(1)}, bf16[2,34,1024]{2,1,0:T(8,128)(2,1)S(1)}, u32[]{:S(2)}, u32[]{:S(2)}) collective-permute-start(bf16[2,34,1024]{2,1,0:T(8,128)(2,1)S(1)} %pad_maximum_fusion), channel_id=1, source_target_pairs={{0,1},{1,2},{2,3},{3,4},{4,5},{5,6},{6,7},{8,9},{9,10},{10,11},{11... | collective-permute-start | bytes 417800 | tf_op jit(solution)/shard_map/ppermute | solution.py:567
  65.1 0.1 pad_maximum_fusion.1
  65.1 1.3 collective-permute-start.7
  66.5 1.3 grads.1
  67.8 0.9 copy-done.13
  68.6 0.9 copy-done.14
  69.5 0.7 copy-done.16
  70.2 6.0 %all-to-all-done = bf16[32,32,512]{2,1,0:T(8,128)(2,1)} async-done(((bf16[32,32,512]{2,1,0:T(8,128)(2,1)}), bf16[32,32,512]{2,1,0:T(8,128)(2,1)}, u32[]{:S(2)}, u32[]{:S(2)}) %all-to-all-start) | async-done | bytes 1048608 | tf_op jit(solution)/shard_map/all_to_all | solution.py:614
  76.3 8.2 %windows.2 = (bf16[512,512]{1,0:T(8,128)(2,1)}, bf16[256,512]{1,0:T(8,128)(2,1)}, bf16[256,512]{1,0:T(8,128)(2,1)}, bf16[256,1536]{1,0:T(8,128)(2,1)}) custom-call(bf16[1024,512]{1,0:T(8,128)(2,1)} %bitcast.6.n_hbm, bf16[256,512]{1,0:T(8,128)(2,1)} %copy-done.16, bf16[64,256]{1,0:T(8,128)(2,1)} %constant.78.clone.refs_0_.take_ref, ...), custom_call_target="tpu_custom_call" | custom-call | flops 7000000000 | bytes 4753408 | tf_op jit(solution)/shard_map/windows/pallas_call | solution.py:545
  84.4 3.2 %all-to-all-start.2 = ((bf16[32,16,512]{2,1,0:T(8,128)(2,1)}), bf16[32,16,512]{2,1,0:T(8,128)(2,1)S(1)}, u32[]{:S(2)}, u32[]{:S(2)}) async-start(bf16[32,16,512]{2,1,0:T(8,128)(2,1)} %bitcast.69), calls=%async_computation.2 | async-start | bytes 1048576 | tf_op jit(solution)/shard_map/all_to_all | solution.py:614
  87.7 20.9 %windows.3 = (bf16[768,512]{1,0:T(8,128)(2,1)}, bf16[256,2048]{1,0:T(8,128)(2,1)}, bf16[256,2048]{1,0:T(8,128)(2,1)}) custom-call(bf16[1024,512]{1,0:T(8,128)(2,1)} %bitcast.6.n_hbm, bf16[768,512]{1,0:T(8,128)(2,1)} %copy-done.14, bf16[192,256]{1,0:T(8,128)(2,1)} %constant.79.clone.refs_1_.take_ref, bf16[192,192]{1,0:T(8,128)(2,1)} %constant.77.clone.back_ref, ...), custom_call_target="tpu_custom_call" | custom-call | flops 16999999488 | bytes 8822788 | tf_op jit(solution)/shard_map/windows/pallas_call | solution.py:545
  108.6 0.0 copy-start.9
  108.6 0.0 copy-start.11
  108.6 0.2 collective-permute-start.8
  108.8 5.7 %all-to-all-start.3 = ((bf16[32,24,512]{2,1,0:T(8,128)(2,1)}), bf16[32,24,512]{2,1,0:T(8,128)(2,1)S(1)}, u32[]{:S(2)}, u32[]{:S(2)}) async-start(bf16[32,24,512]{2,1,0:T(8,128)(2,1)} %bitcast.68), calls=%async_computation.3 | async-start | bytes 1572864 | tf_op jit(solution)/shard_map/all_to_all | solution.py:614
  114.6 0.6 border.1
  115.1 0.6 copy-done.20
  115.8 1.6 %add_convert_fusion = bf16[256,2048]{1,0:T(8,128)(2,1)S(1)} fusion(bf16[256,2048]{1,0:T(8,128)(2,1)} %collective-permute-done.8, bf16[256,2048]{1,0:T(8,128)(2,1)S(1)} %copy-done.20), kind=kLoop, calls=%fused_computation | loop fusion | flops 2097152 | bytes 3145728 | tf_op jit(solution)/shard_map/convert_element_type | solution.py:725
  117.5 0.9 fusion.1
  118.3 2.7 %collective-permute-start.11 = (bf16[64,2048]{1,0:T(8,128)(2,1)}, bf16[64,2048]{1,0:T(8,128)(2,1)S(1)}, u32[]{:S(2)}, u32[]{:S(2)}) collective-permute-start(bf16[64,2048]{1,0:T(8,128)(2,1)} %get-tuple-element.81), channel_id=1, source_target_pairs={{0,24},{8,16},{16,8},{24,0},{1,25},{9,17},{17,9},{25,1},{2,26},{10... | collective-permute-start | bytes 786440 | tf_op jit(solution)/shard_map/ppermute | solution.py:583
  121.0 0.6 collective-permute-start.10
  121.6 0.3 collective-permute-start.9
  121.8 14.7 %all-to-all-done.3 = bf16[32,24,512]{2,1,0:T(8,128)(2,1)S(1)} async-done(((bf16[32,24,512]{2,1,0:T(8,128)(2,1)}), bf16[32,24,512]{2,1,0:T(8,128)(2,1)S(1)}, u32[]{:S(2)}, u32[]{:S(2)}) %all-to-all-start.3) | async-done | bytes 786464 | tf_op jit(solution)/shard_map/all_to_all | solution.py:614
  136.5 6.1 %sums.1 = (bf16[1024,512]{1,0:T(8,128)(2,1)S(1)}, f32[16,512]{1,0:T(8,128)S(1)}) custom-call(bf16[512,256]{1,0:T(8,128)(2,1)S(1)} %copy-done.6, bf16[512,384]{1,0:T(8,128)(2,1)S(1)} %copy-done.5, bf16[512,512]{1,0:T(8,128)(2,1)S(1)} %bitcast.61, bf16[768,512]{1,0:T(8,128)(2,1)S(1)} %bitcast.59, f32[1024,2]{1,0:T(8,128)S(1)} %copy-done.18, ...), custom_call_target="tpu_custom_call" | custom-call | flops 7000000000 | bytes 6408192 | tf_op jit(solution)/shard_map/sums/pallas_call | solution.py:545
  142.6 0.1 collective-permute-start.12
  142.7 1.2 fusion
  143.8 0.0 collective-permute-done.12
  143.9 1.0 collective-permute-start.15
  144.9 1.5 collective-permute-start.14
  146.4 1.1 collective-permute-start.13
  147.5 1.6 collective-permute-done.15
  149.0 0.1 collective-permute-done.14
  149.1 1.2 collective-permute-done.13
  150.3 0.9 collective-permute-start.18
  151.2 0.3 collective-permute-start.17
  151.5 3.3 %collective-permute-start.16 = (bf16[16,2560]{1,0:T(8,128)(2,1)S(1)}, bf16[16,2560]{1,0:T(8,128)(2,1)S(1)}, u32[]{:S(2)}, u32[]{:S(2)}) collective-permute-start(bf16[16,2560]{1,0:T(8,128)(2,1)S(1)} %get-tuple-element.109), channel_id=1, source_target_pairs={{0,2},{1,3},{2,0},{3,1},{4,6},{5,7},{6,4},{7,5},{8,10},{9,11},{10,... | collective-permute-start | bytes 245768 | tf_op jit(solution)/shard_map/ppermute | solution.py:583
  154.8 3.1 %spread.1 = bf16[1024,512]{1,0:T(8,128)(2,1)} custom-call(bf16[1024,512]{1,0:T(8,128)(2,1)S(1)} %get-tuple-element.61.d_ref, bf16[2,16,512]{2,1,0:T(8,128)(2,1)S(1)} %get-tuple-element.66.top_ref, bf16[2,16,512]{2,1,0:T(8,128)(2,1)S(1)} %get-tuple-element.67.bot_ref, bf16[2,34,512]{2,1,0:T(8,128)(2,1)S(1)} %get-tuple-element.68.left_ref, ...), custom_call_target="tpu_custom_call" | custom-call | flops 5000000000 | bytes 2311168 | tf_op jit(solution)/shard_map/spread/pallas_call | solution.py:545
  158.0 1.1 collective-permute-done.17.refs_2_
  159.1 0.7 finish.1
  (66 shorter events, 0.4 us)
Async XLA Ops:
  3.7 22.2 %copy-start.2 = (bf16[3,3,512]{2,1,0:T(4,128)(2,1)S(1)}, bf16[3,3,512]{2,1,0:T(4,128)(2,1)}, u32[]{:S(2)}) copy-start(bf16[3,3,512]{2,1,0:T(4,128)(2,1)} %dw_ref.3) | copy-start | bytes 27652
  3.7 22.2 %copy-start.3 = (f32[512]{0:T(512)S(1)}, f32[512]{0:T(512)}, u32[]{:S(2)}) copy-start(f32[512]{0:T(512)} %param.20) | copy-start | bytes 6148
  3.7 22.2 %copy-start.4 = (bf16[512,512]{1,0:T(8,128)(2,1)S(1)}, bf16[512,512]{1,0:T(8,128)(2,1)}, u32[]{:S(2)}) copy-start(bf16[512,512]{1,0:T(8,128)(2,1)} %constant.73.clone.order) | copy-start | bytes 1572868
  3.7 34.9 %all-to-all-start.1 = ((bf16[32,32,512]{2,1,0:T(8,128)(2,1)}), bf16[32,32,512]{2,1,0:T(8,128)(2,1)S(1)}, u32[]{:S(2)}, u32[]{:S(2)}) async-start(bf16[32,32,512]{2,1,0:T(8,128)(2,1)} %bitcast.67), calls=%async_computation.1 | async-start | bytes 2097152 | tf_op jit(solution)/shard_map/all_to_all | solution.py:614
  11.8 7.3 %collective-permute-start.1 = (bf16[2,16,512]{2,1,0:T(8,128)(2,1)S(1)}, bf16[2,16,512]{2,1,0:T(8,128)(2,1)S(1)}, u32[]{:S(2)}, u32[]{:S(2)}) collective-permute-start(bf16[2,16,512]{2,1,0:T(8,128)(2,1)S(1)} %get-tuple-element.94), channel_id=1, source_target_pairs={{8,0},{16,8},{24,16},{9,1},{17,9},{25,17},{10,2},{18,10},{26,18},{... | collective-permute-start | bytes 98312 | tf_op jit(solution)/shard_map/ppermute | solution.py:567
  13.1 6.4 %collective-permute-start = (bf16[2,16,512]{2,1,0:T(8,128)(2,1)S(1)}, bf16[2,16,512]{2,1,0:T(8,128)(2,1)S(1)}, u32[]{:S(2)}, u32[]{:S(2)}) collective-permute-start(bf16[2,16,512]{2,1,0:T(8,128)(2,1)S(1)} %get-tuple-element.95), channel_id=1, source_target_pairs={{0,8},{8,16},{16,24},{1,9},{9,17},{17,25},{2,10},{10,18},{18,26},{... | collective-permute-start | bytes 98312 | tf_op jit(solution)/shard_map/ppermute | solution.py:567
  19.5 4.4 %collective-permute-start.2 = (bf16[2,34,512]{2,1,0:T(8,128)(2,1)S(1)}, bf16[2,34,512]{2,1,0:T(8,128)(2,1)S(1)}, u32[]{:S(2)}, u32[]{:S(2)}) collective-permute-start(bf16[2,34,512]{2,1,0:T(8,128)(2,1)S(1)} %pad_maximum_fusion.6), channel_id=1, source_target_pairs={{0,1},{1,2},{2,3},{3,4},{4,5},{5,6},{6,7},{8,9},{9,10},{10,11},{11... | collective-permute-start | bytes 208904 | tf_op jit(solution)/shard_map/ppermute | solution.py:567
  21.2 4.7 %collective-permute-start.3 = (bf16[2,34,512]{2,1,0:T(8,128)(2,1)S(1)}, bf16[2,34,512]{2,1,0:T(8,128)(2,1)S(1)}, u32[]{:S(2)}, u32[]{:S(2)}) collective-permute-start(bf16[2,34,512]{2,1,0:T(8,128)(2,1)S(1)} %pad_maximum_fusion.7), channel_id=1, source_target_pairs={{1,0},{2,1},{3,2},{4,3},{5,4},{6,5},{7,6},{9,8},{10,9},{11,10},{12... | collective-permute-start | bytes 208904 | tf_op jit(solution)/shard_map/ppermute | solution.py:567
  32.7 0.8 copy-start.17
  33.6 21.2 %copy-start = (bf16[1024,512]{1,0:T(8,128)(2,1)}, bf16[1024,512]{1,0:T(8,128)(2,1)S(1)}, u32[]{:S(2)}) copy-start(bf16[1024,512]{1,0:T(8,128)(2,1)S(1)} %get-tuple-element.43.refs_5_) | copy-start | bytes 3145732
  38.6 37.7 %all-to-all-start = ((bf16[32,32,512]{2,1,0:T(8,128)(2,1)}), bf16[32,32,512]{2,1,0:T(8,128)(2,1)}, u32[]{:S(2)}, u32[]{:S(2)}) async-start(bf16[32,32,512]{2,1,0:T(8,128)(2,1)} %bitcast.5), calls=%async_computation | async-start | bytes 2097152 | tf_op jit(solution)/shard_map/all_to_all | solution.py:614
  48.7 17.7 %copy-start.1 = (bf16[512,512]{1,0:T(8,128)(2,1)S(1)}, bf16[512,512]{1,0:T(8,128)(2,1)}, u32[]{:S(2)}) copy-start(bf16[512,512]{1,0:T(8,128)(2,1)} %wout_ref.1) | copy-start | bytes 1572868
  48.7 17.7 %copy-start.7 = (bf16[192,256]{1,0:T(8,128)(2,1)S(1)}, bf16[192,256]{1,0:T(8,128)(2,1)}, u32[]{:S(2)}) copy-start(bf16[192,256]{1,0:T(8,128)(2,1)} %constant.79.clone.refs_1_.take_ref) | copy-start | bytes 294916
  48.7 17.7 %copy-start.8 = (bf16[64,256]{1,0:T(8,128)(2,1)S(1)}, bf16[64,256]{1,0:T(8,128)(2,1)}, u32[]{:S(2)}) copy-start(bf16[64,256]{1,0:T(8,128)(2,1)} %constant.78.clone.refs_0_.take_ref) | copy-start | bytes 98308
  50.9 6.8 %collective-permute-start.4 = (bf16[2,16,1024]{2,1,0:T(8,128)(2,1)S(1)}, bf16[2,16,1024]{2,1,0:T(8,128)(2,1)S(1)}, u32[]{:S(2)}, u32[]{:S(2)}) collective-permute-start(bf16[2,16,1024]{2,1,0:T(8,128)(2,1)S(1)} %pad_maximum_fusion.8), channel_id=1, source_target_pairs={{0,8},{8,16},{16,24},{1,9},{9,17},{17,25},{2,10},{10,18},{18,26},{... | collective-permute-start | bytes 196616 | tf_op jit(solution)/shard_map/ppermute | solution.py:567
  54.8 8.2 %collective-permute-start.5 = (bf16[2,16,1024]{2,1,0:T(8,128)(2,1)S(1)}, bf16[2,16,1024]{2,1,0:T(8,128)(2,1)S(1)}, u32[]{:S(2)}, u32[]{:S(2)}) collective-permute-start(bf16[2,16,1024]{2,1,0:T(8,128)(2,1)S(1)} %pad_maximum_fusion.9), channel_id=1, source_target_pairs={{8,0},{16,8},{24,16},{9,1},{17,9},{25,17},{10,2},{18,10},{26,18},{... | collective-permute-start | bytes 196616 | tf_op jit(solution)/shard_map/ppermute | solution.py:567
  63.1 7.1 %collective-permute-start.6 = (bf16[2,34,1024]{2,1,0:T(8,128)(2,1)S(1)}, bf16[2,34,1024]{2,1,0:T(8,128)(2,1)S(1)}, u32[]{:S(2)}, u32[]{:S(2)}) collective-permute-start(bf16[2,34,1024]{2,1,0:T(8,128)(2,1)S(1)} %pad_maximum_fusion), channel_id=1, source_target_pairs={{0,1},{1,2},{2,3},{3,4},{4,5},{5,6},{6,7},{8,9},{9,10},{10,11},{11... | collective-permute-start | bytes 417800 | tf_op jit(solution)/shard_map/ppermute | solution.py:567
  65.1 5.1 %collective-permute-start.7 = (bf16[2,34,1024]{2,1,0:T(8,128)(2,1)S(1)}, bf16[2,34,1024]{2,1,0:T(8,128)(2,1)S(1)}, u32[]{:S(2)}, u32[]{:S(2)}) collective-permute-start(bf16[2,34,1024]{2,1,0:T(8,128)(2,1)S(1)} %pad_maximum_fusion.1), channel_id=1, source_target_pairs={{1,0},{2,1},{3,2},{4,3},{5,4},{6,5},{7,6},{9,8},{10,9},{11,10},{12... | collective-permute-start | bytes 417800 | tf_op jit(solution)/shard_map/ppermute | solution.py:567
  67.7 0.9 copy-start.13
  68.6 0.9 copy-start.14
  69.5 0.7 copy-start.16
  70.2 14.2 %copy-start.15 = (bf16[256,512]{1,0:T(8,128)(2,1)}, bf16[256,512]{1,0:T(8,128)(2,1)S(1)}, u32[]{:S(2)}) copy-start(bf16[256,512]{1,0:T(8,128)(2,1)S(1)} %get-tuple-element.52.refs_5_) | copy-start | bytes 786436
  84.4 24.3 %all-to-all-start.2 = ((bf16[32,16,512]{2,1,0:T(8,128)(2,1)}), bf16[32,16,512]{2,1,0:T(8,128)(2,1)S(1)}, u32[]{:S(2)}, u32[]{:S(2)}) async-start(bf16[32,16,512]{2,1,0:T(8,128)(2,1)} %bitcast.69), calls=%async_computation.2 | async-start | bytes 1048576 | tf_op jit(solution)/shard_map/all_to_all | solution.py:614
  108.6 6.0 %copy-start.9 = (bf16[34,256]{1,0:T(8,128)(2,1)S(1)}, bf16[34,256]{1,0:T(8,128)(2,1)}, u32[]{:S(2)}) copy-start(bf16[34,256]{1,0:T(8,128)(2,1)} %constant.83.clone.refs_3_) | copy-start | bytes 52228
  108.6 6.0 %copy-start.10 = (bf16[34,256]{1,0:T(8,128)(2,1)S(1)}, bf16[34,256]{1,0:T(8,128)(2,1)}, u32[]{:S(2)}) copy-start(bf16[34,256]{1,0:T(8,128)(2,1)} %constant.82.clone.refs_2_) | copy-start | bytes 52228
  108.6 5.9 %copy-start.11 = (bf16[16,256]{1,0:T(8,128)(2,1)S(1)}, bf16[16,256]{1,0:T(8,128)(2,1)}, u32[]{:S(2)}) copy-start(bf16[16,256]{1,0:T(8,128)(2,1)} %constant.81.clone.refs_1_) | copy-start | bytes 24580
  108.6 5.9 %copy-start.12 = (bf16[16,256]{1,0:T(8,128)(2,1)S(1)}, bf16[16,256]{1,0:T(8,128)(2,1)}, u32[]{:S(2)}) copy-start(bf16[16,256]{1,0:T(8,128)(2,1)} %constant.80.clone.refs_0_) | copy-start | bytes 24580
  108.6 6.5 %collective-permute-start.8 = (bf16[256,2048]{1,0:T(8,128)(2,1)}, bf16[256,2048]{1,0:T(8,128)(2,1)}, u32[]{:S(2)}, u32[]{:S(2)}) collective-permute-start(bf16[256,2048]{1,0:T(8,128)(2,1)} %get-tuple-element.58), channel_id=1, source_target_pairs={{0,1},{1,0},{2,3},{3,2},{4,5},{5,4},{6,7},{7,6},{8,9},{9,8},{10,11... | collective-permute-start | bytes 3145736 | tf_op jit(solution)/shard_map/ppermute | solution.py:583
  108.8 27.7 %all-to-all-start.3 = ((bf16[32,24,512]{2,1,0:T(8,128)(2,1)}), bf16[32,24,512]{2,1,0:T(8,128)(2,1)S(1)}, u32[]{:S(2)}, u32[]{:S(2)}) async-start(bf16[32,24,512]{2,1,0:T(8,128)(2,1)} %bitcast.68), calls=%async_computation.3 | async-start | bytes 1572864 | tf_op jit(solution)/shard_map/all_to_all | solution.py:614
  114.6 1.2 copy-start.20
  117.4 4.2 %copy-start.19 = (bf16[256,2048]{1,0:T(8,128)(2,1)}, bf16[256,2048]{1,0:T(8,128)(2,1)S(1)}, u32[]{:S(2)}) copy-start(bf16[256,2048]{1,0:T(8,128)(2,1)S(1)} %add_convert_fusion) | copy-start | bytes 3145732
  117.4 19.1 %copy-start.5 = (bf16[512,384]{1,0:T(8,128)(2,1)S(1)}, bf16[512,384]{1,0:T(8,128)(2,1)}, u32[]{:S(2)}) copy-start(bf16[512,384]{1,0:T(8,128)(2,1)} %constant.76.clone.refs_1_) | copy-start | bytes 1179652
  117.4 19.1 %copy-start.6 = (bf16[512,256]{1,0:T(8,128)(2,1)S(1)}, bf16[512,256]{1,0:T(8,128)(2,1)}, u32[]{:S(2)}) copy-start(bf16[512,256]{1,0:T(8,128)(2,1)} %constant.75.clone.refs_0_) | copy-start | bytes 786436
  117.4 19.1 %copy-start.18 = (f32[1024,2]{1,0:T(8,128)S(1)}, f32[1024,2]{1,0:T(8,128)}, u32[]{:S(2)}) copy-start(f32[1024,2]{1,0:T(8,128)} %copy-done.17) | copy-start | bytes 24580
  118.3 24.2 %collective-permute-start.11 = (bf16[64,2048]{1,0:T(8,128)(2,1)}, bf16[64,2048]{1,0:T(8,128)(2,1)S(1)}, u32[]{:S(2)}, u32[]{:S(2)}) collective-permute-start(bf16[64,2048]{1,0:T(8,128)(2,1)} %get-tuple-element.81), channel_id=1, source_target_pairs={{0,24},{8,16},{16,8},{24,0},{1,25},{9,17},{17,9},{25,1},{2,26},{10... | collective-permute-start | bytes 786440 | tf_op jit(solution)/shard_map/ppermute | solution.py:583
  121.0 21.6 %collective-permute-start.10 = (bf16[64,2048]{1,0:T(8,128)(2,1)}, bf16[64,2048]{1,0:T(8,128)(2,1)S(1)}, u32[]{:S(2)}, u32[]{:S(2)}) collective-permute-start(bf16[64,2048]{1,0:T(8,128)(2,1)} %get-tuple-element.82), channel_id=1, source_target_pairs={{0,16},{8,24},{16,0},{24,8},{1,17},{9,25},{17,1},{25,9},{2,18},{10... | collective-permute-start | bytes 786440 | tf_op jit(solution)/shard_map/ppermute | solution.py:583
  121.6 21.0 %collective-permute-start.9 = (bf16[64,2048]{1,0:T(8,128)(2,1)}, bf16[64,2048]{1,0:T(8,128)(2,1)}, u32[]{:S(2)}, u32[]{:S(2)}) collective-permute-start(bf16[64,2048]{1,0:T(8,128)(2,1)} %get-tuple-element.83), channel_id=1, source_target_pairs={{0,8},{8,0},{16,24},{24,16},{1,9},{9,1},{17,25},{25,17},{2,10},{10... | collective-permute-start | bytes 786440 | tf_op jit(solution)/shard_map/ppermute | solution.py:583
  142.6 1.3 collective-permute-start.12
  143.9 5.1 %collective-permute-start.15 = (f32[16,512]{1,0:T(8,128)S(1)}, f32[16,512]{1,0:T(8,128)S(1)}, u32[]{:S(2)}, u32[]{:S(2)}) collective-permute-start(f32[16,512]{1,0:T(8,128)S(1)} %add.52), channel_id=1, source_target_pairs={{0,24},{8,16},{16,8},{24,0},{1,25},{9,17},{17,9},{25,1},{2,26},{10... | collective-permute-start | bytes 98312 | tf_op jit(solution)/shard_map/ppermute | solution.py:583
  144.9 4.2 %collective-permute-start.14 = (f32[16,512]{1,0:T(8,128)S(1)}, f32[16,512]{1,0:T(8,128)S(1)}, u32[]{:S(2)}, u32[]{:S(2)}) collective-permute-start(f32[16,512]{1,0:T(8,128)S(1)} %add.52), channel_id=1, source_target_pairs={{0,16},{8,24},{16,0},{24,8},{1,17},{9,25},{17,1},{25,9},{2,18},{10... | collective-permute-start | bytes 98312 | tf_op jit(solution)/shard_map/ppermute | solution.py:583
  146.4 3.9 %collective-permute-start.13 = (f32[16,512]{1,0:T(8,128)S(1)}, f32[16,512]{1,0:T(8,128)S(1)}, u32[]{:S(2)}, u32[]{:S(2)}) collective-permute-start(f32[16,512]{1,0:T(8,128)S(1)} %add.52), channel_id=1, source_target_pairs={{0,8},{8,0},{16,24},{24,16},{1,9},{9,1},{17,25},{25,17},{2,10},{10... | collective-permute-start | bytes 98312 | tf_op jit(solution)/shard_map/ppermute | solution.py:583
  150.3 7.6 %collective-permute-start.18 = (bf16[16,2560]{1,0:T(8,128)(2,1)S(1)}, bf16[16,2560]{1,0:T(8,128)(2,1)S(1)}, u32[]{:S(2)}, u32[]{:S(2)}) collective-permute-start(bf16[16,2560]{1,0:T(8,128)(2,1)S(1)} %get-tuple-element.107), channel_id=1, source_target_pairs={{0,6},{1,7},{2,4},{3,5},{4,2},{5,3},{6,0},{7,1},{8,14},{9,15},{10,... | collective-permute-start | bytes 245768 | tf_op jit(solution)/shard_map/ppermute | solution.py:583
  151.2 7.9 %collective-permute-start.17 = (bf16[16,2560]{1,0:T(8,128)(2,1)S(1)}, bf16[16,2560]{1,0:T(8,128)(2,1)S(1)}, u32[]{:S(2)}, u32[]{:S(2)}) collective-permute-start(bf16[16,2560]{1,0:T(8,128)(2,1)S(1)} %get-tuple-element.108), channel_id=1, source_target_pairs={{0,4},{1,5},{2,6},{3,7},{4,0},{5,1},{6,2},{7,3},{8,12},{9,13},{10,... | collective-permute-start | bytes 245768 | tf_op jit(solution)/shard_map/ppermute | solution.py:583
  151.5 7.6 %collective-permute-start.16 = (bf16[16,2560]{1,0:T(8,128)(2,1)S(1)}, bf16[16,2560]{1,0:T(8,128)(2,1)S(1)}, u32[]{:S(2)}, u32[]{:S(2)}) collective-permute-start(bf16[16,2560]{1,0:T(8,128)(2,1)S(1)} %get-tuple-element.109), channel_id=1, source_target_pairs={{0,2},{1,3},{2,0},{3,1},{4,6},{5,7},{6,4},{7,5},{8,10},{9,11},{10,... | collective-permute-start | bytes 245768 | tf_op jit(solution)/shard_map/ppermute | solution.py:583

commit v5 on v4

--- a/solution.py
+++ b/solution.py
@@ -140,6 +140,18 @@
                             target = (i * col_count + j) * size + used[owner]
                             self.index[owner, 0, target] = around[source, slot, rep]
                 used[owner] += 1
+        border = [(h, w) for h in (0, tile_rows - 1) for w in range(tile_cols)]
+        border += [(h, w) for w in (0, tile_cols - 1) for h in range(tile_rows)]
+        self.unpick = np.zeros((cells, len(border)), np.float32)
+        for n, (h, w) in enumerate(border):
+            if n < 2 * tile_cols or h not in (0, tile_rows - 1):
+                self.unpick[h * tile_cols + w, n] = 1
+        self.send_border = self.send_all @ self.unpick
+        self.send_inner = self.send_all * (1 - self.unpick.sum(1))[None]
+        self.columns = np.zeros((4 * tile_rows, cells), np.float32)
+        for n, w in enumerate((0, 1, tile_cols - 2, tile_cols - 1)):
+            for h in range(tile_rows):
+                self.columns[n * tile_rows + h, h * tile_cols + w] = 1
         self.share = share
         self.windows = [m.shape[0] // GROUP for m in self.sort]
         self.rows = [batches * m.shape[0] for m in self.send]
@@ -158,6 +170,10 @@
     four = 4
     width = 256
     for b in range(batches):
+        if left_ref is None:
+            side_l[b] = jnp.zeros(side_l.shape[1:], F32)
+            side_r[b] = jnp.zeros(side_r.shape[1:], F32)
+            continue
         left, right = left_ref[b].astype(F32), right_ref[b].astype(F32)
         side_l[b] = sum(kern[i][0] * left[i : i + rows] for i in range(3))
         side_r[b] = sum(kern[i][2] * right[i : i + rows] for i in range(3))
@@ -194,32 +210,115 @@
     ]
 
 
-def mix_kernel(lat_ref, top_ref, bot_ref, left_ref, right_ref, dw_ref, gain_ref, order, *refs):
-    out, mixed_out, stat_out, pad_out = refs[:4]
-    mixed_ref, stat_ref, pad_ref, normed_ref, side_l, side_r, sems = refs[4:]
+def norm(mixed, gain):
+    mixed = mixed.astype(F32)
+    mean = jnp.mean(mixed, axis=-1, keepdims=True)
+    centred = mixed - mean
+    rstd = lax.rsqrt(jnp.mean(centred * centred, axis=-1, keepdims=True) + 1e-05)
+    return mean, rstd, (centred * rstd * gain).astype(BF16)
+
+
+def inner_kernel(lat_ref, dw_ref, gain_ref, order, columns_ref, *refs):
+    out, mixed_out, rows_ref, cols_ref, mixed_ref, pad_ref, normed_ref, side_l, side_r, sems = refs
     batches, rows, cols, feats = lat_ref.shape
+    cells = rows * cols
+    pad_ref[:, 1 : rows + 1] = lat_ref[...]
+    pad_ref[:, 0] = jnp.zeros((batches, cols, feats), BF16)
+    pad_ref[:, rows + 1] = jnp.zeros((batches, cols, feats), BF16)
+    for b in range(batches):
+        rows_ref[b, :2] = lat_ref[b, :2]
+        rows_ref[b, 2:] = lat_ref[b, rows - 2 :]
+        for h in range(rows):
+            normed_ref[b * cells + h * cols : b * cells + (h + 1) * cols, :] = lat_ref[b, h]
+        cols_ref[b] = dot(columns_ref[...], normed_ref[b * cells : (b + 1) * cells, :]).astype(BF16)
+    convolve(pad_ref, None, None, taps_of(dw_ref, False), side_l, side_r, mixed_ref)
+    copies = moves([(mixed_ref, mixed_out)], sems)
+    block = 64
+
+    def step(n, carry):
+        at = pl.ds(pl.multiple_of(n * block, block), block)
+        normed_ref[at, :] = norm(mixed_ref[at, :], gain_ref[...])[2]
+        return carry
+
+    lax.fori_loop(0, batches * cells // block, step, 0, unroll=2)
+    send_kernel(batches, normed_ref, order, out)
+    for copy in copies:
+        copy.wait()
+
+
+def edge_kernel(
+    inner_ref, rows_ref, cols_ref, top_ref, bot_ref, left_ref, right_ref, dw_ref, gain_ref, order, out, mixed_ref
+):
+    batches, _, cols, feats = rows_ref.shape
+    rows = cols_ref.shape[1] // 4
+    size = out.shape[0] // batches
+    taps = taps_of(dw_ref, False)
+    spot = lax.broadcasted_iota(jnp.int32, (cols, feats), 0)
+
+    def row(x, left, right):
+        low, mid, high = (sum(taps[i][j] * x[i] for i in range(3)) for j in range(3))
+        low = jnp.where(spot == 0, sum(taps[i][0] * left[i : i + 1] for i in range(3)), pltpu.roll(low, 1, 0))
+        high = jnp.where(
+            spot == cols - 1,
+            sum(taps[i][2] * right[i : i + 1] for i in range(3)),
+            pltpu.roll(high, cols - 1, 0),
+        )
+        return (x[1] + (low + mid + high)).astype(BF16)
+
+    def column(x):
+        low, mid, high = (sum(taps[i][j] * x[j][i : i + rows] for i in range(3)) for j in range(3))
+        return (x[1][1 : rows + 1] + (low + mid + high)).astype(BF16)
+
+    for b in range(batches):
+        top, bot = top_ref[b].astype(F32), bot_ref[b].astype(F32)
+        left, right = left_ref[b].astype(F32), right_ref[b].astype(F32)
+        near = [rows_ref[b, n].astype(F32) for n in range(4)]
+        both = cols_ref[b].astype(F32)
+        longer = [
+            jnp.concatenate([top[w : w + 1], both[n * rows : (n + 1) * rows], bot[w : w + 1]], axis=0)
+            for n, w in enumerate((0, 1, cols - 2, cols - 1))
+        ]
+        mixed_ref[b] = jnp.concatenate(
+            [
+                row([top, near[0], near[1]], left[:3], right[:3]),
+                row([near[2], near[3], bot], left[rows - 1 :], right[rows - 1 :]),
+                column([left, longer[0], longer[1]]),
+                column([longer[2], longer[3], right]),
+            ],
+            axis=0,
+        )
+        normed = norm(mixed_ref[b], gain_ref[...])[2]
+        at = slice(b * size, (b + 1) * size)
+        out[at, :] = inner_ref[at, :] + dot(order[...], normed).astype(BF16)
+
+
+def patch_kernel(inner_ref, border_ref, unpick_ref, lat_ref, top_ref, bot_ref, *refs):
+    mixed_out, stat_out, pad_out, mixed_ref, stat_ref, pad_ref, sems = refs
+    batches, rows, cols, feats = lat_ref.shape
+    cells = rows * cols
     pad_ref[:, 1 : rows + 1] = lat_ref[...]
     pad_ref[:, 0] = top_ref[...]
     pad_ref[:, rows + 1] = bot_ref[...]
-    copies = moves([(pad_ref, pad_out)], sems)
-    convolve(pad_ref, left_ref, right_ref, taps_of(dw_ref, False), side_l, side_r, mixed_ref)
+    copies = moves([(pad_ref, pad_out)], sems.at[0:1])
+    cell = lax.broadcasted_iota(jnp.int32, (cells, feats), 0)
+    h, w = cell // cols, cell % cols
+    inside = (h > 0) & (h < rows - 1) & (w > 0) & (w < cols - 1)
+    for b in range(batches):
+        at = slice(b * cells, (b + 1) * cells)
+        patch = dot(unpick_ref[...], border_ref[b])
+        mixed_ref[at, :] = jnp.where(inside, inner_ref[at, :].astype(F32), patch).astype(BF16)
     copies += moves([(mixed_ref, mixed_out)], sems.at[1:2])
     block = 64
 
-    def norm(n, carry):
+    def step(n, carry):
         at = pl.ds(pl.multiple_of(n * block, block), block)
-        mixed = mixed_ref[at, :].astype(F32)
-        mean = jnp.mean(mixed, axis=-1, keepdims=True)
-        centred = mixed - mean
-        rstd = lax.rsqrt(jnp.mean(centred * centred, axis=-1, keepdims=True) + 1e-05)
+        mean, rstd, _ = norm(mixed_ref[at, :], 1.0)
         stat_ref[at, 0:1] = mean
         stat_ref[at, 1:2] = rstd
-        normed_ref[at, :] = (centred * rstd * gain_ref[...]).astype(BF16)
         return carry
 
-    lax.fori_loop(0, batches * rows * cols // block, norm, 0, unroll=2)
+    lax.fori_loop(0, batches * cells // block, step, 0, unroll=2)
     copies += moves([(stat_ref, stat_out)], sems.at[2:3])
-    send_kernel(batches, normed_ref, order, out)
     for copy in copies:
         copy.wait()
 
@@ -624,31 +723,61 @@
     padded = (batches, rows + 2, cols, feats)
     side = pltpu.VMEM((batches, rows, feats), F32)
     stat_shape = (cells, 2)
-    normed, mixed, stat, pad = call(
-        mix_kernel,
-        [flat, flat, shape(stat_shape, F32), shape(padded, BF16)],
+    const = lambda m: jnp.asarray(m, BF16)
+    sent, mixed_inner, own_rows, own_cols = call(
+        inner_kernel,
+        [
+            flat,
+            flat,
+            shape((batches, 4, cols, feats), BF16),
+            shape((batches, 4 * rows, feats), BF16),
+        ],
+        [
+            pltpu.VMEM((cells, feats), BF16),
+            pltpu.VMEM(padded, BF16),
+            pltpu.VMEM((cells, feats), BF16),
+            side,
+            side,
+            pltpu.SemaphoreType.DMA((1,)),
+        ],
+        [latent, dw_kernel, gain, const(plan.send_inner), const(plan.columns)],
+        6,
+        "inner",
+        limit=50 << 20,
+        hbm_outs=(1,),
+    )
+    normed, mixed_border = call(
+        edge_kernel,
+        [flat, shape((batches, plan.unpick.shape[1], feats), BF16)],
+        [],
+        [sent, own_rows, own_cols, above, below, left, right, dw_kernel, gain, const(plan.send_border)],
+        3,
+        "edge",
+        limit=50 << 20,
+    )
+    normed_win = trade(normed)
+    ends = (0, cols, 2 * cols, 2 * cols + rows, 2 * cols + 2 * rows)
+    grad_ends = (grad_out[:, 0], grad_out[:, -1], grad_out[:, :, 0], grad_out[:, :, -1])
+    pairs = halos(
+        *(
+            jnp.concatenate([mixed_border[:, first:last], x], axis=-1)
+            for first, last, x in zip(ends[:-1], ends[1:], grad_ends)
+        )
+    )
+    mixed, stat, pad = call(
+        patch_kernel,
+        [flat, shape(stat_shape, F32), shape(padded, BF16)],
         [
             pltpu.VMEM((cells, feats), BF16),
             pltpu.VMEM(stat_shape, F32),
             pltpu.VMEM(padded, BF16),
-            pltpu.VMEM((cells, feats), BF16),
-            side,
-            side,
             pltpu.SemaphoreType.DMA((3,)),
         ],
-        [latent, above, below, left, right, dw_kernel, gain, send],
-        6,
-        "mix",
+        [mixed_inner, mixed_border, const(plan.unpick), latent, above, below],
+        4,
+        "patch",
         limit=50 << 20,
-        hbm_outs=(1, 2, 3),
-    )
-    normed_win = trade(normed)
-    pair = lambda pick: jnp.concatenate([pick(mixed.reshape(latent.shape)), pick(grad_out)], axis=-1)
-    pairs = halos(
-        pair(lambda x: x[:, 0]),
-        pair(lambda x: x[:, -1]),
-        pair(lambda x: x[:, :, 0]),
-        pair(lambda x: x[:, :, -1]),
+        hbm_outs=(0, 1, 2),
     )
     normed_win, *pairs = lax.optimization_barrier((normed_win, *pairs))
 

time: 161 us -> 158 us (0.981)
  waiting for transfers between devices: 38.8 us -> 30.6 us
  local copies, waits for them, and re-layouts: 11 us -> 17.1 us
  starting transfers between devices: 55 us -> 50.3 us
  Pallas kernels: 50.7 us -> 54 us
    unnamed x48 -> x86, local copies, waits for them, and re-layouts: 4.1 us -> 11.7 us
    ppermute x8, waiting for transfers between devices: 9.12 us -> 3.46 us  [shifted(): lax.ppermute(cells, axis, [(n, n + step) for n in range(count) if 0 <= n...]
    all_to_all x4, starting transfers between devices: 26.4 us -> 22 us  [shards(): lax.all_to_all(x, AXES, split_axis=0, concat_axis=0, tiled=True)]
    pallas_call x9 -> x11, Pallas kernels: 50.7 us -> 54 us  [call(): pl.pallas_call(body, out_shape=outs, in_specs=[smem if n in scalars else...]
    all_to_all x4, waiting for transfers between devices: 25.7 us -> 23.4 us  [shards(): lax.all_to_all(x, AXES, split_axis=0, concat_axis=0, tiled=True)]
  transfers between devices with their start and end apart: 23 -> 23, of which waited for: 11 -> 10; matrix products, arithmetic and copies ran while one was open for 6% -> 6% of each run, Pallas kernels for 24% -> 27%
where the time goes in v5:
time: 158 us; the launch traced here: 157 us
  Pallas kernels  54 us (34%)
  starting transfers between devices  50.3 us (32%)
  waiting for transfers between devices  30.6 us (19%)
  local copies, waits for them, and re-layouts  17.1 us (11%)
  other arithmetic  3.18 us (2%)
    pallas_call x11, Pallas kernels, call(): pl.pallas_call(body, out_shape=outs, in_specs=[smem if n in scalars else...  54 us
    all_to_all x4, waiting for transfers between devices, shards(): lax.all_to_all(x, AXES, split_axis=0, concat_axis=0, tiled=True)  23.4 us
    all_to_all x4, starting transfers between devices, shards(): lax.all_to_all(x, AXES, split_axis=0, concat_axis=0, tiled=True)  22 us
    ppermute x8, starting transfers between devices, shifted(): lax.ppermute(cells, axis, [(n, n + step) for n in range(count) if 0 <= n...  16.6 us
    ppermute x11, starting transfers between devices, swap(): lax.ppermute(x, axis, [(n, n ^ step) for n in range(lax.axis_size(axis))])  11.7 us
    unnamed x86, local copies, waits for them, and re-layouts  11.7 us
    ppermute x11, waiting for transfers between devices, swap(): lax.ppermute(x, axis, [(n, n ^ step) for n in range(lax.axis_size(axis))])  3.73 us
    ppermute x8, waiting for transfers between devices, shifted(): lax.ppermute(cells, axis, [(n, n + step) for n in range(count) if 0 <= n...  3.46 us
  transfers between devices with their start and end apart: 23, of which 10 were waited for; matrix products, arithmetic and copies ran while one was open for 6% of the time, Pallas kernels for 27%

profile of v5, /device:TPU:0, one launch (start us, length us, event | category | flops | bytes accessed | tf_op | source)
XLA Modules:
  0.0 156.6 jit_solution(5355162613634200928)
XLA Ops:
  0.6 3.1 %grad_send.1 = bf16[1024,512]{1,0:T(8,128)(2,1)} custom-call(bf16[1024,512]{1,0:T(8,128)(2,1)} %bitcast.58, bf16[512,512]{1,0:T(8,128)(2,1)} %constant.81.clone.order), custom_call_target="tpu_custom_call" | custom-call | flops 3000000000 | bytes 2621440 | tf_op jit(solution)/shard_map/grad_send/pallas_call | solution.py:644
  3.7 7.3 %all-to-all-start.1 = ((bf16[32,32,512]{2,1,0:T(8,128)(2,1)}), bf16[32,32,512]{2,1,0:T(8,128)(2,1)S(1)}, u32[]{:S(2)}, u32[]{:S(2)}) async-start(bf16[32,32,512]{2,1,0:T(8,128)(2,1)} %bitcast.51), calls=%async_computation.1 | async-start | bytes 2097152 | tf_op jit(solution)/shard_map/all_to_all | solution.py:713
  11.0 0.8 slice_bitcast_fusion.2
  11.8 3.7 %collective-permute-start = (bf16[2,16,512]{2,1,0:T(8,128)(2,1)S(1)}, bf16[2,16,512]{2,1,0:T(8,128)(2,1)S(1)}, u32[]{:S(2)}, u32[]{:S(2)}) collective-permute-start(bf16[2,16,512]{2,1,0:T(8,128)(2,1)S(1)} %get-tuple-element.101), channel_id=1, source_target_pairs={{0,8},{8,16},{16,24},{1,9},{9,17},{17,25},{2,10},{10,18},{18,26},{... | collective-permute-start | bytes 98312 | tf_op jit(solution)/shard_map/ppermute | solution.py:666
  15.5 1.3 collective-permute-start.1
  16.8 6.2 %inner.1 = (bf16[1024,512]{1,0:T(8,128)(2,1)S(1)}, bf16[1024,512]{1,0:T(8,128)(2,1)S(1)}, bf16[2,4,16,512]{3,2,1,0:T(8,128)(2,1)S(1)}, bf16[2,128,512]{2,1,0:T(8,128)(2,1)S(1)}) custom-call(bf16[2,32,16,512]{3,2,1,0:T(8,128)(2,1)} %lat_ref.3, bf16[3,3,512]{2,1,0:T(4,128)(2,1)S(1)} %copy-done.6, f32[1,512]{1,0:T(1,128)S(1)} %bitcast.47, ...), custom_call_target="tpu_custom_call" | custom-call | flops 6000000000 | bytes 4205568 | tf_op jit(solution)/shard_map/inner/pallas_call | solution.py:644
  23.1 1.0 copy-done.22
  24.0 0.7 copy-done.29
  24.7 0.2 fusion.3
  25.1 1.9 %collective-permute-start.2 = (bf16[2,34,512]{2,1,0:T(8,128)(2,1)S(1)}, bf16[2,34,512]{2,1,0:T(8,128)(2,1)S(1)}, u32[]{:S(2)}, u32[]{:S(2)}) collective-permute-start(bf16[2,34,512]{2,1,0:T(8,128)(2,1)S(1)} %pad_maximum_fusion.6), channel_id=1, source_target_pairs={{0,1},{1,2},{2,3},{3,4},{4,5},{5,6},{6,7},{8,9},{9,10},{10,11},{11... | collective-permute-start | bytes 208904 | tf_op jit(solution)/shard_map/ppermute | solution.py:666
  27.0 1.3 collective-permute-start.3
  28.3 1.4 fusion.2
  29.8 0.6 copy.47
  30.4 0.6 copy.46
  31.1 0.4 collective-permute-done.3.right_ref.refs_9_
  31.5 1.2 copy-done.21
  32.7 2.0 %edge.1 = (bf16[1024,512]{1,0:T(8,128)(2,1)}, bf16[2,96,512]{2,1,0:T(8,128)(2,1)S(1)}) custom-call(bf16[1024,512]{1,0:T(8,128)(2,1)S(1)} %copy-done.21, bf16[2,4,16,512]{3,2,1,0:T(8,128)(2,1)S(1)} %get-tuple-element.48.rows_ref, bf16[2,128,512]{2,1,0:T(8,128)(2,1)S(1)} %copy-done.30, bf16[2,16,512]{2,1,0:T(8,128)(2,1)S(1)} %collective-permute-done.top_ref, ...), custom_call_target="tpu_custom_call" | custom-call | flops 3000000000 | bytes 3001344 | tf_op jit(solution)/shard_map/edge/pallas_call | solution.py:644
  34.7 3.9 %all-to-all-done.1 = bf16[32,32,512]{2,1,0:T(8,128)(2,1)S(1)} async-done(((bf16[32,32,512]{2,1,0:T(8,128)(2,1)}), bf16[32,32,512]{2,1,0:T(8,128)(2,1)S(1)}, u32[]{:S(2)}, u32[]{:S(2)}) %all-to-all-start.1) | async-done | bytes 1048608 | tf_op jit(solution)/shard_map/all_to_all | solution.py:713
  38.6 5.7 %all-to-all-start = ((bf16[32,32,512]{2,1,0:T(8,128)(2,1)}), bf16[32,32,512]{2,1,0:T(8,128)(2,1)}, u32[]{:S(2)}, u32[]{:S(2)}) async-start(bf16[32,32,512]{2,1,0:T(8,128)(2,1)} %bitcast.5), calls=%async_computation | async-start | bytes 2097152 | tf_op jit(solution)/shard_map/all_to_all | solution.py:713
  44.3 1.3 dynamic-slice_bitcast_fusion.back_ref
  45.6 0.8 slice_bitcast_fusion
  46.4 1.3 collective-permute-start.5
  47.8 4.5 %collective-permute-start.4 = (bf16[2,16,1024]{2,1,0:T(8,128)(2,1)S(1)}, bf16[2,16,1024]{2,1,0:T(8,128)(2,1)S(1)}, u32[]{:S(2)}, u32[]{:S(2)}) collective-permute-start(bf16[2,16,1024]{2,1,0:T(8,128)(2,1)S(1)} %pad_maximum_fusion.8), channel_id=1, source_target_pairs={{0,8},{8,16},{16,24},{1,9},{9,17},{17,25},{2,10},{10,18},{18,26},{... | collective-permute-start | bytes 196616 | tf_op jit(solution)/shard_map/ppermute | solution.py:666
  52.3 2.2 %collective-permute-done.5.refs_5_ = bf16[2,16,1024]{2,1,0:T(8,128)(2,1)S(1)} collective-permute-done((bf16[2,16,1024]{2,1,0:T(8,128)(2,1)S(1)}, bf16[2,16,1024]{2,1,0:T(8,128)(2,1)S(1)}, u32[]{:S(2)}, u32[]{:S(2)}) %collective-permute-start.5) | collective-permute-done | bytes 65568 | tf_op jit(solution)/shard_map/ppermute | solution.py:666
  54.5 0.9 collective-permute-done.4.refs_4_
  55.5 1.3 collective-permute-start.6
  56.9 1.3 collective-permute-start.7
  58.2 0.7 copy-done.15
  59.0 1.2 grads.1
  60.2 0.9 copy-done.25
  61.1 0.9 copy-done.26
  62.0 0.7 copy-done.31
  62.7 0.7 copy-done.32
  63.4 8.5 %all-to-all-done = bf16[32,32,512]{2,1,0:T(8,128)(2,1)} async-done(((bf16[32,32,512]{2,1,0:T(8,128)(2,1)}), bf16[32,32,512]{2,1,0:T(8,128)(2,1)}, u32[]{:S(2)}, u32[]{:S(2)}) %all-to-all-start) | async-done | bytes 1048608 | tf_op jit(solution)/shard_map/all_to_all | solution.py:713
  71.9 8.1 %windows.2 = (bf16[512,512]{1,0:T(8,128)(2,1)}, bf16[256,512]{1,0:T(8,128)(2,1)}, bf16[256,512]{1,0:T(8,128)(2,1)}, bf16[256,1536]{1,0:T(8,128)(2,1)}) custom-call(bf16[1024,512]{1,0:T(8,128)(2,1)} %bitcast.6.n_hbm, bf16[256,512]{1,0:T(8,128)(2,1)} %copy-done.32, bf16[64,256]{1,0:T(8,128)(2,1)} %constant.86.clone.refs_0_.take_ref, ...), custom_call_target="tpu_custom_call" | custom-call | flops 7000000000 | bytes 4753408 | tf_op jit(solution)/shard_map/windows/pallas_call | solution.py:644
  80.0 3.2 %all-to-all-start.2 = ((bf16[32,16,512]{2,1,0:T(8,128)(2,1)}), bf16[32,16,512]{2,1,0:T(8,128)(2,1)S(1)}, u32[]{:S(2)}, u32[]{:S(2)}) async-start(bf16[32,16,512]{2,1,0:T(8,128)(2,1)} %bitcast.53), calls=%async_computation.2 | async-start | bytes 1048576 | tf_op jit(solution)/shard_map/all_to_all | solution.py:713
  83.3 20.8 %windows.3 = (bf16[768,512]{1,0:T(8,128)(2,1)}, bf16[256,2048]{1,0:T(8,128)(2,1)}, bf16[256,2048]{1,0:T(8,128)(2,1)}) custom-call(bf16[1024,512]{1,0:T(8,128)(2,1)} %bitcast.6.n_hbm, bf16[768,512]{1,0:T(8,128)(2,1)} %copy-done.26, bf16[192,256]{1,0:T(8,128)(2,1)} %constant.87.clone.refs_1_.take_ref, bf16[192,192]{1,0:T(8,128)(2,1)} %constant.85.clone.back_ref, ...), custom_call_target="tpu_custom_call" | custom-call | flops 16999999488 | bytes 8822788 | tf_op jit(solution)/shard_map/windows/pallas_call | solution.py:644
  104.3 5.7 %all-to-all-start.3 = ((bf16[32,24,512]{2,1,0:T(8,128)(2,1)}), bf16[32,24,512]{2,1,0:T(8,128)(2,1)S(1)}, u32[]{:S(2)}, u32[]{:S(2)}) async-start(bf16[32,24,512]{2,1,0:T(8,128)(2,1)} %bitcast.52), calls=%async_computation.3 | async-start | bytes 1572864 | tf_op jit(solution)/shard_map/all_to_all | solution.py:713
  110.1 1.2 copy-done.23
  111.3 2.1 %patch.1 = (bf16[1024,512]{1,0:T(8,128)(2,1)S(1)}, f32[1024,2]{1,0:T(8,128)S(1)}, bf16[2,34,16,512]{3,2,1,0:T(8,128)(2,1)}) custom-call(bf16[1024,512]{1,0:T(8,128)(2,1)S(1)} %copy-done.23, bf16[2,96,512]{2,1,0:T(8,128)(2,1)S(1)} %get-tuple-element.51.border_ref, bf16[512,96]{1,0:T(8,128)(2,1)S(1)} %copy-done.11, bf16[2,32,16,512]{3,2,1,0:T(8,128)(2,1)S(1)} %copy-done, ...), custom_call_target="tpu_custom_call" | custom-call | flops 4000000000 | bytes 4628480 | tf_op jit(solution)/shard_map/patch/pallas_call | solution.py:644
  113.5 0.5 border.1
  114.1 0.3 copy-done.24
  114.4 0.2 copy-done.27
  114.6 0.7 copy-done.38
  115.3 1.6 %add_convert_fusion = bf16[256,2048]{1,0:T(8,128)(2,1)S(1)} fusion(bf16[256,2048]{1,0:T(8,128)(2,1)} %collective-permute-done.8, bf16[256,2048]{1,0:T(8,128)(2,1)S(1)} %copy-done.38), kind=kLoop, calls=%fused_computation | loop fusion | flops 2097152 | bytes 3145728 | tf_op jit(solution)/shard_map/convert_element_type | solution.py:854
  117.0 0.9 fusion.1
  117.8 1.8 %collective-permute-start.9 = (bf16[64,2048]{1,0:T(8,128)(2,1)}, bf16[64,2048]{1,0:T(8,128)(2,1)}, u32[]{:S(2)}, u32[]{:S(2)}) collective-permute-start(bf16[64,2048]{1,0:T(8,128)(2,1)} %get-tuple-element.93), channel_id=1, source_target_pairs={{0,8},{8,0},{16,24},{24,16},{1,9},{9,1},{17,25},{25,17},{2,10},{10... | collective-permute-start | bytes 786440 | tf_op jit(solution)/shard_map/ppermute | solution.py:682
  119.6 1.5 collective-permute-start.10
  121.1 0.3 collective-permute-start.11
  121.3 11.1 %all-to-all-done.3 = bf16[32,24,512]{2,1,0:T(8,128)(2,1)S(1)} async-done(((bf16[32,24,512]{2,1,0:T(8,128)(2,1)}), bf16[32,24,512]{2,1,0:T(8,128)(2,1)S(1)}, u32[]{:S(2)}, u32[]{:S(2)}) %all-to-all-start.3) | async-done | bytes 786464 | tf_op jit(solution)/shard_map/all_to_all | solution.py:713
  132.4 1.0 copy-done.28
  133.5 6.0 %sums.1 = (bf16[1024,512]{1,0:T(8,128)(2,1)S(1)}, f32[16,512]{1,0:T(8,128)S(1)}) custom-call(bf16[512,256]{1,0:T(8,128)(2,1)S(1)} %copy-done.10, bf16[512,384]{1,0:T(8,128)(2,1)S(1)} %copy-done.9, bf16[512,512]{1,0:T(8,128)(2,1)S(1)} %bitcast.46, bf16[768,512]{1,0:T(8,128)(2,1)S(1)} %bitcast.44, f32[1024,2]{1,0:T(8,128)S(1)} %copy-done.28, ...), custom_call_target="tpu_custom_call" | custom-call | flops 7000000000 | bytes 6408192 | tf_op jit(solution)/shard_map/sums/pallas_call | solution.py:644
  139.6 1.3 fusion
  140.9 0.6 collective-permute-start.14
  141.5 1.7 %collective-permute-start.15 = (f32[16,512]{1,0:T(8,128)S(1)}, f32[16,512]{1,0:T(8,128)S(1)}, u32[]{:S(2)}, u32[]{:S(2)}) collective-permute-start(f32[16,512]{1,0:T(8,128)S(1)} %add.52), channel_id=1, source_target_pairs={{0,24},{8,16},{16,8},{24,0},{1,25},{9,17},{17,9},{25,1},{2,26},{10... | collective-permute-start | bytes 98312 | tf_op jit(solution)/shard_map/ppermute | solution.py:682
  143.2 1.3 collective-permute-start.13
  144.5 0.4 collective-permute-done.14
  144.9 1.4 collective-permute-done.15
  146.4 0.8 collective-permute-done.13
  147.3 1.3 collective-permute-start.17
  148.6 3.1 %collective-permute-start.18 = (bf16[16,2560]{1,0:T(8,128)(2,1)S(1)}, bf16[16,2560]{1,0:T(8,128)(2,1)S(1)}, u32[]{:S(2)}, u32[]{:S(2)}) collective-permute-start(bf16[16,2560]{1,0:T(8,128)(2,1)S(1)} %get-tuple-element.117), channel_id=1, source_target_pairs={{0,6},{1,7},{2,4},{3,5},{4,2},{5,3},{6,0},{7,1},{8,14},{9,15},{10,... | collective-permute-start | bytes 245768 | tf_op jit(solution)/shard_map/ppermute | solution.py:682
  151.6 3.1 %spread.1 = bf16[1024,512]{1,0:T(8,128)(2,1)} custom-call(bf16[1024,512]{1,0:T(8,128)(2,1)S(1)} %get-tuple-element.71.d_ref, bf16[2,16,512]{2,1,0:T(8,128)(2,1)S(1)} %copy-done.34, bf16[2,16,512]{2,1,0:T(8,128)(2,1)S(1)} %copy-done.36, bf16[2,34,512]{2,1,0:T(8,128)(2,1)S(1)} %get-tuple-element.78.left_ref, ...), custom_call_target="tpu_custom_call" | custom-call | flops 5000000000 | bytes 2311168 | tf_op jit(solution)/shard_map/spread/pallas_call | solution.py:644
  154.8 1.1 collective-permute-done.17.refs_2_
  155.9 0.7 finish.1
  (106 shorter events, 0.9 us)
Async XLA Ops:
  3.7 13.1 %copy-start.6 = (bf16[3,3,512]{2,1,0:T(4,128)(2,1)S(1)}, bf16[3,3,512]{2,1,0:T(4,128)(2,1)}, u32[]{:S(2)}) copy-start(bf16[3,3,512]{2,1,0:T(4,128)(2,1)} %dw_ref.5) | copy-start | bytes 27652
  3.7 13.1 %copy-start.7 = (f32[512]{0:T(512)S(1)}, f32[512]{0:T(512)}, u32[]{:S(2)}) copy-start(f32[512]{0:T(512)} %param.24) | copy-start | bytes 6148
  3.7 13.1 %copy-start.8 = (bf16[512,512]{1,0:T(8,128)(2,1)S(1)}, bf16[512,512]{1,0:T(8,128)(2,1)}, u32[]{:S(2)}) copy-start(bf16[512,512]{1,0:T(8,128)(2,1)} %constant.88.clone.order) | copy-start | bytes 1572868
  3.7 13.1 %copy-start.13 = (bf16[128,512]{1,0:T(8,128)(2,1)S(1)}, bf16[128,512]{1,0:T(8,128)(2,1)}, u32[]{:S(2)}) copy-start(bf16[128,512]{1,0:T(8,128)(2,1)} %constant.89.clone.columns_ref) | copy-start | bytes 393220
  3.7 34.9 %all-to-all-start.1 = ((bf16[32,32,512]{2,1,0:T(8,128)(2,1)}), bf16[32,32,512]{2,1,0:T(8,128)(2,1)S(1)}, u32[]{:S(2)}, u32[]{:S(2)}) async-start(bf16[32,32,512]{2,1,0:T(8,128)(2,1)} %bitcast.51), calls=%async_computation.1 | async-start | bytes 2097152 | tf_op jit(solution)/shard_map/all_to_all | solution.py:713
  11.8 13.2 %collective-permute-start = (bf16[2,16,512]{2,1,0:T(8,128)(2,1)S(1)}, bf16[2,16,512]{2,1,0:T(8,128)(2,1)S(1)}, u32[]{:S(2)}, u32[]{:S(2)}) collective-permute-start(bf16[2,16,512]{2,1,0:T(8,128)(2,1)S(1)} %get-tuple-element.101), channel_id=1, source_target_pairs={{0,8},{8,16},{16,24},{1,9},{9,17},{17,25},{2,10},{10,18},{18,26},{... | collective-permute-start | bytes 98312 | tf_op jit(solution)/shard_map/ppermute | solution.py:666
  15.5 9.5 %collective-permute-start.1 = (bf16[2,16,512]{2,1,0:T(8,128)(2,1)S(1)}, bf16[2,16,512]{2,1,0:T(8,128)(2,1)S(1)}, u32[]{:S(2)}, u32[]{:S(2)}) collective-permute-start(bf16[2,16,512]{2,1,0:T(8,128)(2,1)S(1)} %get-tuple-element.100), channel_id=1, source_target_pairs={{8,0},{16,8},{24,16},{9,1},{17,9},{25,17},{10,2},{18,10},{26,18},{... | collective-permute-start | bytes 98312 | tf_op jit(solution)/shard_map/ppermute | solution.py:666
  16.8 7.9 %copy-start = (bf16[2,32,16,512]{3,2,1,0:T(8,128)(2,1)S(1)}, bf16[2,32,16,512]{3,2,1,0:T(8,128)(2,1)}, u32[]{:S(2)}) copy-start(bf16[2,32,16,512]{3,2,1,0:T(8,128)(2,1)} %lat_ref.3) | copy-start | bytes 3145732
  23.0 1.0 copy-start.22
  24.0 0.7 copy-start.29
  24.7 2.3 %copy-start.20 = (bf16[1024,512]{1,0:T(8,128)(2,1)}, bf16[1024,512]{1,0:T(8,128)(2,1)S(1)}, u32[]{:S(2)}) copy-start(bf16[1024,512]{1,0:T(8,128)(2,1)S(1)} %get-tuple-element.47.inner_ref) | copy-start | bytes 3145732
  24.7 6.7 %copy-start.12 = (bf16[512,96]{1,0:T(8,128)(2,1)S(1)}, bf16[512,96]{1,0:T(8,128)(2,1)}, u32[]{:S(2)}) copy-start(bf16[512,96]{1,0:T(8,128)(2,1)} %constant.90.clone.order) | copy-start | bytes 294916
  24.9 6.5 %copy-start.30 = (bf16[2,128,512]{2,1,0:T(8,128)(2,1)S(1)}, bf16[2,128,512]{2,1,0:T(8,128)(2,1)}, u32[]{:S(2)}) copy-start(bf16[2,128,512]{2,1,0:T(8,128)(2,1)} %copy-done.29) | copy-start | bytes 786436
  25.1 6.0 %collective-permute-start.2 = (bf16[2,34,512]{2,1,0:T(8,128)(2,1)S(1)}, bf16[2,34,512]{2,1,0:T(8,128)(2,1)S(1)}, u32[]{:S(2)}, u32[]{:S(2)}) collective-permute-start(bf16[2,34,512]{2,1,0:T(8,128)(2,1)S(1)} %pad_maximum_fusion.6), channel_id=1, source_target_pairs={{0,1},{1,2},{2,3},{3,4},{4,5},{5,6},{6,7},{8,9},{9,10},{10,11},{11... | collective-permute-start | bytes 208904 | tf_op jit(solution)/shard_map/ppermute | solution.py:666
  27.0 4.4 %collective-permute-start.3 = (bf16[2,34,512]{2,1,0:T(8,128)(2,1)S(1)}, bf16[2,34,512]{2,1,0:T(8,128)(2,1)S(1)}, u32[]{:S(2)}, u32[]{:S(2)}) collective-permute-start(bf16[2,34,512]{2,1,0:T(8,128)(2,1)S(1)} %pad_maximum_fusion.7), channel_id=1, source_target_pairs={{1,0},{2,1},{3,2},{4,3},{5,4},{6,5},{7,6},{9,8},{10,9},{11,10},{12... | collective-permute-start | bytes 208904 | tf_op jit(solution)/shard_map/ppermute | solution.py:666
  31.4 3.3 %copy-start.4 = (bf16[2,34,512]{2,1,0:T(8,128)(2,1)}, bf16[2,34,512]{2,1,0:T(8,128)(2,1)S(1)}, u32[]{:S(2)}) copy-start(bf16[2,34,512]{2,1,0:T(8,128)(2,1)S(1)} %collective-permute-done.3.right_ref.refs_9_) | copy-start | bytes 208900
  31.4 1.3 copy-start.21
  34.7 20.7 %copy-start.40 = (bf16[2,32,1,512]{3,1,0,2:T(8,128)(2,1)S(1)}, bf16[2,32,1,512]{3,1,0,2:T(8,128)(2,1)}, u32[]{:S(2)}) copy-start(bf16[2,32,1,512]{3,1,0,2:T(8,128)(2,1)} %copy.47) | copy-start | bytes 196612
  38.6 18.2 %copy-start.39 = (bf16[2,32,1,512]{3,1,0,2:T(8,128)(2,1)S(1)}, bf16[2,32,1,512]{3,1,0,2:T(8,128)(2,1)}, u32[]{:S(2)}) copy-start(bf16[2,32,1,512]{3,1,0,2:T(8,128)(2,1)} %copy.46) | copy-start | bytes 196612
  38.6 19.6 %copy-start.1 = (bf16[512,512]{1,0:T(8,128)(2,1)S(1)}, bf16[512,512]{1,0:T(8,128)(2,1)}, u32[]{:S(2)}) copy-start(bf16[512,512]{1,0:T(8,128)(2,1)} %wout_ref.1) | copy-start | bytes 1572868
  38.6 19.6 %copy-start.14 = (bf16[192,256]{1,0:T(8,128)(2,1)S(1)}, bf16[192,256]{1,0:T(8,128)(2,1)}, u32[]{:S(2)}) copy-start(bf16[192,256]{1,0:T(8,128)(2,1)} %constant.87.clone.refs_1_.take_ref) | copy-start | bytes 294916
  38.6 33.3 %all-to-all-start = ((bf16[32,32,512]{2,1,0:T(8,128)(2,1)}), bf16[32,32,512]{2,1,0:T(8,128)(2,1)}, u32[]{:S(2)}, u32[]{:S(2)}) async-start(bf16[32,32,512]{2,1,0:T(8,128)(2,1)} %bitcast.5), calls=%async_computation | async-start | bytes 2097152 | tf_op jit(solution)/shard_map/all_to_all | solution.py:713
  46.4 8.1 %collective-permute-start.5 = (bf16[2,16,1024]{2,1,0:T(8,128)(2,1)S(1)}, bf16[2,16,1024]{2,1,0:T(8,128)(2,1)S(1)}, u32[]{:S(2)}, u32[]{:S(2)}) collective-permute-start(bf16[2,16,1024]{2,1,0:T(8,128)(2,1)S(1)} %pad_maximum_fusion.9), channel_id=1, source_target_pairs={{8,0},{16,8},{24,16},{9,1},{17,9},{25,17},{10,2},{18,10},{26,18},{... | collective-permute-start | bytes 196616 | tf_op jit(solution)/shard_map/ppermute | solution.py:666
  47.8 7.6 %collective-permute-start.4 = (bf16[2,16,1024]{2,1,0:T(8,128)(2,1)S(1)}, bf16[2,16,1024]{2,1,0:T(8,128)(2,1)S(1)}, u32[]{:S(2)}, u32[]{:S(2)}) collective-permute-start(bf16[2,16,1024]{2,1,0:T(8,128)(2,1)S(1)} %pad_maximum_fusion.8), channel_id=1, source_target_pairs={{0,8},{8,16},{16,24},{1,9},{9,17},{17,25},{2,10},{10,18},{18,26},{... | collective-permute-start | bytes 196616 | tf_op jit(solution)/shard_map/ppermute | solution.py:666
  55.5 7.9 %collective-permute-start.6 = (bf16[2,34,1024]{2,1,0:T(8,128)(2,1)S(1)}, bf16[2,34,1024]{2,1,0:T(8,128)(2,1)S(1)}, u32[]{:S(2)}, u32[]{:S(2)}) collective-permute-start(bf16[2,34,1024]{2,1,0:T(8,128)(2,1)S(1)} %pad_maximum_fusion), channel_id=1, source_target_pairs={{0,1},{1,2},{2,3},{3,4},{4,5},{5,6},{6,7},{8,9},{9,10},{10,11},{11... | collective-permute-start | bytes 417800 | tf_op jit(solution)/shard_map/ppermute | solution.py:666
  56.9 6.5 %collective-permute-start.7 = (bf16[2,34,1024]{2,1,0:T(8,128)(2,1)S(1)}, bf16[2,34,1024]{2,1,0:T(8,128)(2,1)S(1)}, u32[]{:S(2)}, u32[]{:S(2)}) collective-permute-start(bf16[2,34,1024]{2,1,0:T(8,128)(2,1)S(1)} %pad_maximum_fusion.1), channel_id=1, source_target_pairs={{1,0},{2,1},{3,2},{4,3},{5,4},{6,5},{7,6},{9,8},{10,9},{11,10},{12... | collective-permute-start | bytes 417800 | tf_op jit(solution)/shard_map/ppermute | solution.py:666
  58.2 0.8 copy-start.15
  60.2 0.9 copy-start.25
  61.1 0.9 copy-start.26
  62.0 0.7 copy-start.31
  62.7 0.7 copy-start.32
  63.4 16.6 %copy-start.2 = (bf16[2,34,1024]{2,1,0:T(8,128)(2,1)}, bf16[2,34,1024]{2,1,0:T(8,128)(2,1)S(1)}, u32[]{:S(2)}) copy-start(bf16[2,34,1024]{2,1,0:T(8,128)(2,1)S(1)} %collective-permute-done.7.refs_7_) | copy-start | bytes 417796
  80.0 24.3 %all-to-all-start.2 = ((bf16[32,16,512]{2,1,0:T(8,128)(2,1)}), bf16[32,16,512]{2,1,0:T(8,128)(2,1)S(1)}, u32[]{:S(2)}, u32[]{:S(2)}) async-start(bf16[32,16,512]{2,1,0:T(8,128)(2,1)} %bitcast.53), calls=%async_computation.2 | async-start | bytes 1048576 | tf_op jit(solution)/shard_map/all_to_all | solution.py:713
  104.1 5.9 %copy-start.11 = (bf16[512,96]{1,0:T(8,128)(2,1)S(1)}, bf16[512,96]{1,0:T(8,128)(2,1)}, u32[]{:S(2)}) copy-start(bf16[512,96]{1,0:T(8,128)(2,1)} %constant.91.clone.unpick_ref) | copy-start | bytes 294916
  104.1 10.5 %collective-permute-start.8 = (bf16[256,2048]{1,0:T(8,128)(2,1)}, bf16[256,2048]{1,0:T(8,128)(2,1)}, u32[]{:S(2)}, u32[]{:S(2)}) collective-permute-start(bf16[256,2048]{1,0:T(8,128)(2,1)} %get-tuple-element.68), channel_id=1, source_target_pairs={{0,1},{1,0},{2,3},{3,2},{4,5},{5,4},{6,7},{7,6},{8,9},{9,8},{10,11... | collective-permute-start | bytes 3145736 | tf_op jit(solution)/shard_map/ppermute | solution.py:682
  104.3 28.1 %all-to-all-start.3 = ((bf16[32,24,512]{2,1,0:T(8,128)(2,1)}), bf16[32,24,512]{2,1,0:T(8,128)(2,1)S(1)}, u32[]{:S(2)}, u32[]{:S(2)}) async-start(bf16[32,24,512]{2,1,0:T(8,128)(2,1)} %bitcast.52), calls=%async_computation.3 | async-start | bytes 1572864 | tf_op jit(solution)/shard_map/all_to_all | solution.py:713
  110.0 1.2 copy-start.23
  111.3 2.2 %copy-start.3 = (bf16[2,34,1024]{2,1,0:T(8,128)(2,1)S(1)}, bf16[2,34,1024]{2,1,0:T(8,128)(2,1)}, u32[]{:S(2)}) copy-start(bf16[2,34,1024]{2,1,0:T(8,128)(2,1)} %copy-done.2) | copy-start | bytes 417796
  111.3 2.2 %copy-start.16 = (bf16[34,256]{1,0:T(8,128)(2,1)S(1)}, bf16[34,256]{1,0:T(8,128)(2,1)}, u32[]{:S(2)}) copy-start(bf16[34,256]{1,0:T(8,128)(2,1)} %constant.94.clone.refs_2_) | copy-start | bytes 52228
  111.3 2.2 %copy-start.17 = (bf16[34,256]{1,0:T(8,128)(2,1)S(1)}, bf16[34,256]{1,0:T(8,128)(2,1)}, u32[]{:S(2)}) copy-start(bf16[34,256]{1,0:T(8,128)(2,1)} %constant.95.clone.refs_3_) | copy-start | bytes 52228
  111.3 2.2 %copy-start.18 = (bf16[16,256]{1,0:T(8,128)(2,1)S(1)}, bf16[16,256]{1,0:T(8,128)(2,1)}, u32[]{:S(2)}) copy-start(bf16[16,256]{1,0:T(8,128)(2,1)} %constant.92.clone.refs_0_) | copy-start | bytes 24580
  111.3 2.2 %copy-start.19 = (bf16[16,256]{1,0:T(8,128)(2,1)S(1)}, bf16[16,256]{1,0:T(8,128)(2,1)}, u32[]{:S(2)}) copy-start(bf16[16,256]{1,0:T(8,128)(2,1)} %constant.93.clone.refs_1_) | copy-start | bytes 24580
  113.5 1.0 copy-start.24
  113.5 1.1 copy-start.27
  113.5 1.7 %copy-start.38 = (bf16[256,2048]{1,0:T(8,128)(2,1)S(1)}, bf16[256,2048]{1,0:T(8,128)(2,1)}, u32[]{:S(2)}) copy-start(bf16[256,2048]{1,0:T(8,128)(2,1)} %get-tuple-element.67) | copy-start | bytes 3145732
  114.6 2.3 %copy-start.33 = (bf16[2,16,512]{2,1,0:T(8,128)(2,1)}, bf16[2,16,512]{2,1,0:T(8,128)(2,1)S(1)}, u32[]{:S(2)}) copy-start(bf16[2,16,512]{2,1,0:T(8,128)(2,1)S(1)} %get-tuple-element.76.top_ref) | copy-start | bytes 98308
  114.6 2.3 %copy-start.35 = (bf16[2,16,512]{2,1,0:T(8,128)(2,1)}, bf16[2,16,512]{2,1,0:T(8,128)(2,1)S(1)}, u32[]{:S(2)}) copy-start(bf16[2,16,512]{2,1,0:T(8,128)(2,1)S(1)} %get-tuple-element.77.bot_ref) | copy-start | bytes 98308
  116.9 4.2 %copy-start.37 = (bf16[256,2048]{1,0:T(8,128)(2,1)}, bf16[256,2048]{1,0:T(8,128)(2,1)S(1)}, u32[]{:S(2)}) copy-start(bf16[256,2048]{1,0:T(8,128)(2,1)S(1)} %add_convert_fusion) | copy-start | bytes 3145732
  116.9 15.5 %copy-start.5 = (bf16[2,34,512]{2,1,0:T(8,128)(2,1)S(1)}, bf16[2,34,512]{2,1,0:T(8,128)(2,1)}, u32[]{:S(2)}) copy-start(bf16[2,34,512]{2,1,0:T(8,128)(2,1)} %copy-done.4) | copy-start | bytes 208900
  116.9 15.5 %copy-start.9 = (bf16[512,384]{1,0:T(8,128)(2,1)S(1)}, bf16[512,384]{1,0:T(8,128)(2,1)}, u32[]{:S(2)}) copy-start(bf16[512,384]{1,0:T(8,128)(2,1)} %constant.84.clone.refs_1_) | copy-start | bytes 1179652
  116.9 15.5 %copy-start.10 = (bf16[512,256]{1,0:T(8,128)(2,1)S(1)}, bf16[512,256]{1,0:T(8,128)(2,1)}, u32[]{:S(2)}) copy-start(bf16[512,256]{1,0:T(8,128)(2,1)} %constant.83.clone.refs_0_) | copy-start | bytes 786436
  117.8 21.6 %collective-permute-start.9 = (bf16[64,2048]{1,0:T(8,128)(2,1)}, bf16[64,2048]{1,0:T(8,128)(2,1)}, u32[]{:S(2)}, u32[]{:S(2)}) collective-permute-start(bf16[64,2048]{1,0:T(8,128)(2,1)} %get-tuple-element.93), channel_id=1, source_target_pairs={{0,8},{8,0},{16,24},{24,16},{1,9},{9,1},{17,25},{25,17},{2,10},{10... | collective-permute-start | bytes 786440 | tf_op jit(solution)/shard_map/ppermute | solution.py:682
  119.6 19.9 %collective-permute-start.10 = (bf16[64,2048]{1,0:T(8,128)(2,1)}, bf16[64,2048]{1,0:T(8,128)(2,1)}, u32[]{:S(2)}, u32[]{:S(2)}) collective-permute-start(bf16[64,2048]{1,0:T(8,128)(2,1)} %get-tuple-element.92), channel_id=1, source_target_pairs={{0,16},{8,24},{16,0},{24,8},{1,17},{9,25},{17,1},{25,9},{2,18},{10... | collective-permute-start | bytes 786440 | tf_op jit(solution)/shard_map/ppermute | solution.py:682
  121.1 18.4 %collective-permute-start.11 = (bf16[64,2048]{1,0:T(8,128)(2,1)}, bf16[64,2048]{1,0:T(8,128)(2,1)}, u32[]{:S(2)}, u32[]{:S(2)}) collective-permute-start(bf16[64,2048]{1,0:T(8,128)(2,1)} %get-tuple-element.91), channel_id=1, source_target_pairs={{0,24},{8,16},{16,8},{24,0},{1,25},{9,17},{17,9},{25,1},{2,26},{10... | collective-permute-start | bytes 786440 | tf_op jit(solution)/shard_map/ppermute | solution.py:682
  132.4 1.0 copy-start.28
  139.5 12.2 %copy-start.34 = (bf16[2,16,512]{2,1,0:T(8,128)(2,1)S(1)}, bf16[2,16,512]{2,1,0:T(8,128)(2,1)}, u32[]{:S(2)}) copy-start(bf16[2,16,512]{2,1,0:T(8,128)(2,1)} %copy-done.33) | copy-start | bytes 98308
  139.5 12.2 %copy-start.36 = (bf16[2,16,512]{2,1,0:T(8,128)(2,1)S(1)}, bf16[2,16,512]{2,1,0:T(8,128)(2,1)}, u32[]{:S(2)}) copy-start(bf16[2,16,512]{2,1,0:T(8,128)(2,1)} %copy-done.35) | copy-start | bytes 98308
  139.5 1.4 collective-permute-start.12
  140.9 4.0 %collective-permute-start.14 = (f32[16,512]{1,0:T(8,128)S(1)}, f32[16,512]{1,0:T(8,128)S(1)}, u32[]{:S(2)}, u32[]{:S(2)}) collective-permute-start(f32[16,512]{1,0:T(8,128)S(1)} %add.52), channel_id=1, source_target_pairs={{0,16},{8,24},{16,0},{24,8},{1,17},{9,25},{17,1},{25,9},{2,18},{10... | collective-permute-start | bytes 98312 | tf_op jit(solution)/shard_map/ppermute | solution.py:682
  141.5 4.8 %collective-permute-start.15 = (f32[16,512]{1,0:T(8,128)S(1)}, f32[16,512]{1,0:T(8,128)S(1)}, u32[]{:S(2)}, u32[]{:S(2)}) collective-permute-start(f32[16,512]{1,0:T(8,128)S(1)} %add.52), channel_id=1, source_target_pairs={{0,24},{8,16},{16,8},{24,0},{1,25},{9,17},{17,9},{25,1},{2,26},{10... | collective-permute-start | bytes 98312 | tf_op jit(solution)/shard_map/ppermute | solution.py:682
  143.2 3.9 %collective-permute-start.13 = (f32[16,512]{1,0:T(8,128)S(1)}, f32[16,512]{1,0:T(8,128)S(1)}, u32[]{:S(2)}, u32[]{:S(2)}) collective-permute-start(f32[16,512]{1,0:T(8,128)S(1)} %add.52), channel_id=1, source_target_pairs={{0,8},{8,0},{16,24},{24,16},{1,9},{9,1},{17,25},{25,17},{2,10},{10... | collective-permute-start | bytes 98312 | tf_op jit(solution)/shard_map/ppermute | solution.py:682
  147.2 7.6 %collective-permute-start.16 = (bf16[16,2560]{1,0:T(8,128)(2,1)S(1)}, bf16[16,2560]{1,0:T(8,128)(2,1)S(1)}, u32[]{:S(2)}, u32[]{:S(2)}) collective-permute-start(bf16[16,2560]{1,0:T(8,128)(2,1)S(1)} %get-tuple-element.119), channel_id=1, source_target_pairs={{0,2},{1,3},{2,0},{3,1},{4,6},{5,7},{6,4},{7,5},{8,10},{9,11},{10,... | collective-permute-start | bytes 245768 | tf_op jit(solution)/shard_map/ppermute | solution.py:682
  147.3 8.7 %collective-permute-start.17 = (bf16[16,2560]{1,0:T(8,128)(2,1)S(1)}, bf16[16,2560]{1,0:T(8,128)(2,1)S(1)}, u32[]{:S(2)}, u32[]{:S(2)}) collective-permute-start(bf16[16,2560]{1,0:T(8,128)(2,1)S(1)} %get-tuple-element.118), channel_id=1, source_target_pairs={{0,4},{1,5},{2,6},{3,7},{4,0},{5,1},{6,2},{7,3},{8,12},{9,13},{10,... | collective-permute-start | bytes 245768 | tf_op jit(solution)/shard_map/ppermute | solution.py:682
  148.6 7.4 %collective-permute-start.18 = (bf16[16,2560]{1,0:T(8,128)(2,1)S(1)}, bf16[16,2560]{1,0:T(8,128)(2,1)S(1)}, u32[]{:S(2)}, u32[]{:S(2)}) collective-permute-start(bf16[16,2560]{1,0:T(8,128)(2,1)S(1)} %get-tuple-element.117), channel_id=1, source_target_pairs={{0,6},{1,7},{2,4},{3,5},{4,2},{5,3},{6,0},{7,1},{8,14},{9,15},{10,... | collective-permute-start | bytes 245768 | tf_op jit(solution)/shard_map/ppermute | solution.py:682

commit v6 on v5

--- a/solution.py
+++ b/solution.py
@@ -164,6 +164,20 @@
         out[at, :] = dot(order[...], x_ref[at, :]).astype(BF16)
 
 
+def grad_kernel(batches, x_hbm, order_hbm, out_hbm, x_ref, order_ref, out_ref, sems):
+    cells = x_ref.shape[0] // batches
+    at = [pl.ds(b * cells, cells) for b in range(batches)]
+    loads = moves([(order_hbm, order_ref), *((x_hbm.at[a], x_ref.at[a]) for a in at)], sems)
+    stores = []
+    loads[0].wait()
+    for b, a in enumerate(at):
+        loads[1 + b].wait()
+        out_ref[a, :] = dot(order_ref[...], x_ref[a, :]).astype(BF16)
+        stores += moves([(out_ref.at[a], out_hbm.at[a])], sems.at[1 + batches + b : 2 + batches + b])
+    for copy in stores:
+        copy.wait()
+
+
 def convolve(pad, left_ref, right_ref, kern, side_l, side_r, out_ref):
     batches, rows, cols, feats = pad.shape
     rows -= 2
@@ -350,7 +364,7 @@
         dn_ref, *results, out_sems = refs[:5]
     else:
         mine_ref, gw_hbm, *old = refs[: 4 * before + 2]
-        dn_ref, keep_hbm, give_hbm, gw, acc, keep_ref, give_ref, out_sems, old_sems, *old_refs = refs[
+        dn_ref, keep_hbm, give_hbm, gw, acc, out_sems, old_sems, *old_refs = refs[
             4 * before + 2 : -10
         ]
         late = moves([(gw_hbm, gw), *zip(old, old_refs)], old_sems)
@@ -426,15 +440,16 @@
             dpacked[at, cols[2]] = fold_heads(dot(probs_b, grad_two)).astype(BF16)
         return carry
 
-    lax.fori_loop(0, count, one, 0, unroll=UNROLL)
+    lax.fori_loop(0, count, one, 0, unroll=6 if count % 6 == 0 else UNROLL)
     if counts is None:
         stores = moves(list(zip((nw, att, dpacked), results)), out_sems)
     else:
         for copy in late:
             copy.wait()
         parts = [old_refs[4 * n : 4 * n + 4] for n in range(before)] + [(nw, att, dpacked, gw)]
-        weight_sums(parts, counts, mine_ref[0], acc, keep_ref, give_ref)
-        stores = moves([(give_ref, give_hbm), (keep_ref, keep_hbm)], out_sems)
+        weight_sums(parts, counts, mine_ref[0], acc)
+        half = feats // 2
+        stores = moves([(acc.at[half:], give_hbm), (acc.at[:half], keep_hbm)], out_sems)
 
     def back(n, carry):
         at = pl.ds(pl.multiple_of(n * block, block), block)
@@ -467,41 +482,30 @@
     return (j % 2) * row_count * chips + i * chips + j // 2
 
 
-def weight_sums(parts, counts, mine, acc, keep_ref, give_ref):
+def weight_sums(parts, counts, mine, acc):
     feats = acc.shape[0]
     row_count, chips = counts
     devices = 2 * row_count * chips
     size = feats // devices
-    half = devices // 2
-    for left, right, start in ((0, 2, 0), (1, 3, 3 * feats)):
-        turned = [part[left][...].T for part in parts]
-        for t in range(parts[0][right].shape[1] // 256):
-            at = slice(t * 256, (t + 1) * 256)
-            acc[:, start + t * 256 : start + (t + 1) * 256] = sum(
-                dot(x, part[right][:, at]) for x, part in zip(turned, parts)
-            ).astype(BF16)
     if size % 16:
         source = lax.broadcasted_iota(jnp.int32, (feats, feats), 1)
         device = source // size
         place = place_of(device // (2 * chips), device % (2 * chips), row_count, chips)
         target = jnp.bitwise_xor(mine, place) * size + source % size
         order = (lax.broadcasted_iota(jnp.int32, (feats, feats), 0) == target).astype(F32).astype(BF16)
-        keep_ref[...] = dot(order[: feats // 2], acc[...]).astype(BF16)
-        give_ref[...] = dot(order[feats // 2 :], acc[...]).astype(BF16)
-        return
-    for n in range(devices):
-        place = place_of(n // (2 * chips), n % (2 * chips), row_count, chips)
-        block = jnp.bitwise_xor(mine, place)
-        rows = acc[n * size : (n + 1) * size, :]
-        at = pl.ds(pl.multiple_of((block % half) * size, size), size)
-
-        @pl.when(block < half)
-        def _(rows=rows, at=at):
-            keep_ref[at, :] = rows
-
-        @pl.when(block >= half)
-        def _(rows=rows, at=at):
-            give_ref[at, :] = rows
+    for left, right, start in ((0, 2, 0), (1, 3, 3 * feats)):
+        turned = [part[left][...].T for part in parts]
+        for t in range(parts[0][right].shape[1] // 256):
+            at = slice(t * 256, (t + 1) * 256)
+            to = slice(start + t * 256, start + (t + 1) * 256)
+            sums = sum(dot(x, part[right][:, at]) for x, part in zip(turned, parts)).astype(BF16)
+            if size % 16:
+                acc[:, to] = dot(order, sums).astype(BF16)
+                continue
+            for n in range(devices):
+                place = place_of(n // (2 * chips), n % (2 * chips), row_count, chips)
+                block = jnp.bitwise_xor(mine, place)
+                acc[pl.ds(pl.multiple_of(block * size, size), size), to] = sums[n * size : (n + 1) * size]
 
 
 def norm_back(d_normed, nhat, rstd, grad, gain):
@@ -715,8 +719,21 @@
 
     flat = shape((cells, feats), BF16)
     (grad_sent,) = call(
-        functools.partial(send_kernel, batches), [flat], [], [grad_flat, send], 3, "grad_send"
-    )
+        functools.partial(grad_kernel, batches),
+        [flat],
+        [
+            pltpu.VMEM((cells, feats), BF16),
+            pltpu.VMEM(send.shape, BF16),
+            pltpu.VMEM((cells, feats), BF16),
+            pltpu.SemaphoreType.DMA((1 + 2 * batches,)),
+        ],
+        [grad_flat, send],
+        3,
+        "grad_send",
+        hbm_ins=(0, 1),
+        hbm_outs=(0,),
+    )
+    grad_sent, latent = lax.optimization_barrier((grad_sent, latent))
     grad_win = trade(grad_sent)
 
     above, below, left, right = halos(latent[:, 0], latent[:, -1], latent[:, :, 0], latent[:, :, -1])
@@ -779,9 +796,11 @@
         limit=50 << 20,
         hbm_outs=(0, 1, 2),
     )
-    normed_win, *pairs = lax.optimization_barrier((normed_win, *pairs))
 
     chips = col_count // 2
+    normed_win, mixed, stat, pad, *pairs = lax.optimization_barrier(
+        (normed_win, mixed, stat, pad, *pairs)
+    )
     ahead = call(
         functools.partial(grads_kernel, parts),
         [grouped[n // 2] for n in range(2 * parts)],
@@ -805,8 +824,6 @@
             scratch = [
                 mat(feats),
                 pltpu.VMEM((feats, 4 * feats), BF16),
-                pltpu.VMEM(half.shape, BF16),
-                pltpu.VMEM(half.shape, BF16),
                 pltpu.SemaphoreType.DMA((2,)),
                 pltpu.SemaphoreType.DMA((1 + len(kept),)),
                 *(pltpu.VMEM(x.shape, BF16) for x in kept),

time: 158 us -> 157 us (level)
  local copies, waits for them, and re-layouts: 17.1 us -> 14.2 us
  waiting for transfers between devices: 30.6 us -> 33.5 us
    ppermute x8, waiting for transfers between devices: 3.46 us -> 7.42 us  [shifted(): lax.ppermute(cells, axis, [(n, n + step) for n in range(count) if 0 <= n...]
    unnamed x86 -> x62, local copies, waits for them, and re-layouts: 11.7 us -> 9.18 us
where the time goes in v6:
time: 157 us; the launch traced here: 156 us
  Pallas kernels  53.4 us (34%)
  starting transfers between devices  50 us (32%)
  waiting for transfers between devices  33.5 us (21%)
  local copies, waits for them, and re-layouts  14.2 us (9%)
  other arithmetic  3.18 us (2%)
    pallas_call x11, Pallas kernels, call(): pl.pallas_call(body, out_shape=outs, in_specs=[smem if n in scalars else...  53.4 us
    all_to_all x4, waiting for transfers between devices, shards(): lax.all_to_all(x, AXES, split_axis=0, concat_axis=0, tiled=True)  22.1 us
    all_to_all x4, starting transfers between devices, shards(): lax.all_to_all(x, AXES, split_axis=0, concat_axis=0, tiled=True)  22 us
    ppermute x8, starting transfers between devices, shifted(): lax.ppermute(cells, axis, [(n, n + step) for n in range(count) if 0 <= n...  16.4 us
    ppermute x11, starting transfers between devices, swap(): lax.ppermute(x, axis, [(n, n ^ step) for n in range(lax.axis_size(axis))])  11.6 us
    unnamed x62, local copies, waits for them, and re-layouts  9.18 us
    ppermute x8, waiting for transfers between devices, shifted(): lax.ppermute(cells, axis, [(n, n + step) for n in range(count) if 0 <= n...  7.42 us
    ppermute x11, waiting for transfers between devices, swap(): lax.ppermute(x, axis, [(n, n ^ step) for n in range(lax.axis_size(axis))])  3.98 us
  transfers between devices with their start and end apart: 23, of which 10 were waited for; matrix products, arithmetic and copies ran while one was open for 6% of the time, Pallas kernels for 27%

profile of v6, /device:TPU:0, one launch (start us, length us, event | category | flops | bytes accessed | tf_op | source)
XLA Modules:
  0.0 155.7 jit_solution(16597202658298141799)
XLA Ops:
  0.6 2.9 %grad_send.1 = bf16[1024,512]{1,0:T(8,128)(2,1)} custom-call(bf16[1024,512]{1,0:T(8,128)(2,1)} %bitcast.50, bf16[512,512]{1,0:T(8,128)(2,1)} %constant.81.clone.order_hbm), custom_call_target="tpu_custom_call" | custom-call | flops 3000000000 | bytes 2621440 | tf_op jit(solution)/shard_map/grad_send/pallas_call | solution.py:648
  3.6 7.3 %all-to-all-start.1 = ((bf16[32,32,512]{2,1,0:T(8,128)(2,1)}), bf16[32,32,512]{2,1,0:T(8,128)(2,1)S(1)}, u32[]{:S(2)}, u32[]{:S(2)}) async-start(bf16[32,32,512]{2,1,0:T(8,128)(2,1)} %bitcast.45), calls=%async_computation.1 | async-start | bytes 2097152 | tf_op jit(solution)/shard_map/all_to_all | solution.py:717
  11.0 1.4 collective-permute-start.1
  12.4 4.5 %collective-permute-start = (bf16[2,16,512]{2,1,0:T(8,128)(2,1)S(1)}, bf16[2,16,512]{2,1,0:T(8,128)(2,1)S(1)}, u32[]{:S(2)}, u32[]{:S(2)}) collective-permute-start(bf16[2,16,512]{2,1,0:T(8,128)(2,1)S(1)} %get-tuple-element.111), channel_id=1, source_target_pairs={{0,8},{8,16},{16,24},{1,9},{9,17},{17,25},{2,10},{10,18},{18,26},{... | collective-permute-start | bytes 98312 | tf_op jit(solution)/shard_map/ppermute | solution.py:670
  17.0 1.4 fusion.2
  18.4 0.6 copy.28
  19.0 6.2 %inner.1 = (bf16[1024,512]{1,0:T(8,128)(2,1)S(1)}, bf16[1024,512]{1,0:T(8,128)(2,1)S(1)}, bf16[2,4,16,512]{3,2,1,0:T(8,128)(2,1)S(1)}, bf16[2,128,512]{2,1,0:T(8,128)(2,1)S(1)}) custom-call(bf16[2,32,16,512]{3,2,1,0:T(8,128)(2,1)} %lat_ref.1, bf16[3,3,512]{2,1,0:T(4,128)(2,1)S(1)} %copy-done.3, f32[1,512]{1,0:T(1,128)S(1)} %bitcast.41, ...), custom_call_target="tpu_custom_call" | custom-call | flops 6000000000 | bytes 4205568 | tf_op jit(solution)/shard_map/inner/pallas_call | solution.py:648
  25.2 1.0 copy-done.17
  26.2 0.8 slice_bitcast_fusion.4
  27.0 0.6 copy.42
  27.6 0.6 copy.43
  28.3 1.6 %collective-permute-start.2 = (bf16[2,34,512]{2,1,0:T(8,128)(2,1)S(1)}, bf16[2,34,512]{2,1,0:T(8,128)(2,1)S(1)}, u32[]{:S(2)}, u32[]{:S(2)}) collective-permute-start(bf16[2,34,512]{2,1,0:T(8,128)(2,1)S(1)} %pad_maximum_fusion.6), channel_id=1, source_target_pairs={{0,1},{1,2},{2,3},{3,4},{4,5},{5,6},{6,7},{8,9},{9,10},{10,11},{11... | collective-permute-start | bytes 208904 | tf_op jit(solution)/shard_map/ppermute | solution.py:670
  30.0 1.3 collective-permute-start.3
  31.3 1.3 dynamic-slice_bitcast_fusion.back_ref
  32.6 2.3 %collective-permute-done.3.right_ref.refs_9_ = bf16[2,34,512]{2,1,0:T(8,128)(2,1)S(1)} collective-permute-done((bf16[2,34,512]{2,1,0:T(8,128)(2,1)S(1)}, bf16[2,34,512]{2,1,0:T(8,128)(2,1)S(1)}, u32[]{:S(2)}, u32[]{:S(2)}) %collective-permute-start.3) | collective-permute-done | bytes 69664 | tf_op jit(solution)/shard_map/ppermute | solution.py:670
  34.9 2.0 %edge.1 = (bf16[1024,512]{1,0:T(8,128)(2,1)}, bf16[2,96,512]{2,1,0:T(8,128)(2,1)S(1)}) custom-call(bf16[1024,512]{1,0:T(8,128)(2,1)S(1)} %get-tuple-element.53.inner_ref, bf16[2,4,16,512]{3,2,1,0:T(8,128)(2,1)S(1)} %get-tuple-element.54.rows_ref, bf16[2,128,512]{2,1,0:T(8,128)(2,1)S(1)} %get-tuple-element.55.cols_ref, ...), custom_call_target="tpu_custom_call" | custom-call | flops 3000000000 | bytes 3001344 | tf_op jit(solution)/shard_map/edge/pallas_call | solution.py:648
  36.9 1.7 %all-to-all-done.1 = bf16[32,32,512]{2,1,0:T(8,128)(2,1)S(1)} async-done(((bf16[32,32,512]{2,1,0:T(8,128)(2,1)}), bf16[32,32,512]{2,1,0:T(8,128)(2,1)S(1)}, u32[]{:S(2)}, u32[]{:S(2)}) %all-to-all-start.1) | async-done | bytes 1048608 | tf_op jit(solution)/shard_map/all_to_all | solution.py:717
  38.6 5.7 %all-to-all-start = ((bf16[32,32,512]{2,1,0:T(8,128)(2,1)}), bf16[32,32,512]{2,1,0:T(8,128)(2,1)}, u32[]{:S(2)}, u32[]{:S(2)}) async-start(bf16[32,32,512]{2,1,0:T(8,128)(2,1)} %bitcast.6), calls=%async_computation | async-start | bytes 2097152 | tf_op jit(solution)/shard_map/all_to_all | solution.py:717
  44.4 3.6 %collective-permute-start.4 = (bf16[2,16,1024]{2,1,0:T(8,128)(2,1)S(1)}, bf16[2,16,1024]{2,1,0:T(8,128)(2,1)S(1)}, u32[]{:S(2)}, u32[]{:S(2)}) collective-permute-start(bf16[2,16,1024]{2,1,0:T(8,128)(2,1)S(1)} %pad_maximum_fusion.8), channel_id=1, source_target_pairs={{0,8},{8,16},{16,24},{1,9},{9,17},{17,25},{2,10},{10,18},{18,26},{... | collective-permute-start | bytes 196616 | tf_op jit(solution)/shard_map/ppermute | solution.py:670
  48.0 1.2 copy-done.18
  49.3 2.1 %patch.1 = (bf16[1024,512]{1,0:T(8,128)(2,1)S(1)}, f32[1024,2]{1,0:T(8,128)S(1)}, bf16[2,34,16,512]{3,2,1,0:T(8,128)(2,1)}) custom-call(bf16[1024,512]{1,0:T(8,128)(2,1)S(1)} %copy-done.18, bf16[2,96,512]{2,1,0:T(8,128)(2,1)S(1)} %get-tuple-element.58.border_ref, bf16[512,96]{1,0:T(8,128)(2,1)S(1)} %copy-done.8, bf16[2,32,16,512]{3,2,1,0:T(8,128)(2,1)S(1)} %copy-done.1, ...), custom_call_target="tpu_custom_call" | custom-call | flops 4000000000 | bytes 4628480 | tf_op jit(solution)/shard_map/patch/pallas_call | solution.py:648
  51.4 1.0 copy-done.19
  52.4 1.3 collective-permute-start.5
  53.7 4.9 %collective-permute-done.5.refs_5_ = bf16[2,16,1024]{2,1,0:T(8,128)(2,1)S(1)} collective-permute-done((bf16[2,16,1024]{2,1,0:T(8,128)(2,1)S(1)}, bf16[2,16,1024]{2,1,0:T(8,128)(2,1)S(1)}, u32[]{:S(2)}, u32[]{:S(2)}) %collective-permute-start.5) | collective-permute-done | bytes 65568 | tf_op jit(solution)/shard_map/ppermute | solution.py:670
  58.6 0.1 pad_maximum_fusion
  58.7 1.3 collective-permute-start.6
  60.0 0.1 pad_maximum_fusion.1
  60.1 1.3 collective-permute-start.7
  61.4 1.3 grads.1
  62.7 0.9 copy-done.20
  63.6 0.9 copy-done.21
  64.5 0.7 copy-done.22
  65.2 0.7 copy-done.23
  65.9 0.2 collective-permute-done.7.refs_7_
  66.1 5.8 %all-to-all-done = bf16[32,32,512]{2,1,0:T(8,128)(2,1)} async-done(((bf16[32,32,512]{2,1,0:T(8,128)(2,1)}), bf16[32,32,512]{2,1,0:T(8,128)(2,1)}, u32[]{:S(2)}, u32[]{:S(2)}) %all-to-all-start) | async-done | bytes 1048608 | tf_op jit(solution)/shard_map/all_to_all | solution.py:717
  71.9 8.2 %windows.2 = (bf16[512,512]{1,0:T(8,128)(2,1)}, bf16[256,512]{1,0:T(8,128)(2,1)}, bf16[256,512]{1,0:T(8,128)(2,1)}, bf16[256,1536]{1,0:T(8,128)(2,1)}) custom-call(bf16[1024,512]{1,0:T(8,128)(2,1)} %bitcast.7.n_hbm, bf16[256,512]{1,0:T(8,128)(2,1)} %copy-done.23, bf16[64,256]{1,0:T(8,128)(2,1)} %constant.86.clone.refs_0_.take_ref, ...), custom_call_target="tpu_custom_call" | custom-call | flops 7000000000 | bytes 4753408 | tf_op jit(solution)/shard_map/windows/pallas_call | solution.py:648
  80.1 3.2 %all-to-all-start.2 = ((bf16[32,16,512]{2,1,0:T(8,128)(2,1)}), bf16[32,16,512]{2,1,0:T(8,128)(2,1)S(1)}, u32[]{:S(2)}, u32[]{:S(2)}) async-start(bf16[32,16,512]{2,1,0:T(8,128)(2,1)} %bitcast.47), calls=%async_computation.2 | async-start | bytes 1048576 | tf_op jit(solution)/shard_map/all_to_all | solution.py:717
  83.3 20.3 %windows.3 = (bf16[768,512]{1,0:T(8,128)(2,1)}, bf16[256,2048]{1,0:T(8,128)(2,1)}, bf16[256,2048]{1,0:T(8,128)(2,1)}) custom-call(bf16[1024,512]{1,0:T(8,128)(2,1)} %bitcast.7.n_hbm, bf16[768,512]{1,0:T(8,128)(2,1)} %copy-done.21, bf16[192,256]{1,0:T(8,128)(2,1)} %constant.87.clone.refs_1_.take_ref, bf16[192,192]{1,0:T(8,128)(2,1)} %constant.85.clone.back_ref, ...), custom_call_target="tpu_custom_call" | custom-call | flops 16999999488 | bytes 8822788 | tf_op jit(solution)/shard_map/windows/pallas_call | solution.py:648
  103.7 0.1 collective-permute-start.8
  103.8 5.7 %all-to-all-start.3 = ((bf16[32,24,512]{2,1,0:T(8,128)(2,1)}), bf16[32,24,512]{2,1,0:T(8,128)(2,1)S(1)}, u32[]{:S(2)}, u32[]{:S(2)}) async-start(bf16[32,24,512]{2,1,0:T(8,128)(2,1)} %bitcast.46), calls=%async_computation.3 | async-start | bytes 1572864 | tf_op jit(solution)/shard_map/all_to_all | solution.py:717
  109.6 0.5 border.1
  110.2 0.6 copy-done.25
  110.8 1.6 %add_convert_fusion = bf16[256,2048]{1,0:T(8,128)(2,1)S(1)} fusion(bf16[256,2048]{1,0:T(8,128)(2,1)} %collective-permute-done.8, bf16[256,2048]{1,0:T(8,128)(2,1)S(1)} %copy-done.25), kind=kLoop, calls=%fused_computation | loop fusion | flops 2097152 | bytes 3145728 | tf_op jit(solution)/shard_map/convert_element_type | solution.py:871
  112.5 0.9 fusion.1
  113.4 2.7 %collective-permute-start.11 = (bf16[64,2048]{1,0:T(8,128)(2,1)}, bf16[64,2048]{1,0:T(8,128)(2,1)}, u32[]{:S(2)}, u32[]{:S(2)}) collective-permute-start(bf16[64,2048]{1,0:T(8,128)(2,1)} %get-tuple-element.101), channel_id=1, source_target_pairs={{0,24},{8,16},{16,8},{24,0},{1,25},{9,17},{17,9},{25,1},{2,26},{10... | collective-permute-start | bytes 786440 | tf_op jit(solution)/shard_map/ppermute | solution.py:686
  116.0 0.6 collective-permute-start.10
  116.6 0.3 collective-permute-start.9
  116.9 14.7 %all-to-all-done.3 = bf16[32,24,512]{2,1,0:T(8,128)(2,1)S(1)} async-done(((bf16[32,24,512]{2,1,0:T(8,128)(2,1)}), bf16[32,24,512]{2,1,0:T(8,128)(2,1)S(1)}, u32[]{:S(2)}, u32[]{:S(2)}) %all-to-all-start.3) | async-done | bytes 786464 | tf_op jit(solution)/shard_map/all_to_all | solution.py:717
  131.5 6.0 %sums.1 = (bf16[1024,512]{1,0:T(8,128)(2,1)S(1)}, f32[16,512]{1,0:T(8,128)S(1)}) custom-call(bf16[512,256]{1,0:T(8,128)(2,1)S(1)} %copy-done.7, bf16[512,384]{1,0:T(8,128)(2,1)S(1)} %copy-done.6, bf16[512,512]{1,0:T(8,128)(2,1)S(1)} %bitcast.40, bf16[768,512]{1,0:T(8,128)(2,1)S(1)} %bitcast.38, f32[1024,2]{1,0:T(8,128)S(1)} %get-tuple-element.73.refs_4_, ...), custom_call_target="tpu_custom_call" | custom-call | flops 7000000000 | bytes 6408192 | tf_op jit(solution)/shard_map/sums/pallas_call | solution.py:648
  137.6 0.7 copy-done.26
  138.3 0.1 copy-done.27
  138.4 1.3 fusion
  139.7 1.0 collective-permute-start.15
  140.8 1.5 collective-permute-start.14
  142.3 1.0 collective-permute-start.13
  143.3 1.6 collective-permute-done.15
  144.9 0.1 collective-permute-done.14
  145.0 1.2 collective-permute-done.13
  146.2 0.9 collective-permute-start.18
  147.1 0.2 collective-permute-start.17
  147.4 3.3 %collective-permute-start.16 = (bf16[16,2560]{1,0:T(8,128)(2,1)S(1)}, bf16[16,2560]{1,0:T(8,128)(2,1)S(1)}, u32[]{:S(2)}, u32[]{:S(2)}) collective-permute-start(bf16[16,2560]{1,0:T(8,128)(2,1)S(1)} %get-tuple-element.129), channel_id=1, source_target_pairs={{0,2},{1,3},{2,0},{3,1},{4,6},{5,7},{6,4},{7,5},{8,10},{9,11},{10,... | collective-permute-start | bytes 245768 | tf_op jit(solution)/shard_map/ppermute | solution.py:686
  150.7 3.1 %spread.1 = bf16[1024,512]{1,0:T(8,128)(2,1)} custom-call(bf16[1024,512]{1,0:T(8,128)(2,1)S(1)} %get-tuple-element.81.d_ref, bf16[2,16,512]{2,1,0:T(8,128)(2,1)S(1)} %get-tuple-element.86.top_ref, bf16[2,16,512]{2,1,0:T(8,128)(2,1)S(1)} %get-tuple-element.87.bot_ref, bf16[2,34,512]{2,1,0:T(8,128)(2,1)S(1)} %get-tuple-element.88.left_ref, ...), custom_call_target="tpu_custom_call" | custom-call | flops 5000000000 | bytes 2311168 | tf_op jit(solution)/shard_map/spread/pallas_call | solution.py:648
  153.9 1.1 collective-permute-done.17.refs_2_
  155.0 0.7 finish.1
  (83 shorter events, 0.4 us)
Async XLA Ops:
  3.6 7.3 %copy-start = (bf16[2,32,16,512]{3,2,1,0:T(8,128)(2,1)S(1)}, bf16[2,32,16,512]{3,2,1,0:T(8,128)(2,1)}, u32[]{:S(2)}) copy-start(bf16[2,32,16,512]{3,2,1,0:T(8,128)(2,1)} %lat_ref.1) | copy-start | bytes 3145732
  3.6 35.0 %all-to-all-start.1 = ((bf16[32,32,512]{2,1,0:T(8,128)(2,1)}), bf16[32,32,512]{2,1,0:T(8,128)(2,1)S(1)}, u32[]{:S(2)}, u32[]{:S(2)}) async-start(bf16[32,32,512]{2,1,0:T(8,128)(2,1)} %bitcast.45), calls=%async_computation.1 | async-start | bytes 2097152 | tf_op jit(solution)/shard_map/all_to_all | solution.py:717
  10.9 8.1 %copy-start.3 = (bf16[3,3,512]{2,1,0:T(4,128)(2,1)S(1)}, bf16[3,3,512]{2,1,0:T(4,128)(2,1)}, u32[]{:S(2)}) copy-start(bf16[3,3,512]{2,1,0:T(4,128)(2,1)} %dw_ref.5) | copy-start | bytes 27652
  10.9 8.1 %copy-start.4 = (f32[512]{0:T(512)S(1)}, f32[512]{0:T(512)}, u32[]{:S(2)}) copy-start(f32[512]{0:T(512)} %param.24) | copy-start | bytes 6148
  10.9 8.1 %copy-start.5 = (bf16[512,512]{1,0:T(8,128)(2,1)S(1)}, bf16[512,512]{1,0:T(8,128)(2,1)}, u32[]{:S(2)}) copy-start(bf16[512,512]{1,0:T(8,128)(2,1)} %constant.88.clone.order) | copy-start | bytes 1572868
  10.9 8.1 %copy-start.10 = (bf16[128,512]{1,0:T(8,128)(2,1)S(1)}, bf16[128,512]{1,0:T(8,128)(2,1)}, u32[]{:S(2)}) copy-start(bf16[128,512]{1,0:T(8,128)(2,1)} %constant.89.clone.columns_ref) | copy-start | bytes 393220
  11.0 17.3 %collective-permute-start.1 = (bf16[2,16,512]{2,1,0:T(8,128)(2,1)S(1)}, bf16[2,16,512]{2,1,0:T(8,128)(2,1)S(1)}, u32[]{:S(2)}, u32[]{:S(2)}) collective-permute-start(bf16[2,16,512]{2,1,0:T(8,128)(2,1)S(1)} %get-tuple-element.110), channel_id=1, source_target_pairs={{8,0},{16,8},{24,16},{9,1},{17,9},{25,17},{10,2},{18,10},{26,18},{... | collective-permute-start | bytes 98312 | tf_op jit(solution)/shard_map/ppermute | solution.py:670
  12.4 15.9 %collective-permute-start = (bf16[2,16,512]{2,1,0:T(8,128)(2,1)S(1)}, bf16[2,16,512]{2,1,0:T(8,128)(2,1)S(1)}, u32[]{:S(2)}, u32[]{:S(2)}) collective-permute-start(bf16[2,16,512]{2,1,0:T(8,128)(2,1)S(1)} %get-tuple-element.111), channel_id=1, source_target_pairs={{0,8},{8,16},{16,24},{1,9},{9,17},{17,25},{2,10},{10,18},{18,26},{... | collective-permute-start | bytes 98312 | tf_op jit(solution)/shard_map/ppermute | solution.py:670
  19.0 15.8 %copy-start.9 = (bf16[512,96]{1,0:T(8,128)(2,1)S(1)}, bf16[512,96]{1,0:T(8,128)(2,1)}, u32[]{:S(2)}) copy-start(bf16[512,96]{1,0:T(8,128)(2,1)} %constant.90.clone.order) | copy-start | bytes 294916
  25.2 1.0 copy-start.17
  28.3 4.2 %collective-permute-start.2 = (bf16[2,34,512]{2,1,0:T(8,128)(2,1)S(1)}, bf16[2,34,512]{2,1,0:T(8,128)(2,1)S(1)}, u32[]{:S(2)}, u32[]{:S(2)}) collective-permute-start(bf16[2,34,512]{2,1,0:T(8,128)(2,1)S(1)} %pad_maximum_fusion.6), channel_id=1, source_target_pairs={{0,1},{1,2},{2,3},{3,4},{4,5},{5,6},{6,7},{8,9},{9,10},{10,11},{11... | collective-permute-start | bytes 208904 | tf_op jit(solution)/shard_map/ppermute | solution.py:670
  30.0 4.9 %collective-permute-start.3 = (bf16[2,34,512]{2,1,0:T(8,128)(2,1)S(1)}, bf16[2,34,512]{2,1,0:T(8,128)(2,1)S(1)}, u32[]{:S(2)}, u32[]{:S(2)}) collective-permute-start(bf16[2,34,512]{2,1,0:T(8,128)(2,1)S(1)} %pad_maximum_fusion.7), channel_id=1, source_target_pairs={{1,0},{2,1},{3,2},{4,3},{5,4},{6,5},{7,6},{9,8},{10,9},{11,10},{12... | collective-permute-start | bytes 208904 | tf_op jit(solution)/shard_map/ppermute | solution.py:670
  36.9 11.1 %copy-start.1 = (bf16[2,32,16,512]{3,2,1,0:T(8,128)(2,1)S(1)}, bf16[2,32,16,512]{3,2,1,0:T(8,128)(2,1)}, u32[]{:S(2)}) copy-start(bf16[2,32,16,512]{3,2,1,0:T(8,128)(2,1)} %lat_ref.1) | copy-start | bytes 3145732
  36.9 11.1 %copy-start.8 = (bf16[512,96]{1,0:T(8,128)(2,1)S(1)}, bf16[512,96]{1,0:T(8,128)(2,1)}, u32[]{:S(2)}) copy-start(bf16[512,96]{1,0:T(8,128)(2,1)} %constant.91.clone.unpick_ref) | copy-start | bytes 294916
  38.6 33.3 %all-to-all-start = ((bf16[32,32,512]{2,1,0:T(8,128)(2,1)}), bf16[32,32,512]{2,1,0:T(8,128)(2,1)}, u32[]{:S(2)}, u32[]{:S(2)}) async-start(bf16[32,32,512]{2,1,0:T(8,128)(2,1)} %bitcast.6), calls=%async_computation | async-start | bytes 2097152 | tf_op jit(solution)/shard_map/all_to_all | solution.py:717
  44.4 9.3 %collective-permute-start.4 = (bf16[2,16,1024]{2,1,0:T(8,128)(2,1)S(1)}, bf16[2,16,1024]{2,1,0:T(8,128)(2,1)S(1)}, u32[]{:S(2)}, u32[]{:S(2)}) collective-permute-start(bf16[2,16,1024]{2,1,0:T(8,128)(2,1)S(1)} %pad_maximum_fusion.8), channel_id=1, source_target_pairs={{0,8},{8,16},{16,24},{1,9},{9,17},{17,25},{2,10},{10,18},{18,26},{... | collective-permute-start | bytes 196616 | tf_op jit(solution)/shard_map/ppermute | solution.py:670
  48.0 1.2 copy-start.18
  49.2 9.4 %copy-start.29 = (bf16[2,32,1,512]{3,1,0,2:T(8,128)(2,1)S(1)}, bf16[2,32,1,512]{3,1,0,2:T(8,128)(2,1)}, u32[]{:S(2)}) copy-start(bf16[2,32,1,512]{3,1,0,2:T(8,128)(2,1)} %copy.43) | copy-start | bytes 196612
  49.2 10.8 %copy-start.28 = (bf16[2,32,1,512]{3,1,0,2:T(8,128)(2,1)S(1)}, bf16[2,32,1,512]{3,1,0,2:T(8,128)(2,1)}, u32[]{:S(2)}) copy-start(bf16[2,32,1,512]{3,1,0,2:T(8,128)(2,1)} %copy.42) | copy-start | bytes 196612
  49.2 12.2 %copy-start.2 = (bf16[512,512]{1,0:T(8,128)(2,1)S(1)}, bf16[512,512]{1,0:T(8,128)(2,1)}, u32[]{:S(2)}) copy-start(bf16[512,512]{1,0:T(8,128)(2,1)} %wout_ref.1) | copy-start | bytes 1572868
  49.2 12.2 %copy-start.11 = (bf16[192,256]{1,0:T(8,128)(2,1)S(1)}, bf16[192,256]{1,0:T(8,128)(2,1)}, u32[]{:S(2)}) copy-start(bf16[192,256]{1,0:T(8,128)(2,1)} %constant.87.clone.refs_1_.take_ref) | copy-start | bytes 294916
  49.2 12.2 %copy-start.12 = (bf16[64,256]{1,0:T(8,128)(2,1)S(1)}, bf16[64,256]{1,0:T(8,128)(2,1)}, u32[]{:S(2)}) copy-start(bf16[64,256]{1,0:T(8,128)(2,1)} %constant.86.clone.refs_0_.take_ref) | copy-start | bytes 98308
  51.4 1.0 copy-start.19
  52.4 6.2 %collective-permute-start.5 = (bf16[2,16,1024]{2,1,0:T(8,128)(2,1)S(1)}, bf16[2,16,1024]{2,1,0:T(8,128)(2,1)S(1)}, u32[]{:S(2)}, u32[]{:S(2)}) collective-permute-start(bf16[2,16,1024]{2,1,0:T(8,128)(2,1)S(1)} %pad_maximum_fusion.9), channel_id=1, source_target_pairs={{8,0},{16,8},{24,16},{9,1},{17,9},{25,17},{10,2},{18,10},{26,18},{... | collective-permute-start | bytes 196616 | tf_op jit(solution)/shard_map/ppermute | solution.py:670
  58.7 7.2 %collective-permute-start.6 = (bf16[2,34,1024]{2,1,0:T(8,128)(2,1)S(1)}, bf16[2,34,1024]{2,1,0:T(8,128)(2,1)S(1)}, u32[]{:S(2)}, u32[]{:S(2)}) collective-permute-start(bf16[2,34,1024]{2,1,0:T(8,128)(2,1)S(1)} %pad_maximum_fusion), channel_id=1, source_target_pairs={{0,1},{1,2},{2,3},{3,4},{4,5},{5,6},{6,7},{8,9},{9,10},{10,11},{11... | collective-permute-start | bytes 417800 | tf_op jit(solution)/shard_map/ppermute | solution.py:670
  60.1 6.0 %collective-permute-start.7 = (bf16[2,34,1024]{2,1,0:T(8,128)(2,1)S(1)}, bf16[2,34,1024]{2,1,0:T(8,128)(2,1)S(1)}, u32[]{:S(2)}, u32[]{:S(2)}) collective-permute-start(bf16[2,34,1024]{2,1,0:T(8,128)(2,1)S(1)} %pad_maximum_fusion.1), channel_id=1, source_target_pairs={{1,0},{2,1},{3,2},{4,3},{5,4},{6,5},{7,6},{9,8},{10,9},{11,10},{12... | collective-permute-start | bytes 417800 | tf_op jit(solution)/shard_map/ppermute | solution.py:670
  62.7 0.9 copy-start.20
  63.6 0.9 copy-start.21
  64.5 0.7 copy-start.22
  65.2 0.7 copy-start.23
  80.1 23.7 %all-to-all-start.2 = ((bf16[32,16,512]{2,1,0:T(8,128)(2,1)}), bf16[32,16,512]{2,1,0:T(8,128)(2,1)S(1)}, u32[]{:S(2)}, u32[]{:S(2)}) async-start(bf16[32,16,512]{2,1,0:T(8,128)(2,1)} %bitcast.47), calls=%async_computation.2 | async-start | bytes 1048576 | tf_op jit(solution)/shard_map/all_to_all | solution.py:717
  103.6 5.9 %copy-start.13 = (bf16[34,256]{1,0:T(8,128)(2,1)S(1)}, bf16[34,256]{1,0:T(8,128)(2,1)}, u32[]{:S(2)}) copy-start(bf16[34,256]{1,0:T(8,128)(2,1)} %constant.95.clone.refs_3_) | copy-start | bytes 52228
  103.6 5.9 %copy-start.14 = (bf16[34,256]{1,0:T(8,128)(2,1)S(1)}, bf16[34,256]{1,0:T(8,128)(2,1)}, u32[]{:S(2)}) copy-start(bf16[34,256]{1,0:T(8,128)(2,1)} %constant.94.clone.refs_2_) | copy-start | bytes 52228
  103.6 5.9 %copy-start.15 = (bf16[16,256]{1,0:T(8,128)(2,1)S(1)}, bf16[16,256]{1,0:T(8,128)(2,1)}, u32[]{:S(2)}) copy-start(bf16[16,256]{1,0:T(8,128)(2,1)} %constant.93.clone.refs_1_) | copy-start | bytes 24580
  103.7 5.9 %copy-start.16 = (bf16[16,256]{1,0:T(8,128)(2,1)S(1)}, bf16[16,256]{1,0:T(8,128)(2,1)}, u32[]{:S(2)}) copy-start(bf16[16,256]{1,0:T(8,128)(2,1)} %constant.92.clone.refs_0_) | copy-start | bytes 24580
  103.7 6.5 %collective-permute-start.8 = (bf16[256,2048]{1,0:T(8,128)(2,1)}, bf16[256,2048]{1,0:T(8,128)(2,1)}, u32[]{:S(2)}, u32[]{:S(2)}) collective-permute-start(bf16[256,2048]{1,0:T(8,128)(2,1)} %get-tuple-element.78), channel_id=1, source_target_pairs={{0,1},{1,0},{2,3},{3,2},{4,5},{5,4},{6,7},{7,6},{8,9},{9,8},{10,11... | collective-permute-start | bytes 3145736 | tf_op jit(solution)/shard_map/ppermute | solution.py:686
  103.8 27.7 %all-to-all-start.3 = ((bf16[32,24,512]{2,1,0:T(8,128)(2,1)}), bf16[32,24,512]{2,1,0:T(8,128)(2,1)S(1)}, u32[]{:S(2)}, u32[]{:S(2)}) async-start(bf16[32,24,512]{2,1,0:T(8,128)(2,1)} %bitcast.46), calls=%async_computation.3 | async-start | bytes 1572864 | tf_op jit(solution)/shard_map/all_to_all | solution.py:717
  109.6 1.2 copy-start.25
  112.5 4.2 %copy-start.24 = (bf16[256,2048]{1,0:T(8,128)(2,1)}, bf16[256,2048]{1,0:T(8,128)(2,1)S(1)}, u32[]{:S(2)}) copy-start(bf16[256,2048]{1,0:T(8,128)(2,1)S(1)} %add_convert_fusion) | copy-start | bytes 3145732
  112.5 19.1 %copy-start.6 = (bf16[512,384]{1,0:T(8,128)(2,1)S(1)}, bf16[512,384]{1,0:T(8,128)(2,1)}, u32[]{:S(2)}) copy-start(bf16[512,384]{1,0:T(8,128)(2,1)} %constant.84.clone.refs_1_) | copy-start | bytes 1179652
  112.5 19.1 %copy-start.7 = (bf16[512,256]{1,0:T(8,128)(2,1)S(1)}, bf16[512,256]{1,0:T(8,128)(2,1)}, u32[]{:S(2)}) copy-start(bf16[512,256]{1,0:T(8,128)(2,1)} %constant.83.clone.refs_0_) | copy-start | bytes 786436
  113.4 24.2 %collective-permute-start.11 = (bf16[64,2048]{1,0:T(8,128)(2,1)}, bf16[64,2048]{1,0:T(8,128)(2,1)}, u32[]{:S(2)}, u32[]{:S(2)}) collective-permute-start(bf16[64,2048]{1,0:T(8,128)(2,1)} %get-tuple-element.101), channel_id=1, source_target_pairs={{0,24},{8,16},{16,8},{24,0},{1,25},{9,17},{17,9},{25,1},{2,26},{10... | collective-permute-start | bytes 786440 | tf_op jit(solution)/shard_map/ppermute | solution.py:686
  116.0 21.5 %collective-permute-start.10 = (bf16[64,2048]{1,0:T(8,128)(2,1)}, bf16[64,2048]{1,0:T(8,128)(2,1)S(1)}, u32[]{:S(2)}, u32[]{:S(2)}) collective-permute-start(bf16[64,2048]{1,0:T(8,128)(2,1)} %get-tuple-element.102), channel_id=1, source_target_pairs={{0,16},{8,24},{16,0},{24,8},{1,17},{9,25},{17,1},{25,9},{2,18},{10... | collective-permute-start | bytes 786440 | tf_op jit(solution)/shard_map/ppermute | solution.py:686
  116.6 21.0 %collective-permute-start.9 = (bf16[64,2048]{1,0:T(8,128)(2,1)}, bf16[64,2048]{1,0:T(8,128)(2,1)S(1)}, u32[]{:S(2)}, u32[]{:S(2)}) collective-permute-start(bf16[64,2048]{1,0:T(8,128)(2,1)} %get-tuple-element.103), channel_id=1, source_target_pairs={{0,8},{8,0},{16,24},{24,16},{1,9},{9,1},{17,25},{25,17},{2,10},{10... | collective-permute-start | bytes 786440 | tf_op jit(solution)/shard_map/ppermute | solution.py:686
  137.6 0.7 copy-start.26
  137.6 0.8 copy-start.27
  138.4 1.3 collective-permute-start.12
  139.7 5.1 %collective-permute-start.15 = (f32[16,512]{1,0:T(8,128)S(1)}, f32[16,512]{1,0:T(8,128)S(1)}, u32[]{:S(2)}, u32[]{:S(2)}) collective-permute-start(f32[16,512]{1,0:T(8,128)S(1)} %add.52), channel_id=1, source_target_pairs={{0,24},{8,16},{16,8},{24,0},{1,25},{9,17},{17,9},{25,1},{2,26},{10... | collective-permute-start | bytes 98312 | tf_op jit(solution)/shard_map/ppermute | solution.py:686
  140.8 4.2 %collective-permute-start.14 = (f32[16,512]{1,0:T(8,128)S(1)}, f32[16,512]{1,0:T(8,128)S(1)}, u32[]{:S(2)}, u32[]{:S(2)}) collective-permute-start(f32[16,512]{1,0:T(8,128)S(1)} %add.52), channel_id=1, source_target_pairs={{0,16},{8,24},{16,0},{24,8},{1,17},{9,25},{17,1},{25,9},{2,18},{10... | collective-permute-start | bytes 98312 | tf_op jit(solution)/shard_map/ppermute | solution.py:686
  142.3 3.9 %collective-permute-start.13 = (f32[16,512]{1,0:T(8,128)S(1)}, f32[16,512]{1,0:T(8,128)S(1)}, u32[]{:S(2)}, u32[]{:S(2)}) collective-permute-start(f32[16,512]{1,0:T(8,128)S(1)} %add.52), channel_id=1, source_target_pairs={{0,8},{8,0},{16,24},{24,16},{1,9},{9,1},{17,25},{25,17},{2,10},{10... | collective-permute-start | bytes 98312 | tf_op jit(solution)/shard_map/ppermute | solution.py:686
  146.2 7.6 %collective-permute-start.18 = (bf16[16,2560]{1,0:T(8,128)(2,1)S(1)}, bf16[16,2560]{1,0:T(8,128)(2,1)S(1)}, u32[]{:S(2)}, u32[]{:S(2)}) collective-permute-start(bf16[16,2560]{1,0:T(8,128)(2,1)S(1)} %get-tuple-element.127), channel_id=1, source_target_pairs={{0,6},{1,7},{2,4},{3,5},{4,2},{5,3},{6,0},{7,1},{8,14},{9,15},{10,... | collective-permute-start | bytes 245768 | tf_op jit(solution)/shard_map/ppermute | solution.py:686
  147.1 7.9 %collective-permute-start.17 = (bf16[16,2560]{1,0:T(8,128)(2,1)S(1)}, bf16[16,2560]{1,0:T(8,128)(2,1)S(1)}, u32[]{:S(2)}, u32[]{:S(2)}) collective-permute-start(bf16[16,2560]{1,0:T(8,128)(2,1)S(1)} %get-tuple-element.128), channel_id=1, source_target_pairs={{0,4},{1,5},{2,6},{3,7},{4,0},{5,1},{6,2},{7,3},{8,12},{9,13},{10,... | collective-permute-start | bytes 245768 | tf_op jit(solution)/shard_map/ppermute | solution.py:686
  147.4 7.6 %collective-permute-start.16 = (bf16[16,2560]{1,0:T(8,128)(2,1)S(1)}, bf16[16,2560]{1,0:T(8,128)(2,1)S(1)}, u32[]{:S(2)}, u32[]{:S(2)}) collective-permute-start(bf16[16,2560]{1,0:T(8,128)(2,1)S(1)} %get-tuple-element.129), channel_id=1, source_target_pairs={{0,2},{1,3},{2,0},{3,1},{4,6},{5,7},{6,4},{7,5},{8,10},{9,11},{10,... | collective-permute-start | bytes 245768 | tf_op jit(solution)/shard_map/ppermute | solution.py:686

commit v7 on v6

--- a/solution.py
+++ b/solution.py
@@ -15,7 +15,7 @@
 AXES = ("row", "col")
 F32 = jnp.float32
 BF16 = jnp.bfloat16
-LIMIT = 56 * 1024 * 1024
+LIMIT = 54 * 1024 * 1024
 UNROLL = 4
 GROUP = 16
 
@@ -568,13 +568,13 @@
         return gain_sum + jnp.sum((d_normed * nhat).reshape(block // 8, 8, feats), axis=0)
 
     gain_sum = lax.fori_loop(
-        0, batches * cells // block, norm, jnp.zeros((8, feats), F32), unroll=2
+        0, batches * cells // block, norm, jnp.zeros((8, feats), F32), unroll=4
     )
     sums_ref[9:10, :] = jnp.sum(gain_sum, axis=0, keepdims=True)
     sums_ref[10:, :] = jnp.zeros((sums_ref.shape[0] - 10, feats), F32)
     loads[count + 3].wait()
 
-    four = 4
+    span = 8
     width = 256
     spot = lax.broadcasted_iota(jnp.int32, (cols, width), 0)
     fold = lambda v: jnp.sum(v.reshape(cols // 8, 8, width), axis=0)
@@ -584,10 +584,10 @@
         for b in range(batches):
 
             def step(n, sums, b=b, lanes=lanes):
-                start = n * four
-                x = [pad_ref[b, start + r, :, lanes].astype(F32) for r in range(four + 2)]
+                start = n * span
+                x = [pad_ref[b, start + r, :, lanes].astype(F32) for r in range(span + 2)]
                 sums = list(sums)
-                for r in range(four):
+                for r in range(span):
                     h = start + r
                     at = pl.ds(pl.multiple_of((b * rows + h) * cols, cols), cols)
                     d_mixed = out_ref[at, lanes].astype(F32)
@@ -603,7 +603,7 @@
                             sums[3 * i + j] = sums[3 * i + j] + fold(moved[j] * x[r + i])
                 return tuple(sums)
 
-            sums = lax.fori_loop(0, rows // four, step, tuple(sums))
+            sums = lax.fori_loop(0, rows // span, step, tuple(sums))
         for n in range(9):
             sums_ref[n : n + 1, lanes] = jnp.sum(sums[n], axis=0, keepdims=True)
     for i in range(3):

time: 157 us -> 157 us (level)
  no operation moved by 1% of the time
where the time goes in v7:
time: 157 us; the launch traced here: 156 us
  Pallas kernels  53.6 us (34%)
  starting transfers between devices  50 us (32%)
  waiting for transfers between devices  33.5 us (21%)
  local copies, waits for them, and re-layouts  14.2 us (9%)
  other arithmetic  3.18 us (2%)
    pallas_call x11, Pallas kernels, call(): pl.pallas_call(body, out_shape=outs, in_specs=[smem if n in scalars else...  53.6 us
    all_to_all x4, waiting for transfers between devices, shards(): lax.all_to_all(x, AXES, split_axis=0, concat_axis=0, tiled=True)  22.1 us
    all_to_all x4, starting transfers between devices, shards(): lax.all_to_all(x, AXES, split_axis=0, concat_axis=0, tiled=True)  22 us
    ppermute x8, starting transfers between devices, shifted(): lax.ppermute(cells, axis, [(n, n + step) for n in range(count) if 0 <= n...  16.4 us
    ppermute x11, starting transfers between devices, swap(): lax.ppermute(x, axis, [(n, n ^ step) for n in range(lax.axis_size(axis))])  11.6 us
    unnamed x62, local copies, waits for them, and re-layouts  9.18 us
    ppermute x8, waiting for transfers between devices, shifted(): lax.ppermute(cells, axis, [(n, n + step) for n in range(count) if 0 <= n...  7.42 us
    ppermute x11, waiting for transfers between devices, swap(): lax.ppermute(x, axis, [(n, n ^ step) for n in range(lax.axis_size(axis))])  3.98 us
  transfers between devices with their start and end apart: 23, of which 10 were waited for; matrix products, arithmetic and copies ran while one was open for 6% of the time, Pallas kernels for 27%

profile of v7, /device:TPU:0, one launch (start us, length us, event | category | flops | bytes accessed | tf_op | source)
XLA Modules:
  0.0 155.9 jit_solution(6127940397621654355)
XLA Ops:
  0.6 2.9 %grad_send.1 = bf16[1024,512]{1,0:T(8,128)(2,1)} custom-call(bf16[1024,512]{1,0:T(8,128)(2,1)} %bitcast.50, bf16[512,512]{1,0:T(8,128)(2,1)} %constant.81.clone.order_hbm), custom_call_target="tpu_custom_call" | custom-call | flops 3000000000 | bytes 2621440 | tf_op jit(solution)/shard_map/grad_send/pallas_call | solution.py:648
  3.6 7.3 %all-to-all-start.1 = ((bf16[32,32,512]{2,1,0:T(8,128)(2,1)}), bf16[32,32,512]{2,1,0:T(8,128)(2,1)S(1)}, u32[]{:S(2)}, u32[]{:S(2)}) async-start(bf16[32,32,512]{2,1,0:T(8,128)(2,1)} %bitcast.45), calls=%async_computation.1 | async-start | bytes 2097152 | tf_op jit(solution)/shard_map/all_to_all | solution.py:717
  11.0 1.4 collective-permute-start.1
  12.4 4.5 %collective-permute-start = (bf16[2,16,512]{2,1,0:T(8,128)(2,1)S(1)}, bf16[2,16,512]{2,1,0:T(8,128)(2,1)S(1)}, u32[]{:S(2)}, u32[]{:S(2)}) collective-permute-start(bf16[2,16,512]{2,1,0:T(8,128)(2,1)S(1)} %get-tuple-element.111), channel_id=1, source_target_pairs={{0,8},{8,16},{16,24},{1,9},{9,17},{17,25},{2,10},{10,18},{18,26},{... | collective-permute-start | bytes 98312 | tf_op jit(solution)/shard_map/ppermute | solution.py:670
  17.0 1.4 fusion.2
  18.4 0.6 copy.28
  19.0 6.2 %inner.1 = (bf16[1024,512]{1,0:T(8,128)(2,1)S(1)}, bf16[1024,512]{1,0:T(8,128)(2,1)S(1)}, bf16[2,4,16,512]{3,2,1,0:T(8,128)(2,1)S(1)}, bf16[2,128,512]{2,1,0:T(8,128)(2,1)S(1)}) custom-call(bf16[2,32,16,512]{3,2,1,0:T(8,128)(2,1)} %lat_ref.1, bf16[3,3,512]{2,1,0:T(4,128)(2,1)S(1)} %copy-done.3, f32[1,512]{1,0:T(1,128)S(1)} %bitcast.41, ...), custom_call_target="tpu_custom_call" | custom-call | flops 6000000000 | bytes 4205568 | tf_op jit(solution)/shard_map/inner/pallas_call | solution.py:648
  25.2 1.0 copy-done.17
  26.2 0.8 slice_bitcast_fusion.4
  27.0 0.6 copy.42
  27.6 0.6 copy.43
  28.3 1.6 %collective-permute-start.2 = (bf16[2,34,512]{2,1,0:T(8,128)(2,1)S(1)}, bf16[2,34,512]{2,1,0:T(8,128)(2,1)S(1)}, u32[]{:S(2)}, u32[]{:S(2)}) collective-permute-start(bf16[2,34,512]{2,1,0:T(8,128)(2,1)S(1)} %pad_maximum_fusion.6), channel_id=1, source_target_pairs={{0,1},{1,2},{2,3},{3,4},{4,5},{5,6},{6,7},{8,9},{9,10},{10,11},{11... | collective-permute-start | bytes 208904 | tf_op jit(solution)/shard_map/ppermute | solution.py:670
  30.0 1.3 collective-permute-start.3
  31.3 1.3 dynamic-slice_bitcast_fusion.back_ref
  32.6 2.3 %collective-permute-done.3.right_ref.refs_9_ = bf16[2,34,512]{2,1,0:T(8,128)(2,1)S(1)} collective-permute-done((bf16[2,34,512]{2,1,0:T(8,128)(2,1)S(1)}, bf16[2,34,512]{2,1,0:T(8,128)(2,1)S(1)}, u32[]{:S(2)}, u32[]{:S(2)}) %collective-permute-start.3) | collective-permute-done | bytes 69664 | tf_op jit(solution)/shard_map/ppermute | solution.py:670
  34.9 2.0 %edge.1 = (bf16[1024,512]{1,0:T(8,128)(2,1)}, bf16[2,96,512]{2,1,0:T(8,128)(2,1)S(1)}) custom-call(bf16[1024,512]{1,0:T(8,128)(2,1)S(1)} %get-tuple-element.53.inner_ref, bf16[2,4,16,512]{3,2,1,0:T(8,128)(2,1)S(1)} %get-tuple-element.54.rows_ref, bf16[2,128,512]{2,1,0:T(8,128)(2,1)S(1)} %get-tuple-element.55.cols_ref, ...), custom_call_target="tpu_custom_call" | custom-call | flops 3000000000 | bytes 3001344 | tf_op jit(solution)/shard_map/edge/pallas_call | solution.py:648
  36.9 1.7 %all-to-all-done.1 = bf16[32,32,512]{2,1,0:T(8,128)(2,1)S(1)} async-done(((bf16[32,32,512]{2,1,0:T(8,128)(2,1)}), bf16[32,32,512]{2,1,0:T(8,128)(2,1)S(1)}, u32[]{:S(2)}, u32[]{:S(2)}) %all-to-all-start.1) | async-done | bytes 1048608 | tf_op jit(solution)/shard_map/all_to_all | solution.py:717
  38.6 5.7 %all-to-all-start = ((bf16[32,32,512]{2,1,0:T(8,128)(2,1)}), bf16[32,32,512]{2,1,0:T(8,128)(2,1)}, u32[]{:S(2)}, u32[]{:S(2)}) async-start(bf16[32,32,512]{2,1,0:T(8,128)(2,1)} %bitcast.6), calls=%async_computation | async-start | bytes 2097152 | tf_op jit(solution)/shard_map/all_to_all | solution.py:717
  44.4 3.6 %collective-permute-start.4 = (bf16[2,16,1024]{2,1,0:T(8,128)(2,1)S(1)}, bf16[2,16,1024]{2,1,0:T(8,128)(2,1)S(1)}, u32[]{:S(2)}, u32[]{:S(2)}) collective-permute-start(bf16[2,16,1024]{2,1,0:T(8,128)(2,1)S(1)} %pad_maximum_fusion.8), channel_id=1, source_target_pairs={{0,8},{8,16},{16,24},{1,9},{9,17},{17,25},{2,10},{10,18},{18,26},{... | collective-permute-start | bytes 196616 | tf_op jit(solution)/shard_map/ppermute | solution.py:670
  48.0 1.2 copy-done.18
  49.3 2.1 %patch.1 = (bf16[1024,512]{1,0:T(8,128)(2,1)S(1)}, f32[1024,2]{1,0:T(8,128)S(1)}, bf16[2,34,16,512]{3,2,1,0:T(8,128)(2,1)}) custom-call(bf16[1024,512]{1,0:T(8,128)(2,1)S(1)} %copy-done.18, bf16[2,96,512]{2,1,0:T(8,128)(2,1)S(1)} %get-tuple-element.58.border_ref, bf16[512,96]{1,0:T(8,128)(2,1)S(1)} %copy-done.8, bf16[2,32,16,512]{3,2,1,0:T(8,128)(2,1)S(1)} %copy-done.1, ...), custom_call_target="tpu_custom_call" | custom-call | flops 4000000000 | bytes 4628480 | tf_op jit(solution)/shard_map/patch/pallas_call | solution.py:648
  51.4 1.0 copy-done.19
  52.4 1.3 collective-permute-start.5
  53.7 4.9 %collective-permute-done.5.refs_5_ = bf16[2,16,1024]{2,1,0:T(8,128)(2,1)S(1)} collective-permute-done((bf16[2,16,1024]{2,1,0:T(8,128)(2,1)S(1)}, bf16[2,16,1024]{2,1,0:T(8,128)(2,1)S(1)}, u32[]{:S(2)}, u32[]{:S(2)}) %collective-permute-start.5) | collective-permute-done | bytes 65568 | tf_op jit(solution)/shard_map/ppermute | solution.py:670
  58.6 0.1 pad_maximum_fusion
  58.7 1.3 collective-permute-start.6
  60.0 0.1 pad_maximum_fusion.1
  60.1 1.3 collective-permute-start.7
  61.4 1.3 grads.1
  62.7 0.9 copy-done.20
  63.6 0.9 copy-done.21
  64.5 0.7 copy-done.22
  65.2 0.7 copy-done.23
  65.9 0.2 collective-permute-done.7.refs_7_
  66.1 5.8 %all-to-all-done = bf16[32,32,512]{2,1,0:T(8,128)(2,1)} async-done(((bf16[32,32,512]{2,1,0:T(8,128)(2,1)}), bf16[32,32,512]{2,1,0:T(8,128)(2,1)}, u32[]{:S(2)}, u32[]{:S(2)}) %all-to-all-start) | async-done | bytes 1048608 | tf_op jit(solution)/shard_map/all_to_all | solution.py:717
  71.9 8.2 %windows.2 = (bf16[512,512]{1,0:T(8,128)(2,1)}, bf16[256,512]{1,0:T(8,128)(2,1)}, bf16[256,512]{1,0:T(8,128)(2,1)}, bf16[256,1536]{1,0:T(8,128)(2,1)}) custom-call(bf16[1024,512]{1,0:T(8,128)(2,1)} %bitcast.7.n_hbm, bf16[256,512]{1,0:T(8,128)(2,1)} %copy-done.23, bf16[64,256]{1,0:T(8,128)(2,1)} %constant.86.clone.refs_0_.take_ref, ...), custom_call_target="tpu_custom_call" | custom-call | flops 7000000000 | bytes 4753408 | tf_op jit(solution)/shard_map/windows/pallas_call | solution.py:648
  80.1 3.2 %all-to-all-start.2 = ((bf16[32,16,512]{2,1,0:T(8,128)(2,1)}), bf16[32,16,512]{2,1,0:T(8,128)(2,1)S(1)}, u32[]{:S(2)}, u32[]{:S(2)}) async-start(bf16[32,16,512]{2,1,0:T(8,128)(2,1)} %bitcast.47), calls=%async_computation.2 | async-start | bytes 1048576 | tf_op jit(solution)/shard_map/all_to_all | solution.py:717
  83.3 20.3 %windows.3 = (bf16[768,512]{1,0:T(8,128)(2,1)}, bf16[256,2048]{1,0:T(8,128)(2,1)}, bf16[256,2048]{1,0:T(8,128)(2,1)}) custom-call(bf16[1024,512]{1,0:T(8,128)(2,1)} %bitcast.7.n_hbm, bf16[768,512]{1,0:T(8,128)(2,1)} %copy-done.21, bf16[192,256]{1,0:T(8,128)(2,1)} %constant.87.clone.refs_1_.take_ref, bf16[192,192]{1,0:T(8,128)(2,1)} %constant.85.clone.back_ref, ...), custom_call_target="tpu_custom_call" | custom-call | flops 16999999488 | bytes 8822788 | tf_op jit(solution)/shard_map/windows/pallas_call | solution.py:648
  103.7 0.1 collective-permute-start.8
  103.8 5.7 %all-to-all-start.3 = ((bf16[32,24,512]{2,1,0:T(8,128)(2,1)}), bf16[32,24,512]{2,1,0:T(8,128)(2,1)S(1)}, u32[]{:S(2)}, u32[]{:S(2)}) async-start(bf16[32,24,512]{2,1,0:T(8,128)(2,1)} %bitcast.46), calls=%async_computation.3 | async-start | bytes 1572864 | tf_op jit(solution)/shard_map/all_to_all | solution.py:717
  109.6 0.5 border.1
  110.2 0.6 copy-done.25
  110.8 1.6 %add_convert_fusion = bf16[256,2048]{1,0:T(8,128)(2,1)S(1)} fusion(bf16[256,2048]{1,0:T(8,128)(2,1)} %collective-permute-done.8, bf16[256,2048]{1,0:T(8,128)(2,1)S(1)} %copy-done.25), kind=kLoop, calls=%fused_computation | loop fusion | flops 2097152 | bytes 3145728 | tf_op jit(solution)/shard_map/convert_element_type | solution.py:871
  112.5 0.9 fusion.1
  113.4 2.7 %collective-permute-start.11 = (bf16[64,2048]{1,0:T(8,128)(2,1)}, bf16[64,2048]{1,0:T(8,128)(2,1)}, u32[]{:S(2)}, u32[]{:S(2)}) collective-permute-start(bf16[64,2048]{1,0:T(8,128)(2,1)} %get-tuple-element.101), channel_id=1, source_target_pairs={{0,24},{8,16},{16,8},{24,0},{1,25},{9,17},{17,9},{25,1},{2,26},{10... | collective-permute-start | bytes 786440 | tf_op jit(solution)/shard_map/ppermute | solution.py:686
  116.0 0.6 collective-permute-start.10
  116.6 0.3 collective-permute-start.9
  116.9 14.7 %all-to-all-done.3 = bf16[32,24,512]{2,1,0:T(8,128)(2,1)S(1)} async-done(((bf16[32,24,512]{2,1,0:T(8,128)(2,1)}), bf16[32,24,512]{2,1,0:T(8,128)(2,1)S(1)}, u32[]{:S(2)}, u32[]{:S(2)}) %all-to-all-start.3) | async-done | bytes 786464 | tf_op jit(solution)/shard_map/all_to_all | solution.py:717
  131.5 6.2 %sums.1 = (bf16[1024,512]{1,0:T(8,128)(2,1)S(1)}, f32[16,512]{1,0:T(8,128)S(1)}) custom-call(bf16[512,256]{1,0:T(8,128)(2,1)S(1)} %copy-done.7, bf16[512,384]{1,0:T(8,128)(2,1)S(1)} %copy-done.6, bf16[512,512]{1,0:T(8,128)(2,1)S(1)} %bitcast.40, bf16[768,512]{1,0:T(8,128)(2,1)S(1)} %bitcast.38, f32[1024,2]{1,0:T(8,128)S(1)} %get-tuple-element.73.refs_4_, ...), custom_call_target="tpu_custom_call" | custom-call | flops 7000000000 | bytes 6408192 | tf_op jit(solution)/shard_map/sums/pallas_call | solution.py:648
  137.8 0.7 copy-done.26
  138.5 0.1 copy-done.27
  138.6 1.3 fusion
  140.0 1.0 collective-permute-start.15
  141.0 1.5 collective-permute-start.14
  142.5 1.0 collective-permute-start.13
  143.6 1.6 collective-permute-done.15
  145.1 0.1 collective-permute-done.14
  145.2 1.2 collective-permute-done.13
  146.5 0.9 collective-permute-start.18
  147.4 0.2 collective-permute-start.17
  147.6 3.3 %collective-permute-start.16 = (bf16[16,2560]{1,0:T(8,128)(2,1)S(1)}, bf16[16,2560]{1,0:T(8,128)(2,1)S(1)}, u32[]{:S(2)}, u32[]{:S(2)}) collective-permute-start(bf16[16,2560]{1,0:T(8,128)(2,1)S(1)} %get-tuple-element.129), channel_id=1, source_target_pairs={{0,2},{1,3},{2,0},{3,1},{4,6},{5,7},{6,4},{7,5},{8,10},{9,11},{10,... | collective-permute-start | bytes 245768 | tf_op jit(solution)/shard_map/ppermute | solution.py:686
  150.9 3.1 %spread.1 = bf16[1024,512]{1,0:T(8,128)(2,1)} custom-call(bf16[1024,512]{1,0:T(8,128)(2,1)S(1)} %get-tuple-element.81.d_ref, bf16[2,16,512]{2,1,0:T(8,128)(2,1)S(1)} %get-tuple-element.86.top_ref, bf16[2,16,512]{2,1,0:T(8,128)(2,1)S(1)} %get-tuple-element.87.bot_ref, bf16[2,34,512]{2,1,0:T(8,128)(2,1)S(1)} %get-tuple-element.88.left_ref, ...), custom_call_target="tpu_custom_call" | custom-call | flops 5000000000 | bytes 2311168 | tf_op jit(solution)/shard_map/spread/pallas_call | solution.py:648
  154.1 1.1 collective-permute-done.17.refs_2_
  155.2 0.7 finish.1
  (83 shorter events, 0.4 us)
Async XLA Ops:
  3.6 7.3 %copy-start = (bf16[2,32,16,512]{3,2,1,0:T(8,128)(2,1)S(1)}, bf16[2,32,16,512]{3,2,1,0:T(8,128)(2,1)}, u32[]{:S(2)}) copy-start(bf16[2,32,16,512]{3,2,1,0:T(8,128)(2,1)} %lat_ref.1) | copy-start | bytes 3145732
  3.6 35.0 %all-to-all-start.1 = ((bf16[32,32,512]{2,1,0:T(8,128)(2,1)}), bf16[32,32,512]{2,1,0:T(8,128)(2,1)S(1)}, u32[]{:S(2)}, u32[]{:S(2)}) async-start(bf16[32,32,512]{2,1,0:T(8,128)(2,1)} %bitcast.45), calls=%async_computation.1 | async-start | bytes 2097152 | tf_op jit(solution)/shard_map/all_to_all | solution.py:717
  10.9 8.1 %copy-start.3 = (bf16[3,3,512]{2,1,0:T(4,128)(2,1)S(1)}, bf16[3,3,512]{2,1,0:T(4,128)(2,1)}, u32[]{:S(2)}) copy-start(bf16[3,3,512]{2,1,0:T(4,128)(2,1)} %dw_ref.5) | copy-start | bytes 27652
  10.9 8.1 %copy-start.4 = (f32[512]{0:T(512)S(1)}, f32[512]{0:T(512)}, u32[]{:S(2)}) copy-start(f32[512]{0:T(512)} %param.24) | copy-start | bytes 6148
  10.9 8.1 %copy-start.5 = (bf16[512,512]{1,0:T(8,128)(2,1)S(1)}, bf16[512,512]{1,0:T(8,128)(2,1)}, u32[]{:S(2)}) copy-start(bf16[512,512]{1,0:T(8,128)(2,1)} %constant.88.clone.order) | copy-start | bytes 1572868
  10.9 8.1 %copy-start.10 = (bf16[128,512]{1,0:T(8,128)(2,1)S(1)}, bf16[128,512]{1,0:T(8,128)(2,1)}, u32[]{:S(2)}) copy-start(bf16[128,512]{1,0:T(8,128)(2,1)} %constant.89.clone.columns_ref) | copy-start | bytes 393220
  11.0 17.3 %collective-permute-start.1 = (bf16[2,16,512]{2,1,0:T(8,128)(2,1)S(1)}, bf16[2,16,512]{2,1,0:T(8,128)(2,1)S(1)}, u32[]{:S(2)}, u32[]{:S(2)}) collective-permute-start(bf16[2,16,512]{2,1,0:T(8,128)(2,1)S(1)} %get-tuple-element.110), channel_id=1, source_target_pairs={{8,0},{16,8},{24,16},{9,1},{17,9},{25,17},{10,2},{18,10},{26,18},{... | collective-permute-start | bytes 98312 | tf_op jit(solution)/shard_map/ppermute | solution.py:670
  12.4 15.9 %collective-permute-start = (bf16[2,16,512]{2,1,0:T(8,128)(2,1)S(1)}, bf16[2,16,512]{2,1,0:T(8,128)(2,1)S(1)}, u32[]{:S(2)}, u32[]{:S(2)}) collective-permute-start(bf16[2,16,512]{2,1,0:T(8,128)(2,1)S(1)} %get-tuple-element.111), channel_id=1, source_target_pairs={{0,8},{8,16},{16,24},{1,9},{9,17},{17,25},{2,10},{10,18},{18,26},{... | collective-permute-start | bytes 98312 | tf_op jit(solution)/shard_map/ppermute | solution.py:670
  19.0 15.8 %copy-start.9 = (bf16[512,96]{1,0:T(8,128)(2,1)S(1)}, bf16[512,96]{1,0:T(8,128)(2,1)}, u32[]{:S(2)}) copy-start(bf16[512,96]{1,0:T(8,128)(2,1)} %constant.90.clone.order) | copy-start | bytes 294916
  25.2 1.0 copy-start.17
  28.3 4.2 %collective-permute-start.2 = (bf16[2,34,512]{2,1,0:T(8,128)(2,1)S(1)}, bf16[2,34,512]{2,1,0:T(8,128)(2,1)S(1)}, u32[]{:S(2)}, u32[]{:S(2)}) collective-permute-start(bf16[2,34,512]{2,1,0:T(8,128)(2,1)S(1)} %pad_maximum_fusion.6), channel_id=1, source_target_pairs={{0,1},{1,2},{2,3},{3,4},{4,5},{5,6},{6,7},{8,9},{9,10},{10,11},{11... | collective-permute-start | bytes 208904 | tf_op jit(solution)/shard_map/ppermute | solution.py:670
  30.0 4.9 %collective-permute-start.3 = (bf16[2,34,512]{2,1,0:T(8,128)(2,1)S(1)}, bf16[2,34,512]{2,1,0:T(8,128)(2,1)S(1)}, u32[]{:S(2)}, u32[]{:S(2)}) collective-permute-start(bf16[2,34,512]{2,1,0:T(8,128)(2,1)S(1)} %pad_maximum_fusion.7), channel_id=1, source_target_pairs={{1,0},{2,1},{3,2},{4,3},{5,4},{6,5},{7,6},{9,8},{10,9},{11,10},{12... | collective-permute-start | bytes 208904 | tf_op jit(solution)/shard_map/ppermute | solution.py:670
  36.9 11.1 %copy-start.1 = (bf16[2,32,16,512]{3,2,1,0:T(8,128)(2,1)S(1)}, bf16[2,32,16,512]{3,2,1,0:T(8,128)(2,1)}, u32[]{:S(2)}) copy-start(bf16[2,32,16,512]{3,2,1,0:T(8,128)(2,1)} %lat_ref.1) | copy-start | bytes 3145732
  36.9 11.1 %copy-start.8 = (bf16[512,96]{1,0:T(8,128)(2,1)S(1)}, bf16[512,96]{1,0:T(8,128)(2,1)}, u32[]{:S(2)}) copy-start(bf16[512,96]{1,0:T(8,128)(2,1)} %constant.91.clone.unpick_ref) | copy-start | bytes 294916
  38.6 33.3 %all-to-all-start = ((bf16[32,32,512]{2,1,0:T(8,128)(2,1)}), bf16[32,32,512]{2,1,0:T(8,128)(2,1)}, u32[]{:S(2)}, u32[]{:S(2)}) async-start(bf16[32,32,512]{2,1,0:T(8,128)(2,1)} %bitcast.6), calls=%async_computation | async-start | bytes 2097152 | tf_op jit(solution)/shard_map/all_to_all | solution.py:717
  44.4 9.3 %collective-permute-start.4 = (bf16[2,16,1024]{2,1,0:T(8,128)(2,1)S(1)}, bf16[2,16,1024]{2,1,0:T(8,128)(2,1)S(1)}, u32[]{:S(2)}, u32[]{:S(2)}) collective-permute-start(bf16[2,16,1024]{2,1,0:T(8,128)(2,1)S(1)} %pad_maximum_fusion.8), channel_id=1, source_target_pairs={{0,8},{8,16},{16,24},{1,9},{9,17},{17,25},{2,10},{10,18},{18,26},{... | collective-permute-start | bytes 196616 | tf_op jit(solution)/shard_map/ppermute | solution.py:670
  48.0 1.2 copy-start.18
  49.2 9.4 %copy-start.29 = (bf16[2,32,1,512]{3,1,0,2:T(8,128)(2,1)S(1)}, bf16[2,32,1,512]{3,1,0,2:T(8,128)(2,1)}, u32[]{:S(2)}) copy-start(bf16[2,32,1,512]{3,1,0,2:T(8,128)(2,1)} %copy.43) | copy-start | bytes 196612
  49.2 10.8 %copy-start.28 = (bf16[2,32,1,512]{3,1,0,2:T(8,128)(2,1)S(1)}, bf16[2,32,1,512]{3,1,0,2:T(8,128)(2,1)}, u32[]{:S(2)}) copy-start(bf16[2,32,1,512]{3,1,0,2:T(8,128)(2,1)} %copy.42) | copy-start | bytes 196612
  49.2 12.2 %copy-start.2 = (bf16[512,512]{1,0:T(8,128)(2,1)S(1)}, bf16[512,512]{1,0:T(8,128)(2,1)}, u32[]{:S(2)}) copy-start(bf16[512,512]{1,0:T(8,128)(2,1)} %wout_ref.1) | copy-start | bytes 1572868
  49.2 12.2 %copy-start.11 = (bf16[192,256]{1,0:T(8,128)(2,1)S(1)}, bf16[192,256]{1,0:T(8,128)(2,1)}, u32[]{:S(2)}) copy-start(bf16[192,256]{1,0:T(8,128)(2,1)} %constant.87.clone.refs_1_.take_ref) | copy-start | bytes 294916
  49.2 12.2 %copy-start.12 = (bf16[64,256]{1,0:T(8,128)(2,1)S(1)}, bf16[64,256]{1,0:T(8,128)(2,1)}, u32[]{:S(2)}) copy-start(bf16[64,256]{1,0:T(8,128)(2,1)} %constant.86.clone.refs_0_.take_ref) | copy-start | bytes 98308
  51.4 1.0 copy-start.19
  52.4 6.2 %collective-permute-start.5 = (bf16[2,16,1024]{2,1,0:T(8,128)(2,1)S(1)}, bf16[2,16,1024]{2,1,0:T(8,128)(2,1)S(1)}, u32[]{:S(2)}, u32[]{:S(2)}) collective-permute-start(bf16[2,16,1024]{2,1,0:T(8,128)(2,1)S(1)} %pad_maximum_fusion.9), channel_id=1, source_target_pairs={{8,0},{16,8},{24,16},{9,1},{17,9},{25,17},{10,2},{18,10},{26,18},{... | collective-permute-start | bytes 196616 | tf_op jit(solution)/shard_map/ppermute | solution.py:670
  58.7 7.2 %collective-permute-start.6 = (bf16[2,34,1024]{2,1,0:T(8,128)(2,1)S(1)}, bf16[2,34,1024]{2,1,0:T(8,128)(2,1)S(1)}, u32[]{:S(2)}, u32[]{:S(2)}) collective-permute-start(bf16[2,34,1024]{2,1,0:T(8,128)(2,1)S(1)} %pad_maximum_fusion), channel_id=1, source_target_pairs={{0,1},{1,2},{2,3},{3,4},{4,5},{5,6},{6,7},{8,9},{9,10},{10,11},{11... | collective-permute-start | bytes 417800 | tf_op jit(solution)/shard_map/ppermute | solution.py:670
  60.1 6.0 %collective-permute-start.7 = (bf16[2,34,1024]{2,1,0:T(8,128)(2,1)S(1)}, bf16[2,34,1024]{2,1,0:T(8,128)(2,1)S(1)}, u32[]{:S(2)}, u32[]{:S(2)}) collective-permute-start(bf16[2,34,1024]{2,1,0:T(8,128)(2,1)S(1)} %pad_maximum_fusion.1), channel_id=1, source_target_pairs={{1,0},{2,1},{3,2},{4,3},{5,4},{6,5},{7,6},{9,8},{10,9},{11,10},{12... | collective-permute-start | bytes 417800 | tf_op jit(solution)/shard_map/ppermute | solution.py:670
  62.7 0.9 copy-start.20
  63.6 0.9 copy-start.21
  64.5 0.7 copy-start.22
  65.2 0.7 copy-start.23
  80.1 23.7 %all-to-all-start.2 = ((bf16[32,16,512]{2,1,0:T(8,128)(2,1)}), bf16[32,16,512]{2,1,0:T(8,128)(2,1)S(1)}, u32[]{:S(2)}, u32[]{:S(2)}) async-start(bf16[32,16,512]{2,1,0:T(8,128)(2,1)} %bitcast.47), calls=%async_computation.2 | async-start | bytes 1048576 | tf_op jit(solution)/shard_map/all_to_all | solution.py:717
  103.6 5.9 %copy-start.13 = (bf16[34,256]{1,0:T(8,128)(2,1)S(1)}, bf16[34,256]{1,0:T(8,128)(2,1)}, u32[]{:S(2)}) copy-start(bf16[34,256]{1,0:T(8,128)(2,1)} %constant.95.clone.refs_3_) | copy-start | bytes 52228
  103.6 5.9 %copy-start.14 = (bf16[34,256]{1,0:T(8,128)(2,1)S(1)}, bf16[34,256]{1,0:T(8,128)(2,1)}, u32[]{:S(2)}) copy-start(bf16[34,256]{1,0:T(8,128)(2,1)} %constant.94.clone.refs_2_) | copy-start | bytes 52228
  103.6 5.9 %copy-start.15 = (bf16[16,256]{1,0:T(8,128)(2,1)S(1)}, bf16[16,256]{1,0:T(8,128)(2,1)}, u32[]{:S(2)}) copy-start(bf16[16,256]{1,0:T(8,128)(2,1)} %constant.93.clone.refs_1_) | copy-start | bytes 24580
  103.7 5.9 %copy-start.16 = (bf16[16,256]{1,0:T(8,128)(2,1)S(1)}, bf16[16,256]{1,0:T(8,128)(2,1)}, u32[]{:S(2)}) copy-start(bf16[16,256]{1,0:T(8,128)(2,1)} %constant.92.clone.refs_0_) | copy-start | bytes 24580
  103.7 6.5 %collective-permute-start.8 = (bf16[256,2048]{1,0:T(8,128)(2,1)}, bf16[256,2048]{1,0:T(8,128)(2,1)}, u32[]{:S(2)}, u32[]{:S(2)}) collective-permute-start(bf16[256,2048]{1,0:T(8,128)(2,1)} %get-tuple-element.78), channel_id=1, source_target_pairs={{0,1},{1,0},{2,3},{3,2},{4,5},{5,4},{6,7},{7,6},{8,9},{9,8},{10,11... | collective-permute-start | bytes 3145736 | tf_op jit(solution)/shard_map/ppermute | solution.py:686
  103.8 27.7 %all-to-all-start.3 = ((bf16[32,24,512]{2,1,0:T(8,128)(2,1)}), bf16[32,24,512]{2,1,0:T(8,128)(2,1)S(1)}, u32[]{:S(2)}, u32[]{:S(2)}) async-start(bf16[32,24,512]{2,1,0:T(8,128)(2,1)} %bitcast.46), calls=%async_computation.3 | async-start | bytes 1572864 | tf_op jit(solution)/shard_map/all_to_all | solution.py:717
  109.6 1.2 copy-start.25
  112.5 4.2 %copy-start.24 = (bf16[256,2048]{1,0:T(8,128)(2,1)}, bf16[256,2048]{1,0:T(8,128)(2,1)S(1)}, u32[]{:S(2)}) copy-start(bf16[256,2048]{1,0:T(8,128)(2,1)S(1)} %add_convert_fusion) | copy-start | bytes 3145732
  112.5 19.1 %copy-start.6 = (bf16[512,384]{1,0:T(8,128)(2,1)S(1)}, bf16[512,384]{1,0:T(8,128)(2,1)}, u32[]{:S(2)}) copy-start(bf16[512,384]{1,0:T(8,128)(2,1)} %constant.84.clone.refs_1_) | copy-start | bytes 1179652
  112.5 19.1 %copy-start.7 = (bf16[512,256]{1,0:T(8,128)(2,1)S(1)}, bf16[512,256]{1,0:T(8,128)(2,1)}, u32[]{:S(2)}) copy-start(bf16[512,256]{1,0:T(8,128)(2,1)} %constant.83.clone.refs_0_) | copy-start | bytes 786436
  113.4 24.4 %collective-permute-start.11 = (bf16[64,2048]{1,0:T(8,128)(2,1)}, bf16[64,2048]{1,0:T(8,128)(2,1)}, u32[]{:S(2)}, u32[]{:S(2)}) collective-permute-start(bf16[64,2048]{1,0:T(8,128)(2,1)} %get-tuple-element.101), channel_id=1, source_target_pairs={{0,24},{8,16},{16,8},{24,0},{1,25},{9,17},{17,9},{25,1},{2,26},{10... | collective-permute-start | bytes 786440 | tf_op jit(solution)/shard_map/ppermute | solution.py:686
  116.0 21.8 %collective-permute-start.10 = (bf16[64,2048]{1,0:T(8,128)(2,1)}, bf16[64,2048]{1,0:T(8,128)(2,1)S(1)}, u32[]{:S(2)}, u32[]{:S(2)}) collective-permute-start(bf16[64,2048]{1,0:T(8,128)(2,1)} %get-tuple-element.102), channel_id=1, source_target_pairs={{0,16},{8,24},{16,0},{24,8},{1,17},{9,25},{17,1},{25,9},{2,18},{10... | collective-permute-start | bytes 786440 | tf_op jit(solution)/shard_map/ppermute | solution.py:686
  116.6 21.2 %collective-permute-start.9 = (bf16[64,2048]{1,0:T(8,128)(2,1)}, bf16[64,2048]{1,0:T(8,128)(2,1)S(1)}, u32[]{:S(2)}, u32[]{:S(2)}) collective-permute-start(bf16[64,2048]{1,0:T(8,128)(2,1)} %get-tuple-element.103), channel_id=1, source_target_pairs={{0,8},{8,0},{16,24},{24,16},{1,9},{9,1},{17,25},{25,17},{2,10},{10... | collective-permute-start | bytes 786440 | tf_op jit(solution)/shard_map/ppermute | solution.py:686
  137.8 0.7 copy-start.26
  137.8 0.8 copy-start.27
  138.6 1.3 collective-permute-start.12
  140.0 5.1 %collective-permute-start.15 = (f32[16,512]{1,0:T(8,128)S(1)}, f32[16,512]{1,0:T(8,128)S(1)}, u32[]{:S(2)}, u32[]{:S(2)}) collective-permute-start(f32[16,512]{1,0:T(8,128)S(1)} %add.52), channel_id=1, source_target_pairs={{0,24},{8,16},{16,8},{24,0},{1,25},{9,17},{17,9},{25,1},{2,26},{10... | collective-permute-start | bytes 98312 | tf_op jit(solution)/shard_map/ppermute | solution.py:686
  141.0 4.2 %collective-permute-start.14 = (f32[16,512]{1,0:T(8,128)S(1)}, f32[16,512]{1,0:T(8,128)S(1)}, u32[]{:S(2)}, u32[]{:S(2)}) collective-permute-start(f32[16,512]{1,0:T(8,128)S(1)} %add.52), channel_id=1, source_target_pairs={{0,16},{8,24},{16,0},{24,8},{1,17},{9,25},{17,1},{25,9},{2,18},{10... | collective-permute-start | bytes 98312 | tf_op jit(solution)/shard_map/ppermute | solution.py:686
  142.5 3.9 %collective-permute-start.13 = (f32[16,512]{1,0:T(8,128)S(1)}, f32[16,512]{1,0:T(8,128)S(1)}, u32[]{:S(2)}, u32[]{:S(2)}) collective-permute-start(f32[16,512]{1,0:T(8,128)S(1)} %add.52), channel_id=1, source_target_pairs={{0,8},{8,0},{16,24},{24,16},{1,9},{9,1},{17,25},{25,17},{2,10},{10... | collective-permute-start | bytes 98312 | tf_op jit(solution)/shard_map/ppermute | solution.py:686
  146.5 7.6 %collective-permute-start.18 = (bf16[16,2560]{1,0:T(8,128)(2,1)S(1)}, bf16[16,2560]{1,0:T(8,128)(2,1)S(1)}, u32[]{:S(2)}, u32[]{:S(2)}) collective-permute-start(bf16[16,2560]{1,0:T(8,128)(2,1)S(1)} %get-tuple-element.127), channel_id=1, source_target_pairs={{0,6},{1,7},{2,4},{3,5},{4,2},{5,3},{6,0},{7,1},{8,14},{9,15},{10,... | collective-permute-start | bytes 245768 | tf_op jit(solution)/shard_map/ppermute | solution.py:686
  147.4 7.9 %collective-permute-start.17 = (bf16[16,2560]{1,0:T(8,128)(2,1)S(1)}, bf16[16,2560]{1,0:T(8,128)(2,1)S(1)}, u32[]{:S(2)}, u32[]{:S(2)}) collective-permute-start(bf16[16,2560]{1,0:T(8,128)(2,1)S(1)} %get-tuple-element.128), channel_id=1, source_target_pairs={{0,4},{1,5},{2,6},{3,7},{4,0},{5,1},{6,2},{7,3},{8,12},{9,13},{10,... | collective-permute-start | bytes 245768 | tf_op jit(solution)/shard_map/ppermute | solution.py:686
  147.6 7.6 %collective-permute-start.16 = (bf16[16,2560]{1,0:T(8,128)(2,1)S(1)}, bf16[16,2560]{1,0:T(8,128)(2,1)S(1)}, u32[]{:S(2)}, u32[]{:S(2)}) collective-permute-start(bf16[16,2560]{1,0:T(8,128)(2,1)S(1)} %get-tuple-element.129), channel_id=1, source_target_pairs={{0,2},{1,3},{2,0},{3,1},{4,6},{5,7},{6,4},{7,5},{8,10},{9,11},{10,... | collective-permute-start | bytes 245768 | tf_op jit(solution)/shard_map/ppermute | solution.py:686
